TPU v7x, 256 devices: a whole 4x4x8 slice. The times are simulated.
256 devices in a mesh: space: 32 (over z, y), snap: 8 (over x, core).
Axes of the slice: x: 4, y: 4, z: 8, core: 2. Of those that a mesh axis runs over, the one named last changes fastest.
Arguments:
- snaps: bfloat16 [512, 1048576], P('snap', 'space'), may hold values from -50 to 50
- sketch: bfloat16 [32, 512], P(None, 'snap'), may hold values from -0.75 to 0.75
- merge_mix: float32 [64, 32], replicated, may hold values from -0.75 to 0.75
Outputs:
- basis: float32 [32, 1048576], P('snap', 'space')
All inputs are finite; a program needn't handle non-finite values.
Results may differ from a plain program's by a relative error of at most 0.0075.
Values may be sent and summed in bfloat16 or wider, within the bound.
No kernel may reach another device: no remote copies, remote signals or barrier semaphores. Data moves between devices by JAX's collectives and lax.ppermute only.
A program may use at most 64 MiB of HBM per device.

v0:
```python
import functools
import math

import jax
import jax.numpy as jnp
from jax import lax
from jax.experimental import pallas as pl
from jax.experimental.pallas import tpu as pltpu
from jax.sharding import PartitionSpec as P

ITERS = 4
PANEL = 8
F32 = jnp.float32
BF16 = jnp.bfloat16
VMEM_LIMIT = 24 * 1024 * 1024


def dot_nn(a, b):
    return jnp.dot(a, b, precision=lax.Precision.HIGHEST, preferred_element_type=F32)


def dot_nt(a, b):
    return lax.dot_general(
        a, b, (((1,), (1,)), ((), ())), precision=lax.Precision.HIGHEST, preferred_element_type=F32
    )


def dot_tn(a, b):
    return lax.dot_general(
        a, b, (((0,), (0,)), ((), ())), precision=lax.Precision.HIGHEST, preferred_element_type=F32
    )


def eliminate_panel(table, wide, first):
    group, inner = divmod(first, 8)
    shape = table[0].shape
    row_ids = lax.broadcasted_iota(jnp.int32, shape, 0)
    columns = [
        [jnp.broadcast_to(t[:, wide + first + k : wide + first + k + 1], shape) for t in table[group:]]
        for k in range(PANEL)
    ]
    rows = [jnp.broadcast_to(table[group][inner + k : inner + k + 1], shape) for k in range(PANEL)]
    corner = {
        (k, l): jnp.broadcast_to(columns[k][0][inner + l : inner + l + 1], shape)
        for k in range(PANEL)
        for l in range(k, PANEL)
    }
    for k in range(PANEL):
        inverse = 1.0 / corner[k, k]
        factors = [c * inverse for c in columns[k]]
        steps = {l: corner[k, l] * inverse for l in range(k + 1, PANEL)}
        for l in range(k + 1, PANEL):
            for m in range(l, PANEL):
                corner[l, m] = corner[l, m] - steps[l] * corner[k, m]
            columns[l] = [c - f * corner[k, l] for c, f in zip(columns[l], factors)]
            rows[l] = rows[l] - steps[l] * rows[k]
        factors[0] = jnp.where(row_ids > inner + k, factors[0], 0.0)
        for g, f in enumerate(factors):
            table[group + g] = table[group + g] - f * rows[k]


def cholesky_solves(pairs):
    modes = pairs[0][0].shape[0]
    wide = pairs[0][1].shape[1]
    tables = []
    for h, b in pairs:
        table = jnp.concatenate([b, h], axis=1)
        tables.append([table[r : r + 8] for r in range(0, modes, 8)])
    for first in range(0, modes, PANEL):
        for table in tables:
            eliminate_panel(table, wide, first)
    solved = []
    for table in tables:
        whole = jnp.concatenate(table, axis=0)
        below = whole[:, wide:]
        same = lax.broadcasted_iota(jnp.int32, below.shape, 0) == lax.broadcasted_iota(
            jnp.int32, below.shape, 1
        )
        diagonal = jnp.sum(jnp.where(same, below, 0.0), axis=1, keepdims=True)
        solved.append(whole[:, :wide] * lax.rsqrt(diagonal))
    return solved


def trace_scale(gram):
    same = lax.broadcasted_iota(jnp.int32, gram.shape, 0) == lax.broadcasted_iota(
        jnp.int32, gram.shape, 1
    )
    diagonal = jnp.where(same, gram, 0.0)
    return lax.rsqrt(jnp.sum(jnp.sum(diagonal, axis=1, keepdims=True), axis=0, keepdims=True))


def mixings(grams, mix):
    pairs = []
    for gram in grams:
        curved_t = dot_tn(mix, gram)
        pairs.append((dot_nn(curved_t, mix), curved_t))
    return [s * trace_scale(g) for s, g in zip(cholesky_solves(pairs), grams)]


def split_two(x):
    high = x.astype(BF16)
    return jnp.concatenate([high, (x - high.astype(F32)).astype(BF16)], axis=0)


def bf16_dot(a, b):
    return jnp.dot(a, b, preferred_element_type=F32)


def bf16_dot_nt(a, b):
    return lax.dot_general(a, b, (((1,), (1,)), ((), ())), preferred_element_type=F32)


def joined(both):
    modes = both.shape[0] // 2
    return both[:modes] + both[modes:]


def own_gram_kernel(place_ref, snaps_ref, gram_ref, mine_ref, away_ref, sems):
    core = place_ref[0]
    width, points = mine_ref.shape
    chips = sems.shape[0] // 2
    chunk = points // chips
    parts = []
    for packed_ref, parity in ((mine_ref, core), (away_ref, 1 - core)):
        copies = []
        for i in range(chips):
            there = pl.ds(pl.multiple_of((2 * i + parity) * chunk, chunk), chunk)
            here = pl.ds(i * chunk, chunk)
            sem = sems.at[len(parts) * chips + i]
            copies.append(pltpu.make_async_copy(snaps_ref.at[:, there], packed_ref.at[:, here], sem))
        parts.append((packed_ref, copies))
    for _, copies in parts:
        for copy in copies:
            copy.start()
    grams = []
    for packed_ref, copies in parts:
        for copy in copies:
            copy.wait()
        rows = packed_ref[...]
        grams.append(bf16_dot_nt(rows, rows))
    gram_ref[...] = jnp.zeros_like(gram_ref)
    gram_ref[:, :width] = grams[0] + grams[1]


def cross_gram_kernel(place_ref, mine_ref, other_ref, gram_ref):
    width = mine_ref.shape[0]
    gram_ref[...] = jnp.zeros_like(gram_ref)

    @pl.when(place_ref[0] == 0)
    def _():
        gram_ref[:, width:] = bf16_dot_nt(mine_ref[...], other_ref[...])

    @pl.when(place_ref[0] != 0)
    def _():
        gram_ref[:, width:] = bf16_dot_nt(other_ref[...], mine_ref[...])


def power_kernel(iters, last, gram_ref, coeffs_ref, out_ref):
    coeffs = coeffs_ref[...].astype(F32)
    width = coeffs.shape[1]
    modes = coeffs.shape[0]
    gram = gram_ref[:, :width]
    scale = 1.0 / math.sqrt(width)
    for _ in range(iters):
        weighted = dot_nn(coeffs, gram)
        solved = cholesky_solves([(dot_nt(weighted, coeffs), weighted)])[0]
        coeffs = solved.astype(BF16).astype(F32) * scale
    if last:
        out_ref[...] = jnp.zeros_like(out_ref)
        out_ref[:, :width] = coeffs
        out_ref[:, width : width + modes] = dot_nt(dot_nn(coeffs, gram), coeffs)
    else:
        out_ref[...] = coeffs


def stack_gram(low, cross, cross_t, high):
    return jnp.concatenate(
        [jnp.concatenate([low, cross], axis=1), jnp.concatenate([cross_t, high], axis=1)], axis=0
    )


def merge_kernel(place_ref, cross_ref, mine_co_ref, other_co_ref, mix_ref, mine_ref, other_hbm, *refs):
    out_refs, (other_ref, sem) = refs[:-2], refs[-2:]
    parts = sem.shape[0]
    part = other_ref.shape[0] // parts
    fetches = [
        pltpu.make_async_copy(other_hbm.at[pl.ds(i * part, part)], other_ref.at[pl.ds(i * part, part)], sem.at[i])
        for i in range(parts)
    ]
    for fetch in fetches:
        fetch.start()
    first = place_ref[0] == 0
    width = mine_ref.shape[0]
    modes = mine_co_ref.shape[0]
    mine_co, other_co = mine_co_ref[...], other_co_ref[...]
    low = jnp.where(first, mine_co, other_co)
    high = jnp.where(first, other_co, mine_co)
    low_co, high_co = low[:, :width], high[:, :width]
    cross = cross_ref[:, width:]
    gram = stack_gram(
        low[:, width : width + modes],
        dot_nt(dot_nn(low_co, cross), high_co),
        dot_nt(dot_nt(high_co, cross), low_co),
        high[:, width : width + modes],
    )
    mixing = mixings([gram], mix_ref[...])[0]
    low_mix = dot_nn(mixing[:, :modes], low_co)
    high_mix = dot_nn(mixing[:, modes:], high_co)
    mine_split = split_two(jnp.where(first, low_mix, high_mix))
    other_split = split_two(jnp.where(first, high_mix, low_mix))
    piece_refs, rest_refs = out_refs[:-2], out_refs[-2:]
    chunk = piece_refs[0].shape[1]
    split = jnp.concatenate([mine_split, other_split], axis=1)
    for fetch in fetches:
        fetch.wait()
    for i, piece_ref in enumerate(piece_refs):
        here = pl.ds(pl.multiple_of((place_ref[1] ^ i) * chunk, chunk), chunk)
        rows = jnp.concatenate([mine_ref[:, here], other_ref[:, here]], axis=0)
        piece = joined(bf16_dot(split, rows)).astype(BF16)
        piece_ref[...] = piece
        for rest_ref, slots in zip(rest_refs, REST_SLOTS):
            if i in slots:
                at = slots.index(i) * modes
                rest_ref[at : at + modes] = piece


NEIGHBOURS = (1, 3)
REST_SLOTS = ((0, 2, 3), (0, 1, 2))


def rows_gram_kernel(place_ref, *refs):
    piece_refs, (_, _, gram_ref, low_rest_ref, high_rest_ref, rows_ref) = refs[:-6], refs[-6:]
    modes = piece_refs[0].shape[0]
    low_rest_ref[3 * modes :] = piece_refs[3][...]
    high_rest_ref[3 * modes :] = piece_refs[1][...]
    for i, piece_ref in enumerate(piece_refs):
        start = pl.multiple_of((place_ref[1] ^ i) * modes, modes)
        rows_ref[pl.ds(start, modes), :] = piece_ref[...]
    rows = rows_ref[...]
    gram = bf16_dot_nt(rows, rows)
    m, h = modes, modes // 2
    gram_ref[:m] = gram[:m]
    gram_ref[m : 2 * m] = gram[m : 2 * m]
    gram_ref[m : 2 * m, :m] = gram[3 * m :, 3 * m :]
    gram_ref[2 * m :, : 2 * m] = gram[2 * m : 2 * m + h, 2 * m :]
    gram_ref[2 * m :, 2 * m :] = gram[2 * m + h : 3 * m, 2 * m :]


def tree_kernel(gram_ref, mix_ref, whole_ref):
    mix = mix_ref[...]
    m = mix.shape[1]
    h = m // 2
    top = gram_ref[:m]
    second = gram_ref[m : 2 * m]
    third = gram_ref[2 * m :]
    low = stack_gram(top[:, :m], top[:, m : 2 * m], top[:, m : 2 * m].T, second[:, m : 2 * m])
    third = jnp.concatenate([third[:, : 2 * m], third[:, 2 * m :]], axis=0)
    high = stack_gram(third[:, :m], third[:, m:], third[:, m:].T, second[:, :m])
    cross = jnp.concatenate([top[:, 2 * m :], second[:, 2 * m :]], axis=0)
    low_mix, high_mix = mixings([low, high], mix)
    gram = stack_gram(
        dot_nt(dot_nn(low_mix, low), low_mix),
        dot_nt(dot_nn(low_mix, cross), high_mix),
        dot_nt(dot_nt(high_mix, cross), low_mix),
        dot_nt(dot_nn(high_mix, high), high_mix),
    )
    last = mixings([gram], mix)[0]
    whole_ref[...] = jnp.concatenate(
        [dot_nn(last[:, :m], low_mix), dot_nn(last[:, m:], high_mix)], axis=1
    )


def finish_kernel(place_ref, whole_ref, *refs):
    own_refs, got_refs = refs[:4], refs[4:7]
    far_ref, low_rest_ref, high_rest_ref, keep_ref, give_ref = refs[7:]
    chips = len(own_refs)
    core, chip = place_ref[0], place_ref[1]
    modes, chunk = own_refs[0].shape
    own = 2 * keep_ref.shape[0]
    mixing = whole_ref[pl.ds(pl.multiple_of(chip * own, own), own), :]
    mixing = jnp.where(chip & 2 != 0, pltpu.roll(mixing, 2 * modes, 1), mixing)
    lanes = lax.broadcasted_iota(jnp.int32, mixing.shape, 1)
    turned = jnp.where(
        (lanes // modes) % 2 == 0,
        pltpu.roll(mixing, (chips - 1) * modes, 1),
        pltpu.roll(mixing, modes, 1),
    )
    split = split_two(jnp.where(chip & 1 != 0, turned, mixing))
    for r in range(chips):
        blocks = [own_refs[r][...]]
        if r == 0:
            blocks += [got_ref[...] for got_ref in got_refs]
        else:
            near = [
                rest_ref[slots.index(apart ^ r) * modes : (slots.index(apart ^ r) + 1) * modes]
                for rest_ref, slots, apart in zip((low_rest_ref, high_rest_ref), REST_SLOTS, NEIGHBOURS)
            ]
            far = {1: low_rest_ref[3 * modes :], 2: far_ref[...], 3: high_rest_ref[3 * modes :]}[r]
            blocks += [near[0], far, near[1]]
        part = joined(bf16_dot(split, jnp.concatenate(blocks, axis=0)))
        low, high = part[: own // 2], part[own // 2 :]
        there = pl.ds(pl.multiple_of((chip ^ r) * chunk, chunk), chunk)
        keep_ref[:, there] = jnp.where(core == 0, low, high)
        give_ref[:, there] = jnp.where(core == 0, high, low)


def assemble_kernel(place_ref, keep_ref, got_ref, out_ref):
    core = place_ref[0]
    chips = out_ref.shape[1] // keep_ref.shape[1] * 2
    chunk = keep_ref.shape[1] // chips
    for i in range(chips):
        here = pl.ds(i * chunk, chunk)
        out_ref[:, pl.ds(pl.multiple_of((2 * i + core) * chunk, chunk), chunk)] = keep_ref[:, here]
        out_ref[:, pl.ds(pl.multiple_of((2 * i + 1 - core) * chunk, chunk), chunk)] = got_ref[:, here]


VMEM = pl.BlockSpec(memory_space=pltpu.VMEM)
SMEM = pl.BlockSpec(memory_space=pltpu.SMEM)
HBM_SPACE = pltpu.HBM


def call(kernel, out_shape, in_specs, name, flops=0, scratch=(), vmem=VMEM_LIMIT, aliases=()):
    return pl.pallas_call(
        kernel,
        out_shape=out_shape,
        in_specs=in_specs,
        out_specs=jax.tree.map(lambda _: VMEM, out_shape),
        scratch_shapes=scratch,
        input_output_aliases=dict(aliases),
        compiler_params=pltpu.CompilerParams(vmem_limit_bytes=vmem),
        cost_estimate=pl.CostEstimate(flops=flops, bytes_accessed=0, transcendentals=0),
        name=name,
    )


def swap(block, axis, mask):
    count = lax.axis_size(axis)
    return lax.ppermute(block, axis, [(i, i ^ mask) for i in range(count)])


def butterfly(block, axis, masks):
    for mask in masks:
        block = block + swap(block, axis, mask)
    return block


EARLY = (1, 4)
LATE = (3, 8, 24)


def shards(snaps, sketch, merge_mix):
    width, points = snaps.shape
    modes = sketch.shape[0]
    snap_count = lax.axis_size("snap")
    chunk = points // snap_count
    chips = snap_count // 2
    position = lax.axis_index("snap")
    place = jnp.stack([position % 2, position // 2]).astype(jnp.int32)
    shape = jax.ShapeDtypeStruct

    own_gram, mine, away = call(
        own_gram_kernel,
        (shape((width, 2 * width), F32),) + (shape((width, chips * chunk), snaps.dtype),) * 2,
        [SMEM, pl.BlockSpec(memory_space=HBM_SPACE)],
        "own_gram",
        scratch=[pltpu.SemaphoreType.DMA((2 * chips,))],
        vmem=2 * VMEM_LIMIT,
    )(place, snaps)
    other = swap(away, "snap", 1)
    own_gram = butterfly(own_gram, "space", EARLY)

    cross = call(
        cross_gram_kernel,
        shape((width, 2 * width), F32),
        [SMEM] + [VMEM] * 2,
        "cross_gram",
    )(place, mine, other)
    cross = butterfly(cross, "snap", (1,))
    grams = butterfly(own_gram + cross, "space", LATE)
    crossed = butterfly(grams, "space", EARLY)

    work = 4 * 10**9
    half = call(
        functools.partial(power_kernel, ITERS // 2, False),
        shape((modes, width), F32),
        [VMEM] * 2,
        "power_first",
        work,
    )(grams, sketch)
    coeffs = call(
        functools.partial(power_kernel, ITERS - ITERS // 2, True),
        shape((modes, 2 * width), F32),
        [VMEM] * 2,
        "power_last",
        work,
    )(grams, half)
    other_coeffs = swap(coeffs, "snap", 1)

    piece = shape((modes, chunk), BF16)
    rest = shape((4 * modes, chunk), BF16)
    *pieces, low_rest, high_rest = call(
        merge_kernel,
        (piece,) * chips + (rest,) * 2,
        [SMEM] + [VMEM] * 5 + [pl.BlockSpec(memory_space=HBM_SPACE)],
        "merge",
        scratch=[pltpu.VMEM(other.shape, BF16), pltpu.SemaphoreType.DMA((4,))],
        vmem=2 * VMEM_LIMIT,
    )(place, crossed, coeffs, other_coeffs, merge_mix, mine, other)

    got = [swap(pieces[i], "snap", 2 * i) for i in range(1, chips)]
    gram, low_rest, high_rest = call(
        rows_gram_kernel,
        (shape((5 * modes // 2, chips * modes), F32), rest, rest),
        [SMEM] + [VMEM] * (chips + 2),
        "rows_gram",
        scratch=[pltpu.VMEM((chips * modes, chunk), BF16)],
        aliases={chips + 1: 1, chips + 2: 2},
    )(place, pieces[0], *got, low_rest, high_rest)
    gram = butterfly(gram, "snap", (1,))
    far = swap(pieces[0], "snap", 4)
    low_rest = swap(low_rest, "snap", 2)
    high_rest = swap(high_rest, "snap", 6)
    gram = butterfly(gram, "space", EARLY + LATE)
    gram = butterfly(gram, "snap", (2, 6))

    whole = call(
        tree_kernel, shape((modes, chips * modes), F32), [VMEM] * 2, "tree", 21 * work // 10
    )(gram, merge_mix)
    half_out = shape((modes // snap_count, points // 2), F32)
    keep, give = call(
        finish_kernel,
        (half_out, half_out),
        [SMEM] + [VMEM] * (2 * chips + 3),
        "finish",
    )(place, whole, *pieces, *got, far, low_rest, high_rest)
    return call(
        assemble_kernel,
        shape((modes // snap_count, points), F32),
        [SMEM] + [VMEM] * 2,
        "assemble",
    )(place, keep, swap(give, "snap", 1))


def solution(mesh):
    in_specs = (P("snap", "space"), P(None, "snap"), P())
    out_specs = P("snap", "space")
    return jax.shard_map(shards, mesh=mesh, in_specs=in_specs, out_specs=out_specs, check_vma=False)
```

profile of v0, /device:TPU:17, one launch (start us, length us, event | category | flops | bytes accessed | tf_op | source)
XLA Modules:
  0.0 111.5 jit_solution(794086719651166877)
XLA Ops:
  0.0 0.1 pad_add_fusion.place_ref
  0.1 4.0 %own_gram.1 = (f32[64,128]{1,0:T(8,128)S(1)}, bf16[64,16384]{1,0:T(8,128)(2,1)S(1)}, bf16[64,16384]{1,0:T(8,128)(2,1)S(1)}) custom-call(s32[2]{0:T(128)S(1)} %pad_add_fusion.place_ref, bf16[64,32768]{1,0:T(8,128)(2,1)} %snaps_ref.1), custom_call_target="tpu_custom_call" | custom-call | tf_op jit(solution)/shard_map/own_gram/pallas_call | solution.py:361
  4.1 0.8 collective-permute-start.2
  4.8 1.0 collective-permute-start
  5.9 1.8 %collective-permute-done = f32[64,128]{1,0:T(8,128)S(1)} collective-permute-done((f32[64,128]{1,0:T(8,128)S(1)}, f32[64,128]{1,0:T(8,128)S(1)}, u32[]{:S(2)}, u32[]{:S(2)}) %collective-permute-start) | collective-permute-done | bytes 32800 | tf_op jit(solution)/shard_map/ppermute | solution.py:338
  7.6 1.6 %collective-permute-start.1 = (f32[64,128]{1,0:T(8,128)S(1)}, f32[64,128]{1,0:T(8,128)S(1)}, u32[]{:S(2)}, u32[]{:S(2)}) collective-permute-start(f32[64,128]{1,0:T(8,128)S(1)} %add.57), channel_id=1, source_target_pairs={{0,32},{8,40},{16,48},{24,56},{32,0},{40,8},{48,16},{56,24},{64,96... | collective-permute-start | bytes 98312 | tf_op jit(solution)/shard_map/ppermute | solution.py:338
  9.3 0.0 collective-permute-done.2.other_ref.other_hbm
  9.3 1.3 %cross_gram.1 = f32[64,128]{1,0:T(8,128)S(1)} custom-call(s32[2]{0:T(128)S(1)} %pad_add_fusion.place_ref, bf16[64,16384]{1,0:T(8,128)(2,1)S(1)} %get-tuple-element.20.mine_ref, bf16[64,16384]{1,0:T(8,128)(2,1)S(1)} %collective-permute-done.2.other_ref.other_hbm), custom_call_target="tpu_custom_call" | custom-call | tf_op jit(solution)/shard_map/cross_gram/pallas_call | solution.py:372
  10.6 0.0 copy-done
  10.6 1.6 %collective-permute-start.3 = (f32[64,128]{1,0:T(8,128)S(1)}, f32[64,128]{1,0:T(8,128)S(1)}, u32[]{:S(2)}, u32[]{:S(2)}) collective-permute-start(f32[64,128]{1,0:T(8,128)S(1)} %cross_gram.1), channel_id=1, source_target_pairs={{0,1},{1,0},{2,3},{3,2},{4,5},{5,4},{6,7},{7,6},{8,9},{9,8},{10,11... | collective-permute-start | bytes 98312 | tf_op jit(solution)/shard_map/ppermute | solution.py:338
  12.2 0.0 collective-permute-done.1
  12.2 0.9 collective-permute-done.3
  13.0 0.3 collective-permute-start.4
  13.3 2.6 %collective-permute-done.4 = f32[64,128]{1,0:T(8,128)S(1)} collective-permute-done((f32[64,128]{1,0:T(8,128)S(1)}, f32[64,128]{1,0:T(8,128)S(1)}, u32[]{:S(2)}, u32[]{:S(2)}) %collective-permute-start.4) | collective-permute-done | bytes 32800 | tf_op jit(solution)/shard_map/ppermute | solution.py:338
  15.9 3.0 %collective-permute-start.5 = (f32[64,128]{1,0:T(8,128)S(1)}, f32[64,128]{1,0:T(8,128)S(1)}, u32[]{:S(2)}, u32[]{:S(2)}) collective-permute-start(f32[64,128]{1,0:T(8,128)S(1)} %add.61), channel_id=1, source_target_pairs={{0,64},{8,72},{16,80},{24,88},{32,96},{40,104},{48,112},{56,120},{... | collective-permute-start | bytes 98312 | tf_op jit(solution)/shard_map/ppermute | solution.py:338
  18.9 1.3 %collective-permute-done.5 = f32[64,128]{1,0:T(8,128)S(1)} collective-permute-done((f32[64,128]{1,0:T(8,128)S(1)}, f32[64,128]{1,0:T(8,128)S(1)}, u32[]{:S(2)}, u32[]{:S(2)}) %collective-permute-start.5) | collective-permute-done | bytes 32800 | tf_op jit(solution)/shard_map/ppermute | solution.py:338
  20.2 4.5 %collective-permute-start.6 = (f32[64,128]{1,0:T(8,128)S(1)}, f32[64,128]{1,0:T(8,128)S(1)}, u32[]{:S(2)}, u32[]{:S(2)}) collective-permute-start(f32[64,128]{1,0:T(8,128)S(1)} %add.62), channel_id=1, source_target_pairs={{0,192},{8,200},{16,208},{24,216},{32,224},{40,232},{48,240},{56,2... | collective-permute-start | bytes 98312 | tf_op jit(solution)/shard_map/ppermute | solution.py:338
  24.7 1.7 %collective-permute-done.6 = f32[64,128]{1,0:T(8,128)S(1)} collective-permute-done((f32[64,128]{1,0:T(8,128)S(1)}, f32[64,128]{1,0:T(8,128)S(1)}, u32[]{:S(2)}, u32[]{:S(2)}) %collective-permute-start.6) | collective-permute-done | bytes 32800 | tf_op jit(solution)/shard_map/ppermute | solution.py:338
  26.4 2.2 %collective-permute-start.7 = (f32[64,128]{1,0:T(8,128)S(1)}, f32[64,128]{1,0:T(8,128)S(1)}, u32[]{:S(2)}, u32[]{:S(2)}) collective-permute-start(f32[64,128]{1,0:T(8,128)S(1)} %add.63.gram_ref), channel_id=1, source_target_pairs={{0,8},{8,0},{16,24},{24,16},{32,40},{40,32},{48,56},{56,48},{64,72... | collective-permute-start | bytes 98312 | tf_op jit(solution)/shard_map/ppermute | solution.py:338
  28.6 0.0 copy-done.1
  28.6 2.8 %power_first.1.coeffs_ref = f32[32,64]{1,0:T(8,128)S(1)} custom-call(f32[64,128]{1,0:T(8,128)S(1)} %add.63.gram_ref, bf16[32,64]{1,0:T(8,128)(2,1)S(1)} %copy-done.1), custom_call_target="tpu_custom_call" | custom-call | flops 4000000000 | tf_op jit(solution)/shard_map/power_first/pallas_call | solution.py:383
  31.3 0.0 collective-permute-done.7
  31.4 0.0 copy-start.2
  31.4 0.5 collective-permute-start.8
  31.8 3.1 %power_last.1.mine_co_ref = f32[32,128]{1,0:T(8,128)S(1)} custom-call(f32[64,128]{1,0:T(8,128)S(1)} %add.63.gram_ref, f32[32,64]{1,0:T(8,128)S(1)} %power_first.1.coeffs_ref), custom_call_target="tpu_custom_call" | custom-call | flops 4000000000 | tf_op jit(solution)/shard_map/power_last/pallas_call | solution.py:390
  35.0 4.5 %collective-permute-start.9 = (f32[32,128]{1,0:T(8,128)S(1)}, f32[32,128]{1,0:T(8,128)S(1)}, u32[]{:S(2)}, u32[]{:S(2)}) collective-permute-start(f32[32,128]{1,0:T(8,128)S(1)} %power_last.1.mine_co_ref), channel_id=1, source_target_pairs={{0,1},{1,0},{2,3},{3,2},{4,5},{5,4},{6,7},{7,6},{8,9},{9,8},{10,11... | collective-permute-start | bytes 49160 | tf_op jit(solution)/shard_map/ppermute | solution.py:338
  39.5 0.1 copy.6.mix_ref
  39.6 0.0 collective-permute-done.8
  39.6 0.7 collective-permute-done.9.other_co_ref
  40.3 4.5 %merge.1 = (bf16[32,4096]{1,0:T(8,128)(2,1)S(1)}, bf16[32,4096]{1,0:T(8,128)(2,1)S(1)}, bf16[32,4096]{1,0:T(8,128)(2,1)S(1)}, bf16[32,4096]{1,0:T(8,128)(2,1)S(1...) custom-call(s32[2]{0:T(128)S(1)} %pad_add_fusion.place_ref, f32[64,128]{1,0:T(8,128)S(1)} %add.65.cross_ref, ...), custom_call_target="tpu_custom_call" | custom-call | tf_op jit(solution)/shard_map/merge/pallas_call | solution.py:401
  44.8 1.5 %collective-permute-start.10 = (bf16[32,4096]{1,0:T(8,128)(2,1)S(1)}, bf16[32,4096]{1,0:T(8,128)(2,1)S(1)}, u32[]{:S(2)}, u32[]{:S(2)}) collective-permute-start(bf16[32,4096]{1,0:T(8,128)(2,1)S(1)} %get-tuple-element.23.refs_1_), channel_id=1, source_target_pairs={{0,2},{1,3},{2,0},{3,1},{4,6},{5,7},{6,4},{7,5},{8,10},{9,11},{10,... | collective-permute-start | bytes 786440 | tf_op jit(solution)/shard_map/ppermute | solution.py:338
  46.3 2.5 %collective-permute-start.11 = (bf16[32,4096]{1,0:T(8,128)(2,1)S(1)}, bf16[32,4096]{1,0:T(8,128)(2,1)S(1)}, u32[]{:S(2)}, u32[]{:S(2)}) collective-permute-start(bf16[32,4096]{1,0:T(8,128)(2,1)S(1)} %get-tuple-element.24.refs_2_), channel_id=1, source_target_pairs={{0,4},{1,5},{2,6},{3,7},{4,0},{5,1},{6,2},{7,3},{8,12},{9,13},{10,... | collective-permute-start | bytes 786440 | tf_op jit(solution)/shard_map/ppermute | solution.py:338
  48.8 0.2 collective-permute-start.12
  49.0 3.7 %collective-permute-done.10.refs_1_.refs_4_ = bf16[32,4096]{1,0:T(8,128)(2,1)S(1)} collective-permute-done((bf16[32,4096]{1,0:T(8,128)(2,1)S(1)}, bf16[32,4096]{1,0:T(8,128)(2,1)S(1)}, u32[]{:S(2)}, u32[]{:S(2)}) %collective-permute-start.10) | collective-permute-done | bytes 262176 | tf_op jit(solution)/shard_map/ppermute | solution.py:338
  52.6 7.9 %collective-permute-done.11.refs_2_.refs_5_ = bf16[32,4096]{1,0:T(8,128)(2,1)S(1)} collective-permute-done((bf16[32,4096]{1,0:T(8,128)(2,1)S(1)}, bf16[32,4096]{1,0:T(8,128)(2,1)S(1)}, u32[]{:S(2)}, u32[]{:S(2)}) %collective-permute-start.11) | collective-permute-done | bytes 262176 | tf_op jit(solution)/shard_map/ppermute | solution.py:338
  60.5 2.0 %collective-permute-done.12.refs_3_.refs_6_ = bf16[32,4096]{1,0:T(8,128)(2,1)S(1)} collective-permute-done((bf16[32,4096]{1,0:T(8,128)(2,1)S(1)}, bf16[32,4096]{1,0:T(8,128)(2,1)S(1)}, u32[]{:S(2)}, u32[]{:S(2)}) %collective-permute-start.12) | collective-permute-done | bytes 262176 | tf_op jit(solution)/shard_map/ppermute | solution.py:338
  62.5 1.1 %rows_gram.1 = (f32[80,128]{1,0:T(8,128)S(1)}, bf16[128,4096]{1,0:T(8,128)(2,1)S(1)}, bf16[128,4096]{1,0:T(8,128)(2,1)S(1)}) custom-call(s32[2]{0:T(128)S(1)} %pad_add_fusion.place_ref, bf16[32,4096]{1,0:T(8,128)(2,1)S(1)} %get-tuple-element.22.refs_0_, ...), custom_call_target="tpu_custom_call", output_to_operand_aliasing={{1}: (5, {}), {2}: (6, {})} | custom-call | tf_op jit(solution)/shard_map/rows_gram/pallas_call | solution.py:411
  63.6 1.9 %collective-permute-start.13 = (f32[80,128]{1,0:T(8,128)S(1)}, f32[80,128]{1,0:T(8,128)S(1)}, u32[]{:S(2)}, u32[]{:S(2)}) collective-permute-start(f32[80,128]{1,0:T(8,128)S(1)} %get-tuple-element.28), channel_id=1, source_target_pairs={{0,1},{1,0},{2,3},{3,2},{4,5},{5,4},{6,7},{7,6},{8,9},{9,8},{10,11... | collective-permute-start | bytes 122888 | tf_op jit(solution)/shard_map/ppermute | solution.py:338
  65.5 0.9 collective-permute-done.13
  66.4 0.8 collective-permute-start.14
  67.2 0.0 collective-permute-start.22
  67.2 0.2 collective-permute-start.23
  67.4 1.8 %collective-permute-done.14 = f32[80,128]{1,0:T(8,128)S(1)} collective-permute-done((f32[80,128]{1,0:T(8,128)S(1)}, f32[80,128]{1,0:T(8,128)S(1)}, u32[]{:S(2)}, u32[]{:S(2)}) %collective-permute-start.14) | collective-permute-done | bytes 40992 | tf_op jit(solution)/shard_map/ppermute | solution.py:338
  69.2 0.6 collective-permute-start.15
  69.9 2.5 %collective-permute-done.15 = f32[80,128]{1,0:T(8,128)S(1)} collective-permute-done((f32[80,128]{1,0:T(8,128)S(1)}, f32[80,128]{1,0:T(8,128)S(1)}, u32[]{:S(2)}, u32[]{:S(2)}) %collective-permute-start.15) | collective-permute-done | bytes 40992 | tf_op jit(solution)/shard_map/ppermute | solution.py:338
  72.4 0.0 collective-permute-start.16
  72.4 3.1 %collective-permute-done.16 = f32[80,128]{1,0:T(8,128)S(1)} collective-permute-done((f32[80,128]{1,0:T(8,128)S(1)}, f32[80,128]{1,0:T(8,128)S(1)}, u32[]{:S(2)}, u32[]{:S(2)}) %collective-permute-start.16) | collective-permute-done | bytes 40992 | tf_op jit(solution)/shard_map/ppermute | solution.py:338
  75.5 2.0 %collective-permute-start.17 = (f32[80,128]{1,0:T(8,128)S(1)}, f32[80,128]{1,0:T(8,128)S(1)}, u32[]{:S(2)}, u32[]{:S(2)}) collective-permute-start(f32[80,128]{1,0:T(8,128)S(1)} %add.69), channel_id=1, source_target_pairs={{0,64},{8,72},{16,80},{24,88},{32,96},{40,104},{48,112},{56,120},{... | collective-permute-start | bytes 122888 | tf_op jit(solution)/shard_map/ppermute | solution.py:338
  77.5 2.5 %collective-permute-done.17 = f32[80,128]{1,0:T(8,128)S(1)} collective-permute-done((f32[80,128]{1,0:T(8,128)S(1)}, f32[80,128]{1,0:T(8,128)S(1)}, u32[]{:S(2)}, u32[]{:S(2)}) %collective-permute-start.17) | collective-permute-done | bytes 40992 | tf_op jit(solution)/shard_map/ppermute | solution.py:338
  80.0 3.4 %collective-permute-start.18 = (f32[80,128]{1,0:T(8,128)S(1)}, f32[80,128]{1,0:T(8,128)S(1)}, u32[]{:S(2)}, u32[]{:S(2)}) collective-permute-start(f32[80,128]{1,0:T(8,128)S(1)} %add.70), channel_id=1, source_target_pairs={{0,192},{8,200},{16,208},{24,216},{32,224},{40,232},{48,240},{56,2... | collective-permute-start | bytes 122888 | tf_op jit(solution)/shard_map/ppermute | solution.py:338
  83.4 1.6 %collective-permute-done.18 = f32[80,128]{1,0:T(8,128)S(1)} collective-permute-done((f32[80,128]{1,0:T(8,128)S(1)}, f32[80,128]{1,0:T(8,128)S(1)}, u32[]{:S(2)}, u32[]{:S(2)}) %collective-permute-start.18) | collective-permute-done | bytes 40992 | tf_op jit(solution)/shard_map/ppermute | solution.py:338
  85.0 0.0 collective-permute-start.19
  85.0 7.2 %collective-permute-done.19 = f32[80,128]{1,0:T(8,128)S(1)} collective-permute-done((f32[80,128]{1,0:T(8,128)S(1)}, f32[80,128]{1,0:T(8,128)S(1)}, u32[]{:S(2)}, u32[]{:S(2)}) %collective-permute-start.19) | collective-permute-done | bytes 40992 | tf_op jit(solution)/shard_map/ppermute | solution.py:338
  92.2 0.2 collective-permute-start.20
  92.4 1.9 %collective-permute-start.21 = (bf16[32,4096]{1,0:T(8,128)(2,1)S(1)}, bf16[32,4096]{1,0:T(8,128)(2,1)S(1)}, u32[]{:S(2)}, u32[]{:S(2)}) collective-permute-start(bf16[32,4096]{1,0:T(8,128)(2,1)S(1)} %get-tuple-element.22.refs_0_), channel_id=1, source_target_pairs={{0,4},{1,5},{2,6},{3,7},{4,0},{5,1},{6,2},{7,3},{8,12},{9,13},{10,... | collective-permute-start | bytes 786440 | tf_op jit(solution)/shard_map/ppermute | solution.py:338
  94.3 2.0 %collective-permute-done.20 = f32[80,128]{1,0:T(8,128)S(1)} collective-permute-done((f32[80,128]{1,0:T(8,128)S(1)}, f32[80,128]{1,0:T(8,128)S(1)}, u32[]{:S(2)}, u32[]{:S(2)}) %collective-permute-start.20) | collective-permute-done | bytes 40992 | tf_op jit(solution)/shard_map/ppermute | solution.py:338
  96.3 4.4 %tree.1.whole_ref = f32[32,128]{1,0:T(8,128)S(1)} custom-call(f32[80,128]{1,0:T(8,128)S(1)} %add.73.gram_ref, f32[64,32]{1,0:T(8,128)S(1)} %copy.6.mix_ref), custom_call_target="tpu_custom_call" | custom-call | flops 8400000000 | tf_op jit(solution)/shard_map/tree/pallas_call | solution.py:426
  100.6 0.0 collective-permute-done.21.refs_7_
  100.6 0.1 collective-permute-done.22.refs_8_
  100.7 0.0 collective-permute-done.23.refs_9_
  100.7 1.3 %finish.1 = (f32[4,16384]{1,0:T(4,128)S(1)}, f32[4,16384]{1,0:T(4,128)S(1)}) custom-call(s32[2]{0:T(128)S(1)} %pad_add_fusion.place_ref, f32[32,128]{1,0:T(8,128)S(1)} %tree.1.whole_ref, bf16[32,4096]{1,0:T(8,128)(2,1)S(1)} %get-tuple-element.22.refs_0_, bf16[32,4096]{1,0:T(8,128)(2,1)S(1)} %get-tuple-element.23.refs_1_, ...), custom_call_target="tpu_custom_call" | custom-call | tf_op jit(solution)/shard_map/finish/pallas_call | solution.py:430
  102.1 6.9 %collective-permute-start.24 = (f32[4,16384]{1,0:T(4,128)S(1)}, f32[4,16384]{1,0:T(4,128)S(1)}, u32[]{:S(2)}, u32[]{:S(2)}) collective-permute-start(f32[4,16384]{1,0:T(4,128)S(1)} %get-tuple-element.32), channel_id=1, source_target_pairs={{0,1},{1,0},{2,3},{3,2},{4,5},{5,4},{6,7},{7,6},{8,9},{9,8},{10,11... | collective-permute-start | bytes 786440 | tf_op jit(solution)/shard_map/ppermute | solution.py:338
  108.9 1.2 %collective-permute-done.24.got_ref = f32[4,16384]{1,0:T(4,128)S(1)} collective-permute-done((f32[4,16384]{1,0:T(4,128)S(1)}, f32[4,16384]{1,0:T(4,128)S(1)}, u32[]{:S(2)}, u32[]{:S(2)}) %collective-permute-start.24) | collective-permute-done | bytes 262176 | tf_op jit(solution)/shard_map/ppermute | solution.py:338
  110.1 1.4 %assemble.1 = f32[4,32768]{1,0:T(4,128)} custom-call(s32[2]{0:T(128)S(1)} %pad_add_fusion.place_ref, f32[4,16384]{1,0:T(4,128)S(1)} %get-tuple-element.31.keep_ref, f32[4,16384]{1,0:T(4,128)S(1)} %collective-permute-done.24.got_ref), custom_call_target="tpu_custom_call" | custom-call | tf_op jit(solution)/shard_map/assemble/pallas_call | solution.py:436
  (18 shorter events, 0.1 us)
Async XLA Ops:
  4.1 5.2 %collective-permute-start.2 = (bf16[64,16384]{1,0:T(8,128)(2,1)S(1)}, bf16[64,16384]{1,0:T(8,128)(2,1)S(1)}, u32[]{:S(2)}, u32[]{:S(2)}) collective-permute-start(bf16[64,16384]{1,0:T(8,128)(2,1)S(1)} %get-tuple-element.21), channel_id=1, source_target_pairs={{0,1},{1,0},{2,3},{3,2},{4,5},{5,4},{6,7},{7,6},{8,9},{9,8},{10,11... | collective-permute-start | bytes 6291464 | tf_op jit(solution)/shard_map/ppermute | solution.py:338
  4.8 2.8 %collective-permute-start = (f32[64,128]{1,0:T(8,128)S(1)}, f32[64,128]{1,0:T(8,128)S(1)}, u32[]{:S(2)}, u32[]{:S(2)}) collective-permute-start(f32[64,128]{1,0:T(8,128)S(1)} %get-tuple-element.19), channel_id=1, source_target_pairs={{0,8},{8,0},{16,24},{24,16},{32,40},{40,32},{48,56},{56,48},{64,72... | collective-permute-start | bytes 98312 | tf_op jit(solution)/shard_map/ppermute | solution.py:338
  7.6 4.6 %collective-permute-start.1 = (f32[64,128]{1,0:T(8,128)S(1)}, f32[64,128]{1,0:T(8,128)S(1)}, u32[]{:S(2)}, u32[]{:S(2)}) collective-permute-start(f32[64,128]{1,0:T(8,128)S(1)} %add.57), channel_id=1, source_target_pairs={{0,32},{8,40},{16,48},{24,56},{32,0},{40,8},{48,16},{56,24},{64,96... | collective-permute-start | bytes 98312 | tf_op jit(solution)/shard_map/ppermute | solution.py:338
  9.3 1.3 %copy-start = (bf16[64,16384]{1,0:T(8,128)(2,1)}, bf16[64,16384]{1,0:T(8,128)(2,1)S(1)}, u32[]{:S(2)}) copy-start(bf16[64,16384]{1,0:T(8,128)(2,1)S(1)} %collective-permute-done.2.other_ref.other_hbm) | copy-start | bytes 6291460
  9.3 19.3 %copy-start.1 = (bf16[32,64]{1,0:T(8,128)(2,1)S(1)}, bf16[32,64]{1,0:T(8,128)(2,1)}, u32[]{:S(2)}) copy-start(bf16[32,64]{1,0:T(8,128)(2,1)} %coeffs_ref.1) | copy-start | bytes 12292
  10.6 2.4 %collective-permute-start.3 = (f32[64,128]{1,0:T(8,128)S(1)}, f32[64,128]{1,0:T(8,128)S(1)}, u32[]{:S(2)}, u32[]{:S(2)}) collective-permute-start(f32[64,128]{1,0:T(8,128)S(1)} %cross_gram.1), channel_id=1, source_target_pairs={{0,1},{1,0},{2,3},{3,2},{4,5},{5,4},{6,7},{7,6},{8,9},{9,8},{10,11... | collective-permute-start | bytes 98312 | tf_op jit(solution)/shard_map/ppermute | solution.py:338
  13.0 2.9 %collective-permute-start.4 = (f32[64,128]{1,0:T(8,128)S(1)}, f32[64,128]{1,0:T(8,128)S(1)}, u32[]{:S(2)}, u32[]{:S(2)}) collective-permute-start(f32[64,128]{1,0:T(8,128)S(1)} %add_add_fusion), channel_id=1, source_target_pairs={{0,24},{8,16},{16,8},{24,0},{32,56},{40,48},{48,40},{56,32},{64,88... | collective-permute-start | bytes 98312 | tf_op jit(solution)/shard_map/ppermute | solution.py:338
  15.9 4.3 %collective-permute-start.5 = (f32[64,128]{1,0:T(8,128)S(1)}, f32[64,128]{1,0:T(8,128)S(1)}, u32[]{:S(2)}, u32[]{:S(2)}) collective-permute-start(f32[64,128]{1,0:T(8,128)S(1)} %add.61), channel_id=1, source_target_pairs={{0,64},{8,72},{16,80},{24,88},{32,96},{40,104},{48,112},{56,120},{... | collective-permute-start | bytes 98312 | tf_op jit(solution)/shard_map/ppermute | solution.py:338
  20.2 6.1 %collective-permute-start.6 = (f32[64,128]{1,0:T(8,128)S(1)}, f32[64,128]{1,0:T(8,128)S(1)}, u32[]{:S(2)}, u32[]{:S(2)}) collective-permute-start(f32[64,128]{1,0:T(8,128)S(1)} %add.62), channel_id=1, source_target_pairs={{0,192},{8,200},{16,208},{24,216},{32,224},{40,232},{48,240},{56,2... | collective-permute-start | bytes 98312 | tf_op jit(solution)/shard_map/ppermute | solution.py:338
  26.4 5.0 %collective-permute-start.7 = (f32[64,128]{1,0:T(8,128)S(1)}, f32[64,128]{1,0:T(8,128)S(1)}, u32[]{:S(2)}, u32[]{:S(2)}) collective-permute-start(f32[64,128]{1,0:T(8,128)S(1)} %add.63.gram_ref), channel_id=1, source_target_pairs={{0,8},{8,0},{16,24},{24,16},{32,40},{40,32},{48,56},{56,48},{64,72... | collective-permute-start | bytes 98312 | tf_op jit(solution)/shard_map/ppermute | solution.py:338
  31.4 8.1 %copy-start.2 = (f32[64,32]{0,1:T(8,128)S(1)}, f32[64,32]{0,1:T(8,128)}, u32[]{:S(2)}) copy-start(f32[64,32]{0,1:T(8,128)} %param.5) | copy-start | bytes 24580
  31.4 8.2 %collective-permute-start.8 = (f32[64,128]{1,0:T(8,128)S(1)}, f32[64,128]{1,0:T(8,128)S(1)}, u32[]{:S(2)}, u32[]{:S(2)}) collective-permute-start(f32[64,128]{1,0:T(8,128)S(1)} %add.64), channel_id=1, source_target_pairs={{0,32},{8,40},{16,48},{24,56},{32,0},{40,8},{48,16},{56,24},{64,96... | collective-permute-start | bytes 98312 | tf_op jit(solution)/shard_map/ppermute | solution.py:338
  35.0 5.4 %collective-permute-start.9 = (f32[32,128]{1,0:T(8,128)S(1)}, f32[32,128]{1,0:T(8,128)S(1)}, u32[]{:S(2)}, u32[]{:S(2)}) collective-permute-start(f32[32,128]{1,0:T(8,128)S(1)} %power_last.1.mine_co_ref), channel_id=1, source_target_pairs={{0,1},{1,0},{2,3},{3,2},{4,5},{5,4},{6,7},{7,6},{8,9},{9,8},{10,11... | collective-permute-start | bytes 49160 | tf_op jit(solution)/shard_map/ppermute | solution.py:338
  44.8 7.8 %collective-permute-start.10 = (bf16[32,4096]{1,0:T(8,128)(2,1)S(1)}, bf16[32,4096]{1,0:T(8,128)(2,1)S(1)}, u32[]{:S(2)}, u32[]{:S(2)}) collective-permute-start(bf16[32,4096]{1,0:T(8,128)(2,1)S(1)} %get-tuple-element.23.refs_1_), channel_id=1, source_target_pairs={{0,2},{1,3},{2,0},{3,1},{4,6},{5,7},{6,4},{7,5},{8,10},{9,11},{10,... | collective-permute-start | bytes 786440 | tf_op jit(solution)/shard_map/ppermute | solution.py:338
  46.3 14.2 %collective-permute-start.11 = (bf16[32,4096]{1,0:T(8,128)(2,1)S(1)}, bf16[32,4096]{1,0:T(8,128)(2,1)S(1)}, u32[]{:S(2)}, u32[]{:S(2)}) collective-permute-start(bf16[32,4096]{1,0:T(8,128)(2,1)S(1)} %get-tuple-element.24.refs_2_), channel_id=1, source_target_pairs={{0,4},{1,5},{2,6},{3,7},{4,0},{5,1},{6,2},{7,3},{8,12},{9,13},{10,... | collective-permute-start | bytes 786440 | tf_op jit(solution)/shard_map/ppermute | solution.py:338
  48.8 13.7 %collective-permute-start.12 = (bf16[32,4096]{1,0:T(8,128)(2,1)S(1)}, bf16[32,4096]{1,0:T(8,128)(2,1)S(1)}, u32[]{:S(2)}, u32[]{:S(2)}) collective-permute-start(bf16[32,4096]{1,0:T(8,128)(2,1)S(1)} %get-tuple-element.25.refs_3_), channel_id=1, source_target_pairs={{0,6},{1,7},{2,4},{3,5},{4,2},{5,3},{6,0},{7,1},{8,14},{9,15},{10,... | collective-permute-start | bytes 786440 | tf_op jit(solution)/shard_map/ppermute | solution.py:338
  63.6 2.7 %collective-permute-start.13 = (f32[80,128]{1,0:T(8,128)S(1)}, f32[80,128]{1,0:T(8,128)S(1)}, u32[]{:S(2)}, u32[]{:S(2)}) collective-permute-start(f32[80,128]{1,0:T(8,128)S(1)} %get-tuple-element.28), channel_id=1, source_target_pairs={{0,1},{1,0},{2,3},{3,2},{4,5},{5,4},{6,7},{7,6},{8,9},{9,8},{10,11... | collective-permute-start | bytes 122888 | tf_op jit(solution)/shard_map/ppermute | solution.py:338
  66.4 2.9 %collective-permute-start.14 = (f32[80,128]{1,0:T(8,128)S(1)}, f32[80,128]{1,0:T(8,128)S(1)}, u32[]{:S(2)}, u32[]{:S(2)}) collective-permute-start(f32[80,128]{1,0:T(8,128)S(1)} %add.66), channel_id=1, source_target_pairs={{0,8},{8,0},{16,24},{24,16},{32,40},{40,32},{48,56},{56,48},{64,72... | collective-permute-start | bytes 122888 | tf_op jit(solution)/shard_map/ppermute | solution.py:338
  67.2 33.5 %collective-permute-start.22 = (bf16[128,4096]{1,0:T(8,128)(2,1)S(1)}, bf16[128,4096]{1,0:T(8,128)(2,1)S(1)}, u32[]{:S(2)}, u32[]{:S(2)}) collective-permute-start(bf16[128,4096]{1,0:T(8,128)(2,1)S(1)} %get-tuple-element.29), channel_id=1, source_target_pairs={{0,2},{1,3},{2,0},{3,1},{4,6},{5,7},{6,4},{7,5},{8,10},{9,11},{10,... | collective-permute-start | bytes 3145736 | tf_op jit(solution)/shard_map/ppermute | solution.py:338
  67.2 33.5 %collective-permute-start.23 = (bf16[128,4096]{1,0:T(8,128)(2,1)S(1)}, bf16[128,4096]{1,0:T(8,128)(2,1)S(1)}, u32[]{:S(2)}, u32[]{:S(2)}) collective-permute-start(bf16[128,4096]{1,0:T(8,128)(2,1)S(1)} %get-tuple-element.30), channel_id=1, source_target_pairs={{0,6},{1,7},{2,4},{3,5},{4,2},{5,3},{6,0},{7,1},{8,14},{9,15},{10,... | collective-permute-start | bytes 3145736 | tf_op jit(solution)/shard_map/ppermute | solution.py:338
  69.2 3.1 %collective-permute-start.15 = (f32[80,128]{1,0:T(8,128)S(1)}, f32[80,128]{1,0:T(8,128)S(1)}, u32[]{:S(2)}, u32[]{:S(2)}) collective-permute-start(f32[80,128]{1,0:T(8,128)S(1)} %add.67), channel_id=1, source_target_pairs={{0,32},{8,40},{16,48},{24,56},{32,0},{40,8},{48,16},{56,24},{64,96... | collective-permute-start | bytes 122888 | tf_op jit(solution)/shard_map/ppermute | solution.py:338
  72.4 3.1 %collective-permute-start.16 = (f32[80,128]{1,0:T(8,128)S(1)}, f32[80,128]{1,0:T(8,128)S(1)}, u32[]{:S(2)}, u32[]{:S(2)}) collective-permute-start(f32[80,128]{1,0:T(8,128)S(1)} %add.68), channel_id=1, source_target_pairs={{0,24},{8,16},{16,8},{24,0},{32,56},{40,48},{48,40},{56,32},{64,88... | collective-permute-start | bytes 122888 | tf_op jit(solution)/shard_map/ppermute | solution.py:338
  75.5 4.5 %collective-permute-start.17 = (f32[80,128]{1,0:T(8,128)S(1)}, f32[80,128]{1,0:T(8,128)S(1)}, u32[]{:S(2)}, u32[]{:S(2)}) collective-permute-start(f32[80,128]{1,0:T(8,128)S(1)} %add.69), channel_id=1, source_target_pairs={{0,64},{8,72},{16,80},{24,88},{32,96},{40,104},{48,112},{56,120},{... | collective-permute-start | bytes 122888 | tf_op jit(solution)/shard_map/ppermute | solution.py:338
  80.0 5.0 %collective-permute-start.18 = (f32[80,128]{1,0:T(8,128)S(1)}, f32[80,128]{1,0:T(8,128)S(1)}, u32[]{:S(2)}, u32[]{:S(2)}) collective-permute-start(f32[80,128]{1,0:T(8,128)S(1)} %add.70), channel_id=1, source_target_pairs={{0,192},{8,200},{16,208},{24,216},{32,224},{40,232},{48,240},{56,2... | collective-permute-start | bytes 122888 | tf_op jit(solution)/shard_map/ppermute | solution.py:338
  85.0 7.2 %collective-permute-start.19 = (f32[80,128]{1,0:T(8,128)S(1)}, f32[80,128]{1,0:T(8,128)S(1)}, u32[]{:S(2)}, u32[]{:S(2)}) collective-permute-start(f32[80,128]{1,0:T(8,128)S(1)} %add.71), channel_id=1, source_target_pairs={{0,2},{1,3},{2,0},{3,1},{4,6},{5,7},{6,4},{7,5},{8,10},{9,11},{10,... | collective-permute-start | bytes 122888 | tf_op jit(solution)/shard_map/ppermute | solution.py:338
  92.2 4.1 %collective-permute-start.20 = (f32[80,128]{1,0:T(8,128)S(1)}, f32[80,128]{1,0:T(8,128)S(1)}, u32[]{:S(2)}, u32[]{:S(2)}) collective-permute-start(f32[80,128]{1,0:T(8,128)S(1)} %add.72), channel_id=1, source_target_pairs={{0,6},{1,7},{2,4},{3,5},{4,2},{5,3},{6,0},{7,1},{8,14},{9,15},{10,... | collective-permute-start | bytes 122888 | tf_op jit(solution)/shard_map/ppermute | solution.py:338
  92.4 8.3 %collective-permute-start.21 = (bf16[32,4096]{1,0:T(8,128)(2,1)S(1)}, bf16[32,4096]{1,0:T(8,128)(2,1)S(1)}, u32[]{:S(2)}, u32[]{:S(2)}) collective-permute-start(bf16[32,4096]{1,0:T(8,128)(2,1)S(1)} %get-tuple-element.22.refs_0_), channel_id=1, source_target_pairs={{0,4},{1,5},{2,6},{3,7},{4,0},{5,1},{6,2},{7,3},{8,12},{9,13},{10,... | collective-permute-start | bytes 786440 | tf_op jit(solution)/shard_map/ppermute | solution.py:338
  102.1 8.0 %collective-permute-start.24 = (f32[4,16384]{1,0:T(4,128)S(1)}, f32[4,16384]{1,0:T(4,128)S(1)}, u32[]{:S(2)}, u32[]{:S(2)}) collective-permute-start(f32[4,16384]{1,0:T(4,128)S(1)} %get-tuple-element.32), channel_id=1, source_target_pairs={{0,1},{1,0},{2,3},{3,2},{4,5},{5,4},{6,7},{7,6},{8,9},{9,8},{10,11... | collective-permute-start | bytes 786440 | tf_op jit(solution)/shard_map/ppermute | solution.py:338
where the time goes:
time: 112 us; the launch traced here: 111 us
  waiting for transfers between devices  45.2 us (40%)
  starting transfers between devices  41.9 us (37%)
  Pallas kernels  23.9 us (21%)
    ppermute x25, waiting for transfers between devices, swap(): return lax.ppermute(block, axis, [(i, i ^ mask) for i in range(count)])  45.2 us
    ppermute x25, starting transfers between devices, swap(): return lax.ppermute(block, axis, [(i, i ^ mask) for i in range(count)])  41.9 us
    pallas_call x1, Pallas kernels, shards(): call(merge_kernel, (piece,) * chips + (rest,) * 2, [SMEM] + [VMEM] * 5 +...  4.49 us
    pallas_call x1, Pallas kernels, shards(): call(tree_kernel, shape((modes, chips * modes), F32), [VMEM] * 2, 'tree',...  4.39 us
    pallas_call x1, Pallas kernels, shards(): call(own_gram_kernel, (shape((width, 2 * width), F32),) + (shape((width,...  3.99 us
    pallas_call x1, Pallas kernels, shards(): call(functools.partial(power_kernel, ITERS - ITERS // 2, True), shape((mo...  3.14 us
    pallas_call x1, Pallas kernels, shards(): call(functools.partial(power_kernel, ITERS // 2, False), shape((modes, wi...  2.76 us
  transfers between devices with their start and end apart: 25, of which 19 were waited for; matrix products, arithmetic and copies ran while one was open for 0% of the time, Pallas kernels for 10%

commit v1 on v0

--- a/solution.py
+++ b/solution.py
@@ -375,7 +375,6 @@
         [SMEM] + [VMEM] * 2,
         "cross_gram",
     )(place, mine, other)
-    cross = butterfly(cross, "snap", (1,))
     grams = butterfly(own_gram + cross, "space", LATE)
     crossed = butterfly(grams, "space", EARLY)
 
@@ -394,7 +393,9 @@
         "power_last",
         work,
     )(grams, half)
+    crossed, coeffs = lax.optimization_barrier((crossed, coeffs))
     other_coeffs = swap(coeffs, "snap", 1)
+    crossed = butterfly(crossed, "snap", (1,))
 
     piece = shape((modes, chunk), BF16)
     rest = shape((4 * modes, chunk), BF16)
@@ -417,11 +418,13 @@
         aliases={chips + 1: 1, chips + 2: 2},
     )(place, pieces[0], *got, low_rest, high_rest)
     gram = butterfly(gram, "snap", (1,))
-    far = swap(pieces[0], "snap", 4)
     low_rest = swap(low_rest, "snap", 2)
     high_rest = swap(high_rest, "snap", 6)
+    gram, far = lax.optimization_barrier((gram, pieces[0]))
+    far = swap(far, "snap", 4)
     gram = butterfly(gram, "space", EARLY + LATE)
     gram = butterfly(gram, "snap", (2, 6))
+    gram, far = lax.optimization_barrier((gram, far))
 
     whole = call(
         tree_kernel, shape((modes, chips * modes), F32), [VMEM] * 2, "tree", 21 * work // 10

time: 112 us -> 113 us (level)
  starting transfers between devices: 41.9 us -> 43.4 us
    ppermute x25, starting transfers between devices: 41.9 us -> 43.4 us  [swap(): return lax.ppermute(block, axis, [(i, i ^ mask) for i in range(count)])]
  transfers between devices with their start and end apart: 25 -> 25, of which waited for: 19 -> 18; matrix products, arithmetic and copies ran while one was open for 0% -> 0% of each run, Pallas kernels for 10% -> 10%
where the time goes in v1:
time: 113 us
  waiting for transfers between devices  44.9 us (40%)
  starting transfers between devices  43.4 us (38%)
  Pallas kernels  23.9 us (21%)
    ppermute x25, waiting for transfers between devices, swap(): return lax.ppermute(block, axis, [(i, i ^ mask) for i in range(count)])  44.9 us
    ppermute x25, starting transfers between devices, swap(): return lax.ppermute(block, axis, [(i, i ^ mask) for i in range(count)])  43.4 us
    pallas_call x1, Pallas kernels, shards(): call(merge_kernel, (piece,) * chips + (rest,) * 2, [SMEM] + [VMEM] * 5 +...  4.5 us
    pallas_call x1, Pallas kernels, shards(): call(tree_kernel, shape((modes, chips * modes), F32), [VMEM] * 2, 'tree',...  4.39 us
    pallas_call x1, Pallas kernels, shards(): call(own_gram_kernel, (shape((width, 2 * width), F32),) + (shape((width,...  3.99 us
    pallas_call x1, Pallas kernels, shards(): call(functools.partial(power_kernel, ITERS - ITERS // 2, True), shape((mo...  3.14 us
    pallas_call x1, Pallas kernels, shards(): call(functools.partial(power_kernel, ITERS // 2, False), shape((modes, wi...  2.76 us
  transfers between devices with their start and end apart: 25, of which 18 were waited for; matrix products, arithmetic and copies ran while one was open for 0% of the time, Pallas kernels for 10%

profile of v1, /device:TPU:17, one launch (start us, length us, event | category | flops | bytes accessed | tf_op | source)
XLA Modules:
  0.0 112.6 jit_solution(10470954800544204215)
XLA Ops:
  0.0 0.1 pad_add_fusion.place_ref
  0.1 4.0 %own_gram.1 = (f32[64,128]{1,0:T(8,128)S(1)}, bf16[64,16384]{1,0:T(8,128)(2,1)S(1)}, bf16[64,16384]{1,0:T(8,128)(2,1)S(1)}) custom-call(s32[2]{0:T(128)S(1)} %pad_add_fusion.place_ref, bf16[64,32768]{1,0:T(8,128)(2,1)} %snaps_ref.1), custom_call_target="tpu_custom_call" | custom-call | tf_op jit(solution)/shard_map/own_gram/pallas_call | solution.py:361
  4.1 0.8 collective-permute-start.2
  4.8 1.0 collective-permute-start
  5.9 1.8 %collective-permute-done = f32[64,128]{1,0:T(8,128)S(1)} collective-permute-done((f32[64,128]{1,0:T(8,128)S(1)}, f32[64,128]{1,0:T(8,128)S(1)}, u32[]{:S(2)}, u32[]{:S(2)}) %collective-permute-start) | collective-permute-done | bytes 32800 | tf_op jit(solution)/shard_map/ppermute | solution.py:338
  7.6 1.6 %collective-permute-start.1 = (f32[64,128]{1,0:T(8,128)S(1)}, f32[64,128]{1,0:T(8,128)S(1)}, u32[]{:S(2)}, u32[]{:S(2)}) collective-permute-start(f32[64,128]{1,0:T(8,128)S(1)} %add.57), channel_id=1, source_target_pairs={{0,32},{8,40},{16,48},{24,56},{32,0},{40,8},{48,16},{56,24},{64,96... | collective-permute-start | bytes 98312 | tf_op jit(solution)/shard_map/ppermute | solution.py:338
  9.3 0.0 collective-permute-done.2.other_ref.other_hbm
  9.3 1.3 %cross_gram.1 = f32[64,128]{1,0:T(8,128)S(1)} custom-call(s32[2]{0:T(128)S(1)} %pad_add_fusion.place_ref, bf16[64,16384]{1,0:T(8,128)(2,1)S(1)} %get-tuple-element.26.mine_ref, bf16[64,16384]{1,0:T(8,128)(2,1)S(1)} %collective-permute-done.2.other_ref.other_hbm), custom_call_target="tpu_custom_call" | custom-call | tf_op jit(solution)/shard_map/cross_gram/pallas_call | solution.py:372
  10.6 0.0 copy-done
  10.6 0.0 collective-permute-done.1
  10.6 0.8 collective-permute-start.3
  11.4 2.0 %collective-permute-done.3 = f32[64,128]{1,0:T(8,128)S(1)} collective-permute-done((f32[64,128]{1,0:T(8,128)S(1)}, f32[64,128]{1,0:T(8,128)S(1)}, u32[]{:S(2)}, u32[]{:S(2)}) %collective-permute-start.3) | collective-permute-done | bytes 32800 | tf_op jit(solution)/shard_map/ppermute | solution.py:338
  13.5 3.0 %collective-permute-start.4 = (f32[64,128]{1,0:T(8,128)S(1)}, f32[64,128]{1,0:T(8,128)S(1)}, u32[]{:S(2)}, u32[]{:S(2)}) collective-permute-start(f32[64,128]{1,0:T(8,128)S(1)} %add.60), channel_id=1, source_target_pairs={{0,64},{8,72},{16,80},{24,88},{32,96},{40,104},{48,112},{56,120},{... | collective-permute-start | bytes 98312 | tf_op jit(solution)/shard_map/ppermute | solution.py:338
  16.5 1.3 %collective-permute-done.4 = f32[64,128]{1,0:T(8,128)S(1)} collective-permute-done((f32[64,128]{1,0:T(8,128)S(1)}, f32[64,128]{1,0:T(8,128)S(1)}, u32[]{:S(2)}, u32[]{:S(2)}) %collective-permute-start.4) | collective-permute-done | bytes 32800 | tf_op jit(solution)/shard_map/ppermute | solution.py:338
  17.8 5.2 %collective-permute-start.5 = (f32[64,128]{1,0:T(8,128)S(1)}, f32[64,128]{1,0:T(8,128)S(1)}, u32[]{:S(2)}, u32[]{:S(2)}) collective-permute-start(f32[64,128]{1,0:T(8,128)S(1)} %add.61), channel_id=1, source_target_pairs={{0,192},{8,200},{16,208},{24,216},{32,224},{40,232},{48,240},{56,2... | collective-permute-start | bytes 98312 | tf_op jit(solution)/shard_map/ppermute | solution.py:338
  22.9 1.3 %collective-permute-done.5 = f32[64,128]{1,0:T(8,128)S(1)} collective-permute-done((f32[64,128]{1,0:T(8,128)S(1)}, f32[64,128]{1,0:T(8,128)S(1)}, u32[]{:S(2)}, u32[]{:S(2)}) %collective-permute-start.5) | collective-permute-done | bytes 32800 | tf_op jit(solution)/shard_map/ppermute | solution.py:338
  24.3 2.2 %collective-permute-start.6 = (f32[64,128]{1,0:T(8,128)S(1)}, f32[64,128]{1,0:T(8,128)S(1)}, u32[]{:S(2)}, u32[]{:S(2)}) collective-permute-start(f32[64,128]{1,0:T(8,128)S(1)} %add.62.gram_ref), channel_id=1, source_target_pairs={{0,8},{8,0},{16,24},{24,16},{32,40},{40,32},{48,56},{56,48},{64,72... | collective-permute-start | bytes 98312 | tf_op jit(solution)/shard_map/ppermute | solution.py:338
  26.5 0.0 copy-done.1
  26.5 2.8 %power_first.1.coeffs_ref = f32[32,64]{1,0:T(8,128)S(1)} custom-call(f32[64,128]{1,0:T(8,128)S(1)} %add.62.gram_ref, bf16[32,64]{1,0:T(8,128)(2,1)S(1)} %copy-done.1), custom_call_target="tpu_custom_call" | custom-call | flops 4000000000 | tf_op jit(solution)/shard_map/power_first/pallas_call | solution.py:382
  29.2 0.0 collective-permute-done.6
  29.3 0.0 copy-start.2
  29.3 0.8 collective-permute-start.7
  30.1 3.1 %power_last.1.mine_co_ref = f32[32,128]{1,0:T(8,128)S(1)} custom-call(f32[64,128]{1,0:T(8,128)S(1)} %add.62.gram_ref, f32[32,64]{1,0:T(8,128)S(1)} %power_first.1.coeffs_ref), custom_call_target="tpu_custom_call" | custom-call | flops 4000000000 | tf_op jit(solution)/shard_map/power_last/pallas_call | solution.py:389
  33.2 0.0 collective-permute-done.7
  33.3 6.2 %collective-permute-start.8 = (f32[64,128]{1,0:T(8,128)S(1)}, f32[64,128]{1,0:T(8,128)S(1)}, u32[]{:S(2)}, u32[]{:S(2)}) collective-permute-start(f32[64,128]{1,0:T(8,128)S(1)} %add.64), channel_id=1, source_target_pairs={{0,1},{1,0},{2,3},{3,2},{4,5},{5,4},{6,7},{7,6},{8,9},{9,8},{10,11... | collective-permute-start | bytes 98312 | tf_op jit(solution)/shard_map/ppermute | solution.py:338
  39.5 0.1 collective-permute-start.9
  39.6 0.1 copy.6.mix_ref
  39.6 0.7 collective-permute-done.8
  40.3 0.3 collective-permute-done.9.other_co_ref
  40.6 4.5 %merge.1 = (bf16[32,4096]{1,0:T(8,128)(2,1)S(1)}, bf16[32,4096]{1,0:T(8,128)(2,1)S(1)}, bf16[32,4096]{1,0:T(8,128)(2,1)S(1)}, bf16[32,4096]{1,0:T(8,128)(2,1)S(1...) custom-call(s32[2]{0:T(128)S(1)} %pad_add_fusion.place_ref, f32[64,128]{1,0:T(8,128)S(1)} %add.65.cross_ref, ...), custom_call_target="tpu_custom_call" | custom-call | tf_op jit(solution)/shard_map/merge/pallas_call | solution.py:402
  45.1 1.5 %collective-permute-start.10 = (bf16[32,4096]{1,0:T(8,128)(2,1)S(1)}, bf16[32,4096]{1,0:T(8,128)(2,1)S(1)}, u32[]{:S(2)}, u32[]{:S(2)}) collective-permute-start(bf16[32,4096]{1,0:T(8,128)(2,1)S(1)} %get-tuple-element.31.refs_1_), channel_id=1, source_target_pairs={{0,2},{1,3},{2,0},{3,1},{4,6},{5,7},{6,4},{7,5},{8,10},{9,11},{10,... | collective-permute-start | bytes 786440 | tf_op jit(solution)/shard_map/ppermute | solution.py:338
  46.6 2.5 %collective-permute-start.11 = (bf16[32,4096]{1,0:T(8,128)(2,1)S(1)}, bf16[32,4096]{1,0:T(8,128)(2,1)S(1)}, u32[]{:S(2)}, u32[]{:S(2)}) collective-permute-start(bf16[32,4096]{1,0:T(8,128)(2,1)S(1)} %get-tuple-element.32.refs_2_), channel_id=1, source_target_pairs={{0,4},{1,5},{2,6},{3,7},{4,0},{5,1},{6,2},{7,3},{8,12},{9,13},{10,... | collective-permute-start | bytes 786440 | tf_op jit(solution)/shard_map/ppermute | solution.py:338
  49.1 0.2 collective-permute-start.12
  49.3 3.9 %collective-permute-done.10.refs_1_.refs_4_ = bf16[32,4096]{1,0:T(8,128)(2,1)S(1)} collective-permute-done((bf16[32,4096]{1,0:T(8,128)(2,1)S(1)}, bf16[32,4096]{1,0:T(8,128)(2,1)S(1)}, u32[]{:S(2)}, u32[]{:S(2)}) %collective-permute-start.10) | collective-permute-done | bytes 262176 | tf_op jit(solution)/shard_map/ppermute | solution.py:338
  53.2 7.9 %collective-permute-done.11.refs_2_.refs_5_ = bf16[32,4096]{1,0:T(8,128)(2,1)S(1)} collective-permute-done((bf16[32,4096]{1,0:T(8,128)(2,1)S(1)}, bf16[32,4096]{1,0:T(8,128)(2,1)S(1)}, u32[]{:S(2)}, u32[]{:S(2)}) %collective-permute-start.11) | collective-permute-done | bytes 262176 | tf_op jit(solution)/shard_map/ppermute | solution.py:338
  61.0 2.0 %collective-permute-done.12.refs_3_.refs_6_ = bf16[32,4096]{1,0:T(8,128)(2,1)S(1)} collective-permute-done((bf16[32,4096]{1,0:T(8,128)(2,1)S(1)}, bf16[32,4096]{1,0:T(8,128)(2,1)S(1)}, u32[]{:S(2)}, u32[]{:S(2)}) %collective-permute-start.12) | collective-permute-done | bytes 262176 | tf_op jit(solution)/shard_map/ppermute | solution.py:338
  63.0 1.1 %rows_gram.1 = (f32[80,128]{1,0:T(8,128)S(1)}, bf16[128,4096]{1,0:T(8,128)(2,1)S(1)}, bf16[128,4096]{1,0:T(8,128)(2,1)S(1)}) custom-call(s32[2]{0:T(128)S(1)} %pad_add_fusion.place_ref, bf16[32,4096]{1,0:T(8,128)(2,1)S(1)} %get-tuple-element.38.refs_0_, ...), custom_call_target="tpu_custom_call", output_to_operand_aliasing={{1}: (5, {}), {2}: (6, {})} | custom-call | tf_op jit(solution)/shard_map/rows_gram/pallas_call | solution.py:412
  64.2 1.6 %collective-permute-start.13 = (f32[80,128]{1,0:T(8,128)S(1)}, f32[80,128]{1,0:T(8,128)S(1)}, u32[]{:S(2)}, u32[]{:S(2)}) collective-permute-start(f32[80,128]{1,0:T(8,128)S(1)} %get-tuple-element.36), channel_id=1, source_target_pairs={{0,1},{1,0},{2,3},{3,2},{4,5},{5,4},{6,7},{7,6},{8,9},{9,8},{10,11... | collective-permute-start | bytes 122888 | tf_op jit(solution)/shard_map/ppermute | solution.py:338
  65.8 0.9 collective-permute-done.13
  66.7 0.8 collective-permute-start.14
  67.5 0.0 collective-permute-start.21
  67.5 0.8 collective-permute-start.22
  68.3 2.5 %collective-permute-start.23 = (bf16[128,4096]{1,0:T(8,128)(2,1)S(1)}, bf16[128,4096]{1,0:T(8,128)(2,1)S(1)}, u32[]{:S(2)}, u32[]{:S(2)}) collective-permute-start(bf16[128,4096]{1,0:T(8,128)(2,1)S(1)} %get-tuple-element.42), channel_id=1, source_target_pairs={{0,6},{1,7},{2,4},{3,5},{4,2},{5,3},{6,0},{7,1},{8,14},{9,15},{10,... | collective-permute-start | bytes 3145736 | tf_op jit(solution)/shard_map/ppermute | solution.py:338
  70.8 0.0 collective-permute-done.14
  70.8 0.8 collective-permute-start.15
  71.6 2.4 %collective-permute-done.15 = f32[80,128]{1,0:T(8,128)S(1)} collective-permute-done((f32[80,128]{1,0:T(8,128)S(1)}, f32[80,128]{1,0:T(8,128)S(1)}, u32[]{:S(2)}, u32[]{:S(2)}) %collective-permute-start.15) | collective-permute-done | bytes 40992 | tf_op jit(solution)/shard_map/ppermute | solution.py:338
  74.0 0.0 collective-permute-start.16
  74.1 3.1 %collective-permute-done.16 = f32[80,128]{1,0:T(8,128)S(1)} collective-permute-done((f32[80,128]{1,0:T(8,128)S(1)}, f32[80,128]{1,0:T(8,128)S(1)}, u32[]{:S(2)}, u32[]{:S(2)}) %collective-permute-start.16) | collective-permute-done | bytes 40992 | tf_op jit(solution)/shard_map/ppermute | solution.py:338
  77.2 1.7 %collective-permute-start.17 = (f32[80,128]{1,0:T(8,128)S(1)}, f32[80,128]{1,0:T(8,128)S(1)}, u32[]{:S(2)}, u32[]{:S(2)}) collective-permute-start(f32[80,128]{1,0:T(8,128)S(1)} %add.69), channel_id=1, source_target_pairs={{0,64},{8,72},{16,80},{24,88},{32,96},{40,104},{48,112},{56,120},{... | collective-permute-start | bytes 122888 | tf_op jit(solution)/shard_map/ppermute | solution.py:338
  78.9 2.3 %collective-permute-done.17 = f32[80,128]{1,0:T(8,128)S(1)} collective-permute-done((f32[80,128]{1,0:T(8,128)S(1)}, f32[80,128]{1,0:T(8,128)S(1)}, u32[]{:S(2)}, u32[]{:S(2)}) %collective-permute-start.17) | collective-permute-done | bytes 40992 | tf_op jit(solution)/shard_map/ppermute | solution.py:338
  81.3 4.0 %collective-permute-start.18 = (f32[80,128]{1,0:T(8,128)S(1)}, f32[80,128]{1,0:T(8,128)S(1)}, u32[]{:S(2)}, u32[]{:S(2)}) collective-permute-start(f32[80,128]{1,0:T(8,128)S(1)} %add.70), channel_id=1, source_target_pairs={{0,192},{8,200},{16,208},{24,216},{32,224},{40,232},{48,240},{56,2... | collective-permute-start | bytes 122888 | tf_op jit(solution)/shard_map/ppermute | solution.py:338
  85.3 1.4 %collective-permute-done.18 = f32[80,128]{1,0:T(8,128)S(1)} collective-permute-done((f32[80,128]{1,0:T(8,128)S(1)}, f32[80,128]{1,0:T(8,128)S(1)}, u32[]{:S(2)}, u32[]{:S(2)}) %collective-permute-start.18) | collective-permute-done | bytes 40992 | tf_op jit(solution)/shard_map/ppermute | solution.py:338
  86.7 0.0 collective-permute-start.19
  86.7 10.8 %collective-permute-done.19 = f32[80,128]{1,0:T(8,128)S(1)} collective-permute-done((f32[80,128]{1,0:T(8,128)S(1)}, f32[80,128]{1,0:T(8,128)S(1)}, u32[]{:S(2)}, u32[]{:S(2)}) %collective-permute-start.19) | collective-permute-done | bytes 40992 | tf_op jit(solution)/shard_map/ppermute | solution.py:338
  97.5 2.5 %collective-permute-start.20 = (f32[80,128]{1,0:T(8,128)S(1)}, f32[80,128]{1,0:T(8,128)S(1)}, u32[]{:S(2)}, u32[]{:S(2)}) collective-permute-start(f32[80,128]{1,0:T(8,128)S(1)} %add.72), channel_id=1, source_target_pairs={{0,6},{1,7},{2,4},{3,5},{4,2},{5,3},{6,0},{7,1},{8,14},{9,15},{10,... | collective-permute-start | bytes 122888 | tf_op jit(solution)/shard_map/ppermute | solution.py:338
  100.0 1.6 %collective-permute-done.20 = f32[80,128]{1,0:T(8,128)S(1)} collective-permute-done((f32[80,128]{1,0:T(8,128)S(1)}, f32[80,128]{1,0:T(8,128)S(1)}, u32[]{:S(2)}, u32[]{:S(2)}) %collective-permute-start.20) | collective-permute-done | bytes 40992 | tf_op jit(solution)/shard_map/ppermute | solution.py:338
  101.5 0.0 collective-permute-done.21.refs_7_
  101.5 4.4 %tree.1.whole_ref = f32[32,128]{1,0:T(8,128)S(1)} custom-call(f32[80,128]{1,0:T(8,128)S(1)} %add.73.gram_ref, f32[64,32]{1,0:T(8,128)S(1)} %copy.6.mix_ref), custom_call_target="tpu_custom_call" | custom-call | flops 8400000000 | tf_op jit(solution)/shard_map/tree/pallas_call | solution.py:429
  105.9 0.0 collective-permute-done.22.refs_8_
  105.9 0.1 collective-permute-done.23.refs_9_
  106.0 1.3 %finish.1 = (f32[4,16384]{1,0:T(4,128)S(1)}, f32[4,16384]{1,0:T(4,128)S(1)}) custom-call(s32[2]{0:T(128)S(1)} %pad_add_fusion.place_ref, f32[32,128]{1,0:T(8,128)S(1)} %tree.1.whole_ref, bf16[32,4096]{1,0:T(8,128)(2,1)S(1)} %get-tuple-element.38.refs_0_, bf16[32,4096]{1,0:T(8,128)(2,1)S(1)} %get-tuple-element.31.refs_1_, ...), custom_call_target="tpu_custom_call" | custom-call | tf_op jit(solution)/shard_map/finish/pallas_call | solution.py:433
  107.3 2.7 %collective-permute-start.24 = (f32[4,16384]{1,0:T(4,128)S(1)}, f32[4,16384]{1,0:T(4,128)S(1)}, u32[]{:S(2)}, u32[]{:S(2)}) collective-permute-start(f32[4,16384]{1,0:T(4,128)S(1)} %get-tuple-element.44), channel_id=1, source_target_pairs={{0,1},{1,0},{2,3},{3,2},{4,5},{5,4},{6,7},{7,6},{8,9},{9,8},{10,11... | collective-permute-start | bytes 786440 | tf_op jit(solution)/shard_map/ppermute | solution.py:338
  110.1 1.2 %collective-permute-done.24.got_ref = f32[4,16384]{1,0:T(4,128)S(1)} collective-permute-done((f32[4,16384]{1,0:T(4,128)S(1)}, f32[4,16384]{1,0:T(4,128)S(1)}, u32[]{:S(2)}, u32[]{:S(2)}) %collective-permute-start.24) | collective-permute-done | bytes 262176 | tf_op jit(solution)/shard_map/ppermute | solution.py:338
  111.2 1.4 %assemble.1 = f32[4,32768]{1,0:T(4,128)} custom-call(s32[2]{0:T(128)S(1)} %pad_add_fusion.place_ref, f32[4,16384]{1,0:T(4,128)S(1)} %get-tuple-element.43.keep_ref, f32[4,16384]{1,0:T(4,128)S(1)} %collective-permute-done.24.got_ref), custom_call_target="tpu_custom_call" | custom-call | tf_op jit(solution)/shard_map/assemble/pallas_call | solution.py:439
  (19 shorter events, 0.1 us)
Async XLA Ops:
  4.1 5.2 %collective-permute-start.2 = (bf16[64,16384]{1,0:T(8,128)(2,1)S(1)}, bf16[64,16384]{1,0:T(8,128)(2,1)S(1)}, u32[]{:S(2)}, u32[]{:S(2)}) collective-permute-start(bf16[64,16384]{1,0:T(8,128)(2,1)S(1)} %get-tuple-element.27), channel_id=1, source_target_pairs={{0,1},{1,0},{2,3},{3,2},{4,5},{5,4},{6,7},{7,6},{8,9},{9,8},{10,11... | collective-permute-start | bytes 6291464 | tf_op jit(solution)/shard_map/ppermute | solution.py:338
  4.8 2.8 %collective-permute-start = (f32[64,128]{1,0:T(8,128)S(1)}, f32[64,128]{1,0:T(8,128)S(1)}, u32[]{:S(2)}, u32[]{:S(2)}) collective-permute-start(f32[64,128]{1,0:T(8,128)S(1)} %get-tuple-element.25), channel_id=1, source_target_pairs={{0,8},{8,0},{16,24},{24,16},{32,40},{40,32},{48,56},{56,48},{64,72... | collective-permute-start | bytes 98312 | tf_op jit(solution)/shard_map/ppermute | solution.py:338
  7.6 3.0 %collective-permute-start.1 = (f32[64,128]{1,0:T(8,128)S(1)}, f32[64,128]{1,0:T(8,128)S(1)}, u32[]{:S(2)}, u32[]{:S(2)}) collective-permute-start(f32[64,128]{1,0:T(8,128)S(1)} %add.57), channel_id=1, source_target_pairs={{0,32},{8,40},{16,48},{24,56},{32,0},{40,8},{48,16},{56,24},{64,96... | collective-permute-start | bytes 98312 | tf_op jit(solution)/shard_map/ppermute | solution.py:338
  9.3 1.3 %copy-start = (bf16[64,16384]{1,0:T(8,128)(2,1)}, bf16[64,16384]{1,0:T(8,128)(2,1)S(1)}, u32[]{:S(2)}) copy-start(bf16[64,16384]{1,0:T(8,128)(2,1)S(1)} %collective-permute-done.2.other_ref.other_hbm) | copy-start | bytes 6291460
  9.3 17.2 %copy-start.1 = (bf16[32,64]{1,0:T(8,128)(2,1)S(1)}, bf16[32,64]{1,0:T(8,128)(2,1)}, u32[]{:S(2)}) copy-start(bf16[32,64]{1,0:T(8,128)(2,1)} %coeffs_ref.1) | copy-start | bytes 12292
  10.6 2.9 %collective-permute-start.3 = (f32[64,128]{1,0:T(8,128)S(1)}, f32[64,128]{1,0:T(8,128)S(1)}, u32[]{:S(2)}, u32[]{:S(2)}) collective-permute-start(f32[64,128]{1,0:T(8,128)S(1)} %add_add_fusion), channel_id=1, source_target_pairs={{0,24},{8,16},{16,8},{24,0},{32,56},{40,48},{48,40},{56,32},{64,88... | collective-permute-start | bytes 98312 | tf_op jit(solution)/shard_map/ppermute | solution.py:338
  13.5 4.3 %collective-permute-start.4 = (f32[64,128]{1,0:T(8,128)S(1)}, f32[64,128]{1,0:T(8,128)S(1)}, u32[]{:S(2)}, u32[]{:S(2)}) collective-permute-start(f32[64,128]{1,0:T(8,128)S(1)} %add.60), channel_id=1, source_target_pairs={{0,64},{8,72},{16,80},{24,88},{32,96},{40,104},{48,112},{56,120},{... | collective-permute-start | bytes 98312 | tf_op jit(solution)/shard_map/ppermute | solution.py:338
  17.8 6.5 %collective-permute-start.5 = (f32[64,128]{1,0:T(8,128)S(1)}, f32[64,128]{1,0:T(8,128)S(1)}, u32[]{:S(2)}, u32[]{:S(2)}) collective-permute-start(f32[64,128]{1,0:T(8,128)S(1)} %add.61), channel_id=1, source_target_pairs={{0,192},{8,200},{16,208},{24,216},{32,224},{40,232},{48,240},{56,2... | collective-permute-start | bytes 98312 | tf_op jit(solution)/shard_map/ppermute | solution.py:338
  24.3 5.0 %collective-permute-start.6 = (f32[64,128]{1,0:T(8,128)S(1)}, f32[64,128]{1,0:T(8,128)S(1)}, u32[]{:S(2)}, u32[]{:S(2)}) collective-permute-start(f32[64,128]{1,0:T(8,128)S(1)} %add.62.gram_ref), channel_id=1, source_target_pairs={{0,8},{8,0},{16,24},{24,16},{32,40},{40,32},{48,56},{56,48},{64,72... | collective-permute-start | bytes 98312 | tf_op jit(solution)/shard_map/ppermute | solution.py:338
  29.3 10.3 %copy-start.2 = (f32[64,32]{0,1:T(8,128)S(1)}, f32[64,32]{0,1:T(8,128)}, u32[]{:S(2)}) copy-start(f32[64,32]{0,1:T(8,128)} %param.5) | copy-start | bytes 24580
  29.3 4.0 %collective-permute-start.7 = (f32[64,128]{1,0:T(8,128)S(1)}, f32[64,128]{1,0:T(8,128)S(1)}, u32[]{:S(2)}, u32[]{:S(2)}) collective-permute-start(f32[64,128]{1,0:T(8,128)S(1)} %add.63), channel_id=1, source_target_pairs={{0,32},{8,40},{16,48},{24,56},{32,0},{40,8},{48,16},{56,24},{64,96... | collective-permute-start | bytes 98312 | tf_op jit(solution)/shard_map/ppermute | solution.py:338
  33.3 7.1 %collective-permute-start.8 = (f32[64,128]{1,0:T(8,128)S(1)}, f32[64,128]{1,0:T(8,128)S(1)}, u32[]{:S(2)}, u32[]{:S(2)}) collective-permute-start(f32[64,128]{1,0:T(8,128)S(1)} %add.64), channel_id=1, source_target_pairs={{0,1},{1,0},{2,3},{3,2},{4,5},{5,4},{6,7},{7,6},{8,9},{9,8},{10,11... | collective-permute-start | bytes 98312 | tf_op jit(solution)/shard_map/ppermute | solution.py:338
  39.5 1.2 %collective-permute-start.9 = (f32[32,128]{1,0:T(8,128)S(1)}, f32[32,128]{1,0:T(8,128)S(1)}, u32[]{:S(2)}, u32[]{:S(2)}) collective-permute-start(f32[32,128]{1,0:T(8,128)S(1)} %power_last.1.mine_co_ref), channel_id=1, source_target_pairs={{0,1},{1,0},{2,3},{3,2},{4,5},{5,4},{6,7},{7,6},{8,9},{9,8},{10,11... | collective-permute-start | bytes 49160 | tf_op jit(solution)/shard_map/ppermute | solution.py:338
  45.1 8.0 %collective-permute-start.10 = (bf16[32,4096]{1,0:T(8,128)(2,1)S(1)}, bf16[32,4096]{1,0:T(8,128)(2,1)S(1)}, u32[]{:S(2)}, u32[]{:S(2)}) collective-permute-start(bf16[32,4096]{1,0:T(8,128)(2,1)S(1)} %get-tuple-element.31.refs_1_), channel_id=1, source_target_pairs={{0,2},{1,3},{2,0},{3,1},{4,6},{5,7},{6,4},{7,5},{8,10},{9,11},{10,... | collective-permute-start | bytes 786440 | tf_op jit(solution)/shard_map/ppermute | solution.py:338
  46.6 14.4 %collective-permute-start.11 = (bf16[32,4096]{1,0:T(8,128)(2,1)S(1)}, bf16[32,4096]{1,0:T(8,128)(2,1)S(1)}, u32[]{:S(2)}, u32[]{:S(2)}) collective-permute-start(bf16[32,4096]{1,0:T(8,128)(2,1)S(1)} %get-tuple-element.32.refs_2_), channel_id=1, source_target_pairs={{0,4},{1,5},{2,6},{3,7},{4,0},{5,1},{6,2},{7,3},{8,12},{9,13},{10,... | collective-permute-start | bytes 786440 | tf_op jit(solution)/shard_map/ppermute | solution.py:338
  49.1 13.9 %collective-permute-start.12 = (bf16[32,4096]{1,0:T(8,128)(2,1)S(1)}, bf16[32,4096]{1,0:T(8,128)(2,1)S(1)}, u32[]{:S(2)}, u32[]{:S(2)}) collective-permute-start(bf16[32,4096]{1,0:T(8,128)(2,1)S(1)} %get-tuple-element.33.refs_3_), channel_id=1, source_target_pairs={{0,6},{1,7},{2,4},{3,5},{4,2},{5,3},{6,0},{7,1},{8,14},{9,15},{10,... | collective-permute-start | bytes 786440 | tf_op jit(solution)/shard_map/ppermute | solution.py:338
  64.2 2.5 %collective-permute-start.13 = (f32[80,128]{1,0:T(8,128)S(1)}, f32[80,128]{1,0:T(8,128)S(1)}, u32[]{:S(2)}, u32[]{:S(2)}) collective-permute-start(f32[80,128]{1,0:T(8,128)S(1)} %get-tuple-element.36), channel_id=1, source_target_pairs={{0,1},{1,0},{2,3},{3,2},{4,5},{5,4},{6,7},{7,6},{8,9},{9,8},{10,11... | collective-permute-start | bytes 122888 | tf_op jit(solution)/shard_map/ppermute | solution.py:338
  66.7 4.1 %collective-permute-start.14 = (f32[80,128]{1,0:T(8,128)S(1)}, f32[80,128]{1,0:T(8,128)S(1)}, u32[]{:S(2)}, u32[]{:S(2)}) collective-permute-start(f32[80,128]{1,0:T(8,128)S(1)} %add.66), channel_id=1, source_target_pairs={{0,8},{8,0},{16,24},{24,16},{32,40},{40,32},{48,56},{56,48},{64,72... | collective-permute-start | bytes 122888 | tf_op jit(solution)/shard_map/ppermute | solution.py:338
  67.5 34.0 %collective-permute-start.21 = (bf16[32,4096]{1,0:T(8,128)(2,1)S(1)}, bf16[32,4096]{1,0:T(8,128)(2,1)S(1)}, u32[]{:S(2)}, u32[]{:S(2)}) collective-permute-start(bf16[32,4096]{1,0:T(8,128)(2,1)S(1)} %get-tuple-element.38.refs_0_), channel_id=1, source_target_pairs={{0,4},{1,5},{2,6},{3,7},{4,0},{5,1},{6,2},{7,3},{8,12},{9,13},{10,... | collective-permute-start | bytes 786440 | tf_op jit(solution)/shard_map/ppermute | solution.py:338
  67.5 38.4 %collective-permute-start.22 = (bf16[128,4096]{1,0:T(8,128)(2,1)S(1)}, bf16[128,4096]{1,0:T(8,128)(2,1)S(1)}, u32[]{:S(2)}, u32[]{:S(2)}) collective-permute-start(bf16[128,4096]{1,0:T(8,128)(2,1)S(1)} %get-tuple-element.41), channel_id=1, source_target_pairs={{0,2},{1,3},{2,0},{3,1},{4,6},{5,7},{6,4},{7,5},{8,10},{9,11},{10,... | collective-permute-start | bytes 3145736 | tf_op jit(solution)/shard_map/ppermute | solution.py:338
  68.3 37.7 %collective-permute-start.23 = (bf16[128,4096]{1,0:T(8,128)(2,1)S(1)}, bf16[128,4096]{1,0:T(8,128)(2,1)S(1)}, u32[]{:S(2)}, u32[]{:S(2)}) collective-permute-start(bf16[128,4096]{1,0:T(8,128)(2,1)S(1)} %get-tuple-element.42), channel_id=1, source_target_pairs={{0,6},{1,7},{2,4},{3,5},{4,2},{5,3},{6,0},{7,1},{8,14},{9,15},{10,... | collective-permute-start | bytes 3145736 | tf_op jit(solution)/shard_map/ppermute | solution.py:338
  70.8 3.2 %collective-permute-start.15 = (f32[80,128]{1,0:T(8,128)S(1)}, f32[80,128]{1,0:T(8,128)S(1)}, u32[]{:S(2)}, u32[]{:S(2)}) collective-permute-start(f32[80,128]{1,0:T(8,128)S(1)} %add.67), channel_id=1, source_target_pairs={{0,32},{8,40},{16,48},{24,56},{32,0},{40,8},{48,16},{56,24},{64,96... | collective-permute-start | bytes 122888 | tf_op jit(solution)/shard_map/ppermute | solution.py:338
  74.0 3.1 %collective-permute-start.16 = (f32[80,128]{1,0:T(8,128)S(1)}, f32[80,128]{1,0:T(8,128)S(1)}, u32[]{:S(2)}, u32[]{:S(2)}) collective-permute-start(f32[80,128]{1,0:T(8,128)S(1)} %add.68), channel_id=1, source_target_pairs={{0,24},{8,16},{16,8},{24,0},{32,56},{40,48},{48,40},{56,32},{64,88... | collective-permute-start | bytes 122888 | tf_op jit(solution)/shard_map/ppermute | solution.py:338
  77.2 4.0 %collective-permute-start.17 = (f32[80,128]{1,0:T(8,128)S(1)}, f32[80,128]{1,0:T(8,128)S(1)}, u32[]{:S(2)}, u32[]{:S(2)}) collective-permute-start(f32[80,128]{1,0:T(8,128)S(1)} %add.69), channel_id=1, source_target_pairs={{0,64},{8,72},{16,80},{24,88},{32,96},{40,104},{48,112},{56,120},{... | collective-permute-start | bytes 122888 | tf_op jit(solution)/shard_map/ppermute | solution.py:338
  81.3 5.4 %collective-permute-start.18 = (f32[80,128]{1,0:T(8,128)S(1)}, f32[80,128]{1,0:T(8,128)S(1)}, u32[]{:S(2)}, u32[]{:S(2)}) collective-permute-start(f32[80,128]{1,0:T(8,128)S(1)} %add.70), channel_id=1, source_target_pairs={{0,192},{8,200},{16,208},{24,216},{32,224},{40,232},{48,240},{56,2... | collective-permute-start | bytes 122888 | tf_op jit(solution)/shard_map/ppermute | solution.py:338
  86.7 10.8 %collective-permute-start.19 = (f32[80,128]{1,0:T(8,128)S(1)}, f32[80,128]{1,0:T(8,128)S(1)}, u32[]{:S(2)}, u32[]{:S(2)}) collective-permute-start(f32[80,128]{1,0:T(8,128)S(1)} %add.71), channel_id=1, source_target_pairs={{0,2},{1,3},{2,0},{3,1},{4,6},{5,7},{6,4},{7,5},{8,10},{9,11},{10,... | collective-permute-start | bytes 122888 | tf_op jit(solution)/shard_map/ppermute | solution.py:338
  97.5 4.1 %collective-permute-start.20 = (f32[80,128]{1,0:T(8,128)S(1)}, f32[80,128]{1,0:T(8,128)S(1)}, u32[]{:S(2)}, u32[]{:S(2)}) collective-permute-start(f32[80,128]{1,0:T(8,128)S(1)} %add.72), channel_id=1, source_target_pairs={{0,6},{1,7},{2,4},{3,5},{4,2},{5,3},{6,0},{7,1},{8,14},{9,15},{10,... | collective-permute-start | bytes 122888 | tf_op jit(solution)/shard_map/ppermute | solution.py:338
  107.3 3.9 %collective-permute-start.24 = (f32[4,16384]{1,0:T(4,128)S(1)}, f32[4,16384]{1,0:T(4,128)S(1)}, u32[]{:S(2)}, u32[]{:S(2)}) collective-permute-start(f32[4,16384]{1,0:T(4,128)S(1)} %get-tuple-element.44), channel_id=1, source_target_pairs={{0,1},{1,0},{2,3},{3,2},{4,5},{5,4},{6,7},{7,6},{8,9},{9,8},{10,11... | collective-permute-start | bytes 786440 | tf_op jit(solution)/shard_map/ppermute | solution.py:338

commit v2 on v0

--- a/solution.py
+++ b/solution.py
@@ -416,15 +416,16 @@
         scratch=[pltpu.VMEM((chips * modes, chunk), BF16)],
         aliases={chips + 1: 1, chips + 2: 2},
     )(place, pieces[0], *got, low_rest, high_rest)
-    gram = butterfly(gram, "snap", (1,))
-    far = swap(pieces[0], "snap", 4)
+    gram = butterfly(gram, "snap", (1, 2))
+    gram, far, low_rest, high_rest = lax.optimization_barrier((gram, pieces[0], low_rest, high_rest))
+    far = swap(far, "snap", 4)
     low_rest = swap(low_rest, "snap", 2)
     high_rest = swap(high_rest, "snap", 6)
+    gram = butterfly(gram, "snap", (6,))
     gram = butterfly(gram, "space", EARLY + LATE)
-    gram = butterfly(gram, "snap", (2, 6))
 
     whole = call(
-        tree_kernel, shape((modes, chips * modes), F32), [VMEM] * 2, "tree", 21 * work // 10
+        tree_kernel, shape((modes, chips * modes), F32), [VMEM] * 2, "tree", 22 * work // 10
     )(gram, merge_mix)
     half_out = shape((modes // snap_count, points // 2), F32)
     keep, give = call(

time: 112 us -> 111 us (level); the launches traced: 111 us -> 109 us
  waiting for transfers between devices: 45.2 us -> 43.7 us
    ppermute x25, waiting for transfers between devices: 45.2 us -> 43.7 us  [swap(): return lax.ppermute(block, axis, [(i, i ^ mask) for i in range(count)])]
  transfers between devices with their start and end apart: 25 -> 25, of which waited for: 19 -> 19; matrix products, arithmetic and copies ran while one was open for 0% -> 0% of each run, Pallas kernels for 10% -> 11%
where the time goes in v2:
time: 111 us; the launch traced here: 109 us
  waiting for transfers between devices  43.7 us (39%)
  starting transfers between devices  41.3 us (37%)
  Pallas kernels  23.9 us (22%)
    ppermute x25, waiting for transfers between devices, swap(): return lax.ppermute(block, axis, [(i, i ^ mask) for i in range(count)])  43.7 us
    ppermute x25, starting transfers between devices, swap(): return lax.ppermute(block, axis, [(i, i ^ mask) for i in range(count)])  41.3 us
    pallas_call x1, Pallas kernels, shards(): call(merge_kernel, (piece,) * chips + (rest,) * 2, [SMEM] + [VMEM] * 5 +...  4.49 us
    pallas_call x1, Pallas kernels, shards(): call(tree_kernel, shape((modes, chips * modes), F32), [VMEM] * 2, 'tree',...  4.39 us
    pallas_call x1, Pallas kernels, shards(): call(own_gram_kernel, (shape((width, 2 * width), F32),) + (shape((width,...  3.99 us
    pallas_call x1, Pallas kernels, shards(): call(functools.partial(power_kernel, ITERS - ITERS // 2, True), shape((mo...  3.14 us
    pallas_call x1, Pallas kernels, shards(): call(functools.partial(power_kernel, ITERS // 2, False), shape((modes, wi...  2.76 us
  transfers between devices with their start and end apart: 25, of which 19 were waited for; matrix products, arithmetic and copies ran while one was open for 0% of the time, Pallas kernels for 11%

profile of v2, /device:TPU:17, one launch (start us, length us, event | category | flops | bytes accessed | tf_op | source)
XLA Modules:
  0.0 109.4 jit_solution(2878387731445457670)
XLA Ops:
  0.0 0.1 pad_add_fusion.place_ref
  0.1 4.0 %own_gram.1 = (f32[64,128]{1,0:T(8,128)S(1)}, bf16[64,16384]{1,0:T(8,128)(2,1)S(1)}, bf16[64,16384]{1,0:T(8,128)(2,1)S(1)}) custom-call(s32[2]{0:T(128)S(1)} %pad_add_fusion.place_ref, bf16[64,32768]{1,0:T(8,128)(2,1)} %snaps_ref.1), custom_call_target="tpu_custom_call" | custom-call | tf_op jit(solution)/shard_map/own_gram/pallas_call | solution.py:361
  4.1 0.8 collective-permute-start.2
  4.8 1.0 collective-permute-start
  5.9 1.8 %collective-permute-done = f32[64,128]{1,0:T(8,128)S(1)} collective-permute-done((f32[64,128]{1,0:T(8,128)S(1)}, f32[64,128]{1,0:T(8,128)S(1)}, u32[]{:S(2)}, u32[]{:S(2)}) %collective-permute-start) | collective-permute-done | bytes 32800 | tf_op jit(solution)/shard_map/ppermute | solution.py:338
  7.6 1.6 %collective-permute-start.1 = (f32[64,128]{1,0:T(8,128)S(1)}, f32[64,128]{1,0:T(8,128)S(1)}, u32[]{:S(2)}, u32[]{:S(2)}) collective-permute-start(f32[64,128]{1,0:T(8,128)S(1)} %add.57), channel_id=1, source_target_pairs={{0,32},{8,40},{16,48},{24,56},{32,0},{40,8},{48,16},{56,24},{64,96... | collective-permute-start | bytes 98312 | tf_op jit(solution)/shard_map/ppermute | solution.py:338
  9.3 0.0 collective-permute-done.2.other_ref.other_hbm
  9.3 1.3 %cross_gram.1 = f32[64,128]{1,0:T(8,128)S(1)} custom-call(s32[2]{0:T(128)S(1)} %pad_add_fusion.place_ref, bf16[64,16384]{1,0:T(8,128)(2,1)S(1)} %get-tuple-element.24.mine_ref, bf16[64,16384]{1,0:T(8,128)(2,1)S(1)} %collective-permute-done.2.other_ref.other_hbm), custom_call_target="tpu_custom_call" | custom-call | tf_op jit(solution)/shard_map/cross_gram/pallas_call | solution.py:372
  10.6 0.0 copy-done
  10.6 1.6 %collective-permute-start.3 = (f32[64,128]{1,0:T(8,128)S(1)}, f32[64,128]{1,0:T(8,128)S(1)}, u32[]{:S(2)}, u32[]{:S(2)}) collective-permute-start(f32[64,128]{1,0:T(8,128)S(1)} %cross_gram.1), channel_id=1, source_target_pairs={{0,1},{1,0},{2,3},{3,2},{4,5},{5,4},{6,7},{7,6},{8,9},{9,8},{10,11... | collective-permute-start | bytes 98312 | tf_op jit(solution)/shard_map/ppermute | solution.py:338
  12.2 0.0 collective-permute-done.1
  12.2 0.9 collective-permute-done.3
  13.0 0.3 collective-permute-start.4
  13.3 2.6 %collective-permute-done.4 = f32[64,128]{1,0:T(8,128)S(1)} collective-permute-done((f32[64,128]{1,0:T(8,128)S(1)}, f32[64,128]{1,0:T(8,128)S(1)}, u32[]{:S(2)}, u32[]{:S(2)}) %collective-permute-start.4) | collective-permute-done | bytes 32800 | tf_op jit(solution)/shard_map/ppermute | solution.py:338
  15.9 3.0 %collective-permute-start.5 = (f32[64,128]{1,0:T(8,128)S(1)}, f32[64,128]{1,0:T(8,128)S(1)}, u32[]{:S(2)}, u32[]{:S(2)}) collective-permute-start(f32[64,128]{1,0:T(8,128)S(1)} %add.61), channel_id=1, source_target_pairs={{0,64},{8,72},{16,80},{24,88},{32,96},{40,104},{48,112},{56,120},{... | collective-permute-start | bytes 98312 | tf_op jit(solution)/shard_map/ppermute | solution.py:338
  18.9 1.3 %collective-permute-done.5 = f32[64,128]{1,0:T(8,128)S(1)} collective-permute-done((f32[64,128]{1,0:T(8,128)S(1)}, f32[64,128]{1,0:T(8,128)S(1)}, u32[]{:S(2)}, u32[]{:S(2)}) %collective-permute-start.5) | collective-permute-done | bytes 32800 | tf_op jit(solution)/shard_map/ppermute | solution.py:338
  20.2 4.5 %collective-permute-start.6 = (f32[64,128]{1,0:T(8,128)S(1)}, f32[64,128]{1,0:T(8,128)S(1)}, u32[]{:S(2)}, u32[]{:S(2)}) collective-permute-start(f32[64,128]{1,0:T(8,128)S(1)} %add.62), channel_id=1, source_target_pairs={{0,192},{8,200},{16,208},{24,216},{32,224},{40,232},{48,240},{56,2... | collective-permute-start | bytes 98312 | tf_op jit(solution)/shard_map/ppermute | solution.py:338
  24.7 1.7 %collective-permute-done.6 = f32[64,128]{1,0:T(8,128)S(1)} collective-permute-done((f32[64,128]{1,0:T(8,128)S(1)}, f32[64,128]{1,0:T(8,128)S(1)}, u32[]{:S(2)}, u32[]{:S(2)}) %collective-permute-start.6) | collective-permute-done | bytes 32800 | tf_op jit(solution)/shard_map/ppermute | solution.py:338
  26.4 2.2 %collective-permute-start.7 = (f32[64,128]{1,0:T(8,128)S(1)}, f32[64,128]{1,0:T(8,128)S(1)}, u32[]{:S(2)}, u32[]{:S(2)}) collective-permute-start(f32[64,128]{1,0:T(8,128)S(1)} %add.63.gram_ref), channel_id=1, source_target_pairs={{0,8},{8,0},{16,24},{24,16},{32,40},{40,32},{48,56},{56,48},{64,72... | collective-permute-start | bytes 98312 | tf_op jit(solution)/shard_map/ppermute | solution.py:338
  28.6 0.0 copy-done.1
  28.6 2.8 %power_first.1.coeffs_ref = f32[32,64]{1,0:T(8,128)S(1)} custom-call(f32[64,128]{1,0:T(8,128)S(1)} %add.63.gram_ref, bf16[32,64]{1,0:T(8,128)(2,1)S(1)} %copy-done.1), custom_call_target="tpu_custom_call" | custom-call | flops 4000000000 | tf_op jit(solution)/shard_map/power_first/pallas_call | solution.py:383
  31.3 0.0 collective-permute-done.7
  31.4 0.0 copy-start.2
  31.4 0.5 collective-permute-start.8
  31.8 3.1 %power_last.1.mine_co_ref = f32[32,128]{1,0:T(8,128)S(1)} custom-call(f32[64,128]{1,0:T(8,128)S(1)} %add.63.gram_ref, f32[32,64]{1,0:T(8,128)S(1)} %power_first.1.coeffs_ref), custom_call_target="tpu_custom_call" | custom-call | flops 4000000000 | tf_op jit(solution)/shard_map/power_last/pallas_call | solution.py:390
  35.0 4.5 %collective-permute-start.9 = (f32[32,128]{1,0:T(8,128)S(1)}, f32[32,128]{1,0:T(8,128)S(1)}, u32[]{:S(2)}, u32[]{:S(2)}) collective-permute-start(f32[32,128]{1,0:T(8,128)S(1)} %power_last.1.mine_co_ref), channel_id=1, source_target_pairs={{0,1},{1,0},{2,3},{3,2},{4,5},{5,4},{6,7},{7,6},{8,9},{9,8},{10,11... | collective-permute-start | bytes 49160 | tf_op jit(solution)/shard_map/ppermute | solution.py:338
  39.5 0.1 copy.6.mix_ref
  39.6 0.0 collective-permute-done.8
  39.6 0.7 collective-permute-done.9.other_co_ref
  40.3 4.5 %merge.1 = (bf16[32,4096]{1,0:T(8,128)(2,1)S(1)}, bf16[32,4096]{1,0:T(8,128)(2,1)S(1)}, bf16[32,4096]{1,0:T(8,128)(2,1)S(1)}, bf16[32,4096]{1,0:T(8,128)(2,1)S(1...) custom-call(s32[2]{0:T(128)S(1)} %pad_add_fusion.place_ref, f32[64,128]{1,0:T(8,128)S(1)} %add.65.cross_ref, ...), custom_call_target="tpu_custom_call" | custom-call | tf_op jit(solution)/shard_map/merge/pallas_call | solution.py:401
  44.8 1.5 %collective-permute-start.10 = (bf16[32,4096]{1,0:T(8,128)(2,1)S(1)}, bf16[32,4096]{1,0:T(8,128)(2,1)S(1)}, u32[]{:S(2)}, u32[]{:S(2)}) collective-permute-start(bf16[32,4096]{1,0:T(8,128)(2,1)S(1)} %get-tuple-element.27.refs_1_), channel_id=1, source_target_pairs={{0,2},{1,3},{2,0},{3,1},{4,6},{5,7},{6,4},{7,5},{8,10},{9,11},{10,... | collective-permute-start | bytes 786440 | tf_op jit(solution)/shard_map/ppermute | solution.py:338
  46.3 2.5 %collective-permute-start.11 = (bf16[32,4096]{1,0:T(8,128)(2,1)S(1)}, bf16[32,4096]{1,0:T(8,128)(2,1)S(1)}, u32[]{:S(2)}, u32[]{:S(2)}) collective-permute-start(bf16[32,4096]{1,0:T(8,128)(2,1)S(1)} %get-tuple-element.28.refs_2_), channel_id=1, source_target_pairs={{0,4},{1,5},{2,6},{3,7},{4,0},{5,1},{6,2},{7,3},{8,12},{9,13},{10,... | collective-permute-start | bytes 786440 | tf_op jit(solution)/shard_map/ppermute | solution.py:338
  48.8 0.2 collective-permute-start.12
  49.0 3.7 %collective-permute-done.10.refs_1_.refs_4_ = bf16[32,4096]{1,0:T(8,128)(2,1)S(1)} collective-permute-done((bf16[32,4096]{1,0:T(8,128)(2,1)S(1)}, bf16[32,4096]{1,0:T(8,128)(2,1)S(1)}, u32[]{:S(2)}, u32[]{:S(2)}) %collective-permute-start.10) | collective-permute-done | bytes 262176 | tf_op jit(solution)/shard_map/ppermute | solution.py:338
  52.6 7.9 %collective-permute-done.11.refs_2_.refs_5_ = bf16[32,4096]{1,0:T(8,128)(2,1)S(1)} collective-permute-done((bf16[32,4096]{1,0:T(8,128)(2,1)S(1)}, bf16[32,4096]{1,0:T(8,128)(2,1)S(1)}, u32[]{:S(2)}, u32[]{:S(2)}) %collective-permute-start.11) | collective-permute-done | bytes 262176 | tf_op jit(solution)/shard_map/ppermute | solution.py:338
  60.5 2.0 %collective-permute-done.12.refs_3_.refs_6_ = bf16[32,4096]{1,0:T(8,128)(2,1)S(1)} collective-permute-done((bf16[32,4096]{1,0:T(8,128)(2,1)S(1)}, bf16[32,4096]{1,0:T(8,128)(2,1)S(1)}, u32[]{:S(2)}, u32[]{:S(2)}) %collective-permute-start.12) | collective-permute-done | bytes 262176 | tf_op jit(solution)/shard_map/ppermute | solution.py:338
  62.5 1.1 %rows_gram.1 = (f32[80,128]{1,0:T(8,128)S(1)}, bf16[128,4096]{1,0:T(8,128)(2,1)S(1)}, bf16[128,4096]{1,0:T(8,128)(2,1)S(1)}) custom-call(s32[2]{0:T(128)S(1)} %pad_add_fusion.place_ref, bf16[32,4096]{1,0:T(8,128)(2,1)S(1)} %get-tuple-element.36.refs_0_, ...), custom_call_target="tpu_custom_call", output_to_operand_aliasing={{1}: (5, {}), {2}: (6, {})} | custom-call | tf_op jit(solution)/shard_map/rows_gram/pallas_call | solution.py:411
  63.6 1.9 %collective-permute-start.13 = (f32[80,128]{1,0:T(8,128)S(1)}, f32[80,128]{1,0:T(8,128)S(1)}, u32[]{:S(2)}, u32[]{:S(2)}) collective-permute-start(f32[80,128]{1,0:T(8,128)S(1)} %get-tuple-element.32), channel_id=1, source_target_pairs={{0,1},{1,0},{2,3},{3,2},{4,5},{5,4},{6,7},{7,6},{8,9},{9,8},{10,11... | collective-permute-start | bytes 122888 | tf_op jit(solution)/shard_map/ppermute | solution.py:338
  65.5 0.9 collective-permute-done.13
  66.4 0.0 collective-permute-start.14
  66.4 2.8 %collective-permute-done.14 = f32[80,128]{1,0:T(8,128)S(1)} collective-permute-done((f32[80,128]{1,0:T(8,128)S(1)}, f32[80,128]{1,0:T(8,128)S(1)}, u32[]{:S(2)}, u32[]{:S(2)}) %collective-permute-start.14) | collective-permute-done | bytes 40992 | tf_op jit(solution)/shard_map/ppermute | solution.py:338
  69.2 0.2 collective-permute-start.15
  69.4 0.0 collective-permute-start.22
  69.4 2.5 %collective-permute-start.23 = (bf16[128,4096]{1,0:T(8,128)(2,1)S(1)}, bf16[128,4096]{1,0:T(8,128)(2,1)S(1)}, u32[]{:S(2)}, u32[]{:S(2)}) collective-permute-start(bf16[128,4096]{1,0:T(8,128)(2,1)S(1)} %get-tuple-element.38), channel_id=1, source_target_pairs={{0,6},{1,7},{2,4},{3,5},{4,2},{5,3},{6,0},{7,1},{8,14},{9,15},{10,... | collective-permute-start | bytes 3145736 | tf_op jit(solution)/shard_map/ppermute | solution.py:338
  71.9 1.4 %collective-permute-done.15 = f32[80,128]{1,0:T(8,128)S(1)} collective-permute-done((f32[80,128]{1,0:T(8,128)S(1)}, f32[80,128]{1,0:T(8,128)S(1)}, u32[]{:S(2)}, u32[]{:S(2)}) %collective-permute-start.15) | collective-permute-done | bytes 40992 | tf_op jit(solution)/shard_map/ppermute | solution.py:338
  73.3 0.8 collective-permute-start.16
  74.2 2.3 %collective-permute-done.16 = f32[80,128]{1,0:T(8,128)S(1)} collective-permute-done((f32[80,128]{1,0:T(8,128)S(1)}, f32[80,128]{1,0:T(8,128)S(1)}, u32[]{:S(2)}, u32[]{:S(2)}) %collective-permute-start.16) | collective-permute-done | bytes 40992 | tf_op jit(solution)/shard_map/ppermute | solution.py:338
  76.5 0.6 collective-permute-start.17
  77.1 2.5 %collective-permute-done.17 = f32[80,128]{1,0:T(8,128)S(1)} collective-permute-done((f32[80,128]{1,0:T(8,128)S(1)}, f32[80,128]{1,0:T(8,128)S(1)}, u32[]{:S(2)}, u32[]{:S(2)}) %collective-permute-start.17) | collective-permute-done | bytes 40992 | tf_op jit(solution)/shard_map/ppermute | solution.py:338
  79.6 0.0 collective-permute-start.18
  79.6 3.1 %collective-permute-done.18 = f32[80,128]{1,0:T(8,128)S(1)} collective-permute-done((f32[80,128]{1,0:T(8,128)S(1)}, f32[80,128]{1,0:T(8,128)S(1)}, u32[]{:S(2)}, u32[]{:S(2)}) %collective-permute-start.18) | collective-permute-done | bytes 40992 | tf_op jit(solution)/shard_map/ppermute | solution.py:338
  82.8 2.0 %collective-permute-start.19 = (f32[80,128]{1,0:T(8,128)S(1)}, f32[80,128]{1,0:T(8,128)S(1)}, u32[]{:S(2)}, u32[]{:S(2)}) collective-permute-start(f32[80,128]{1,0:T(8,128)S(1)} %add.71), channel_id=1, source_target_pairs={{0,64},{8,72},{16,80},{24,88},{32,96},{40,104},{48,112},{56,120},{... | collective-permute-start | bytes 122888 | tf_op jit(solution)/shard_map/ppermute | solution.py:338
  84.7 2.5 %collective-permute-done.19 = f32[80,128]{1,0:T(8,128)S(1)} collective-permute-done((f32[80,128]{1,0:T(8,128)S(1)}, f32[80,128]{1,0:T(8,128)S(1)}, u32[]{:S(2)}, u32[]{:S(2)}) %collective-permute-start.19) | collective-permute-done | bytes 40992 | tf_op jit(solution)/shard_map/ppermute | solution.py:338
  87.3 3.4 %collective-permute-start.20 = (f32[80,128]{1,0:T(8,128)S(1)}, f32[80,128]{1,0:T(8,128)S(1)}, u32[]{:S(2)}, u32[]{:S(2)}) collective-permute-start(f32[80,128]{1,0:T(8,128)S(1)} %add.72), channel_id=1, source_target_pairs={{0,192},{8,200},{16,208},{24,216},{32,224},{40,232},{48,240},{56,2... | collective-permute-start | bytes 122888 | tf_op jit(solution)/shard_map/ppermute | solution.py:338
  90.7 0.0 collective-permute-start.21
  90.7 1.6 %collective-permute-done.20 = f32[80,128]{1,0:T(8,128)S(1)} collective-permute-done((f32[80,128]{1,0:T(8,128)S(1)}, f32[80,128]{1,0:T(8,128)S(1)}, u32[]{:S(2)}, u32[]{:S(2)}) %collective-permute-start.20) | collective-permute-done | bytes 40992 | tf_op jit(solution)/shard_map/ppermute | solution.py:338
  92.2 4.4 %tree.1.whole_ref = f32[32,128]{1,0:T(8,128)S(1)} custom-call(f32[80,128]{1,0:T(8,128)S(1)} %add.73.gram_ref, f32[64,32]{1,0:T(8,128)S(1)} %copy.6.mix_ref), custom_call_target="tpu_custom_call" | custom-call | flops 8800000000 | tf_op jit(solution)/shard_map/tree/pallas_call | solution.py:427
  96.6 2.9 %collective-permute-done.21.refs_7_ = bf16[32,4096]{1,0:T(8,128)(2,1)S(1)} collective-permute-done((bf16[32,4096]{1,0:T(8,128)(2,1)S(1)}, bf16[32,4096]{1,0:T(8,128)(2,1)S(1)}, u32[]{:S(2)}, u32[]{:S(2)}) %collective-permute-start.21) | collective-permute-done | bytes 262176 | tf_op jit(solution)/shard_map/ppermute | solution.py:338
  99.5 0.0 collective-permute-done.22.refs_8_
  99.6 0.0 collective-permute-done.23.refs_9_
  99.6 1.3 %finish.1 = (f32[4,16384]{1,0:T(4,128)S(1)}, f32[4,16384]{1,0:T(4,128)S(1)}) custom-call(s32[2]{0:T(128)S(1)} %pad_add_fusion.place_ref, f32[32,128]{1,0:T(8,128)S(1)} %tree.1.whole_ref, bf16[32,4096]{1,0:T(8,128)(2,1)S(1)} %get-tuple-element.36.refs_0_, bf16[32,4096]{1,0:T(8,128)(2,1)S(1)} %get-tuple-element.27.refs_1_, ...), custom_call_target="tpu_custom_call" | custom-call | tf_op jit(solution)/shard_map/finish/pallas_call | solution.py:431
  100.9 5.9 %collective-permute-start.24 = (f32[4,16384]{1,0:T(4,128)S(1)}, f32[4,16384]{1,0:T(4,128)S(1)}, u32[]{:S(2)}, u32[]{:S(2)}) collective-permute-start(f32[4,16384]{1,0:T(4,128)S(1)} %get-tuple-element.40), channel_id=1, source_target_pairs={{0,1},{1,0},{2,3},{3,2},{4,5},{5,4},{6,7},{7,6},{8,9},{9,8},{10,11... | collective-permute-start | bytes 786440 | tf_op jit(solution)/shard_map/ppermute | solution.py:338
  106.8 1.2 %collective-permute-done.24.got_ref = f32[4,16384]{1,0:T(4,128)S(1)} collective-permute-done((f32[4,16384]{1,0:T(4,128)S(1)}, f32[4,16384]{1,0:T(4,128)S(1)}, u32[]{:S(2)}, u32[]{:S(2)}) %collective-permute-start.24) | collective-permute-done | bytes 262176 | tf_op jit(solution)/shard_map/ppermute | solution.py:338
  108.0 1.4 %assemble.1 = f32[4,32768]{1,0:T(4,128)} custom-call(s32[2]{0:T(128)S(1)} %pad_add_fusion.place_ref, f32[4,16384]{1,0:T(4,128)S(1)} %get-tuple-element.39.keep_ref, f32[4,16384]{1,0:T(4,128)S(1)} %collective-permute-done.24.got_ref), custom_call_target="tpu_custom_call" | custom-call | tf_op jit(solution)/shard_map/assemble/pallas_call | solution.py:437
  (18 shorter events, 0.1 us)
Async XLA Ops:
  4.1 5.2 %collective-permute-start.2 = (bf16[64,16384]{1,0:T(8,128)(2,1)S(1)}, bf16[64,16384]{1,0:T(8,128)(2,1)S(1)}, u32[]{:S(2)}, u32[]{:S(2)}) collective-permute-start(bf16[64,16384]{1,0:T(8,128)(2,1)S(1)} %get-tuple-element.25), channel_id=1, source_target_pairs={{0,1},{1,0},{2,3},{3,2},{4,5},{5,4},{6,7},{7,6},{8,9},{9,8},{10,11... | collective-permute-start | bytes 6291464 | tf_op jit(solution)/shard_map/ppermute | solution.py:338
  4.8 2.8 %collective-permute-start = (f32[64,128]{1,0:T(8,128)S(1)}, f32[64,128]{1,0:T(8,128)S(1)}, u32[]{:S(2)}, u32[]{:S(2)}) collective-permute-start(f32[64,128]{1,0:T(8,128)S(1)} %get-tuple-element.23), channel_id=1, source_target_pairs={{0,8},{8,0},{16,24},{24,16},{32,40},{40,32},{48,56},{56,48},{64,72... | collective-permute-start | bytes 98312 | tf_op jit(solution)/shard_map/ppermute | solution.py:338
  7.6 4.6 %collective-permute-start.1 = (f32[64,128]{1,0:T(8,128)S(1)}, f32[64,128]{1,0:T(8,128)S(1)}, u32[]{:S(2)}, u32[]{:S(2)}) collective-permute-start(f32[64,128]{1,0:T(8,128)S(1)} %add.57), channel_id=1, source_target_pairs={{0,32},{8,40},{16,48},{24,56},{32,0},{40,8},{48,16},{56,24},{64,96... | collective-permute-start | bytes 98312 | tf_op jit(solution)/shard_map/ppermute | solution.py:338
  9.3 1.3 %copy-start = (bf16[64,16384]{1,0:T(8,128)(2,1)}, bf16[64,16384]{1,0:T(8,128)(2,1)S(1)}, u32[]{:S(2)}) copy-start(bf16[64,16384]{1,0:T(8,128)(2,1)S(1)} %collective-permute-done.2.other_ref.other_hbm) | copy-start | bytes 6291460
  9.3 19.3 %copy-start.1 = (bf16[32,64]{1,0:T(8,128)(2,1)S(1)}, bf16[32,64]{1,0:T(8,128)(2,1)}, u32[]{:S(2)}) copy-start(bf16[32,64]{1,0:T(8,128)(2,1)} %coeffs_ref.1) | copy-start | bytes 12292
  10.6 2.4 %collective-permute-start.3 = (f32[64,128]{1,0:T(8,128)S(1)}, f32[64,128]{1,0:T(8,128)S(1)}, u32[]{:S(2)}, u32[]{:S(2)}) collective-permute-start(f32[64,128]{1,0:T(8,128)S(1)} %cross_gram.1), channel_id=1, source_target_pairs={{0,1},{1,0},{2,3},{3,2},{4,5},{5,4},{6,7},{7,6},{8,9},{9,8},{10,11... | collective-permute-start | bytes 98312 | tf_op jit(solution)/shard_map/ppermute | solution.py:338
  13.0 2.9 %collective-permute-start.4 = (f32[64,128]{1,0:T(8,128)S(1)}, f32[64,128]{1,0:T(8,128)S(1)}, u32[]{:S(2)}, u32[]{:S(2)}) collective-permute-start(f32[64,128]{1,0:T(8,128)S(1)} %add_add_fusion), channel_id=1, source_target_pairs={{0,24},{8,16},{16,8},{24,0},{32,56},{40,48},{48,40},{56,32},{64,88... | collective-permute-start | bytes 98312 | tf_op jit(solution)/shard_map/ppermute | solution.py:338
  15.9 4.3 %collective-permute-start.5 = (f32[64,128]{1,0:T(8,128)S(1)}, f32[64,128]{1,0:T(8,128)S(1)}, u32[]{:S(2)}, u32[]{:S(2)}) collective-permute-start(f32[64,128]{1,0:T(8,128)S(1)} %add.61), channel_id=1, source_target_pairs={{0,64},{8,72},{16,80},{24,88},{32,96},{40,104},{48,112},{56,120},{... | collective-permute-start | bytes 98312 | tf_op jit(solution)/shard_map/ppermute | solution.py:338
  20.2 6.1 %collective-permute-start.6 = (f32[64,128]{1,0:T(8,128)S(1)}, f32[64,128]{1,0:T(8,128)S(1)}, u32[]{:S(2)}, u32[]{:S(2)}) collective-permute-start(f32[64,128]{1,0:T(8,128)S(1)} %add.62), channel_id=1, source_target_pairs={{0,192},{8,200},{16,208},{24,216},{32,224},{40,232},{48,240},{56,2... | collective-permute-start | bytes 98312 | tf_op jit(solution)/shard_map/ppermute | solution.py:338
  26.4 5.0 %collective-permute-start.7 = (f32[64,128]{1,0:T(8,128)S(1)}, f32[64,128]{1,0:T(8,128)S(1)}, u32[]{:S(2)}, u32[]{:S(2)}) collective-permute-start(f32[64,128]{1,0:T(8,128)S(1)} %add.63.gram_ref), channel_id=1, source_target_pairs={{0,8},{8,0},{16,24},{24,16},{32,40},{40,32},{48,56},{56,48},{64,72... | collective-permute-start | bytes 98312 | tf_op jit(solution)/shard_map/ppermute | solution.py:338
  31.4 8.1 %copy-start.2 = (f32[64,32]{0,1:T(8,128)S(1)}, f32[64,32]{0,1:T(8,128)}, u32[]{:S(2)}) copy-start(f32[64,32]{0,1:T(8,128)} %param.5) | copy-start | bytes 24580
  31.4 8.2 %collective-permute-start.8 = (f32[64,128]{1,0:T(8,128)S(1)}, f32[64,128]{1,0:T(8,128)S(1)}, u32[]{:S(2)}, u32[]{:S(2)}) collective-permute-start(f32[64,128]{1,0:T(8,128)S(1)} %add.64), channel_id=1, source_target_pairs={{0,32},{8,40},{16,48},{24,56},{32,0},{40,8},{48,16},{56,24},{64,96... | collective-permute-start | bytes 98312 | tf_op jit(solution)/shard_map/ppermute | solution.py:338
  35.0 5.4 %collective-permute-start.9 = (f32[32,128]{1,0:T(8,128)S(1)}, f32[32,128]{1,0:T(8,128)S(1)}, u32[]{:S(2)}, u32[]{:S(2)}) collective-permute-start(f32[32,128]{1,0:T(8,128)S(1)} %power_last.1.mine_co_ref), channel_id=1, source_target_pairs={{0,1},{1,0},{2,3},{3,2},{4,5},{5,4},{6,7},{7,6},{8,9},{9,8},{10,11... | collective-permute-start | bytes 49160 | tf_op jit(solution)/shard_map/ppermute | solution.py:338
  44.8 7.8 %collective-permute-start.10 = (bf16[32,4096]{1,0:T(8,128)(2,1)S(1)}, bf16[32,4096]{1,0:T(8,128)(2,1)S(1)}, u32[]{:S(2)}, u32[]{:S(2)}) collective-permute-start(bf16[32,4096]{1,0:T(8,128)(2,1)S(1)} %get-tuple-element.27.refs_1_), channel_id=1, source_target_pairs={{0,2},{1,3},{2,0},{3,1},{4,6},{5,7},{6,4},{7,5},{8,10},{9,11},{10,... | collective-permute-start | bytes 786440 | tf_op jit(solution)/shard_map/ppermute | solution.py:338
  46.3 14.2 %collective-permute-start.11 = (bf16[32,4096]{1,0:T(8,128)(2,1)S(1)}, bf16[32,4096]{1,0:T(8,128)(2,1)S(1)}, u32[]{:S(2)}, u32[]{:S(2)}) collective-permute-start(bf16[32,4096]{1,0:T(8,128)(2,1)S(1)} %get-tuple-element.28.refs_2_), channel_id=1, source_target_pairs={{0,4},{1,5},{2,6},{3,7},{4,0},{5,1},{6,2},{7,3},{8,12},{9,13},{10,... | collective-permute-start | bytes 786440 | tf_op jit(solution)/shard_map/ppermute | solution.py:338
  48.8 13.7 %collective-permute-start.12 = (bf16[32,4096]{1,0:T(8,128)(2,1)S(1)}, bf16[32,4096]{1,0:T(8,128)(2,1)S(1)}, u32[]{:S(2)}, u32[]{:S(2)}) collective-permute-start(bf16[32,4096]{1,0:T(8,128)(2,1)S(1)} %get-tuple-element.29.refs_3_), channel_id=1, source_target_pairs={{0,6},{1,7},{2,4},{3,5},{4,2},{5,3},{6,0},{7,1},{8,14},{9,15},{10,... | collective-permute-start | bytes 786440 | tf_op jit(solution)/shard_map/ppermute | solution.py:338
  63.6 2.7 %collective-permute-start.13 = (f32[80,128]{1,0:T(8,128)S(1)}, f32[80,128]{1,0:T(8,128)S(1)}, u32[]{:S(2)}, u32[]{:S(2)}) collective-permute-start(f32[80,128]{1,0:T(8,128)S(1)} %get-tuple-element.32), channel_id=1, source_target_pairs={{0,1},{1,0},{2,3},{3,2},{4,5},{5,4},{6,7},{7,6},{8,9},{9,8},{10,11... | collective-permute-start | bytes 122888 | tf_op jit(solution)/shard_map/ppermute | solution.py:338
  66.4 2.9 %collective-permute-start.14 = (f32[80,128]{1,0:T(8,128)S(1)}, f32[80,128]{1,0:T(8,128)S(1)}, u32[]{:S(2)}, u32[]{:S(2)}) collective-permute-start(f32[80,128]{1,0:T(8,128)S(1)} %add.66), channel_id=1, source_target_pairs={{0,2},{1,3},{2,0},{3,1},{4,6},{5,7},{6,4},{7,5},{8,10},{9,11},{10,... | collective-permute-start | bytes 122888 | tf_op jit(solution)/shard_map/ppermute | solution.py:338
  69.2 4.1 %collective-permute-start.15 = (f32[80,128]{1,0:T(8,128)S(1)}, f32[80,128]{1,0:T(8,128)S(1)}, u32[]{:S(2)}, u32[]{:S(2)}) collective-permute-start(f32[80,128]{1,0:T(8,128)S(1)} %add.67), channel_id=1, source_target_pairs={{0,6},{1,7},{2,4},{3,5},{4,2},{5,3},{6,0},{7,1},{8,14},{9,15},{10,... | collective-permute-start | bytes 122888 | tf_op jit(solution)/shard_map/ppermute | solution.py:338
  69.4 30.1 %collective-permute-start.22 = (bf16[128,4096]{1,0:T(8,128)(2,1)S(1)}, bf16[128,4096]{1,0:T(8,128)(2,1)S(1)}, u32[]{:S(2)}, u32[]{:S(2)}) collective-permute-start(bf16[128,4096]{1,0:T(8,128)(2,1)S(1)} %get-tuple-element.37), channel_id=1, source_target_pairs={{0,2},{1,3},{2,0},{3,1},{4,6},{5,7},{6,4},{7,5},{8,10},{9,11},{10,... | collective-permute-start | bytes 3145736 | tf_op jit(solution)/shard_map/ppermute | solution.py:338
  69.4 30.1 %collective-permute-start.23 = (bf16[128,4096]{1,0:T(8,128)(2,1)S(1)}, bf16[128,4096]{1,0:T(8,128)(2,1)S(1)}, u32[]{:S(2)}, u32[]{:S(2)}) collective-permute-start(bf16[128,4096]{1,0:T(8,128)(2,1)S(1)} %get-tuple-element.38), channel_id=1, source_target_pairs={{0,6},{1,7},{2,4},{3,5},{4,2},{5,3},{6,0},{7,1},{8,14},{9,15},{10,... | collective-permute-start | bytes 3145736 | tf_op jit(solution)/shard_map/ppermute | solution.py:338
  73.3 3.1 %collective-permute-start.16 = (f32[80,128]{1,0:T(8,128)S(1)}, f32[80,128]{1,0:T(8,128)S(1)}, u32[]{:S(2)}, u32[]{:S(2)}) collective-permute-start(f32[80,128]{1,0:T(8,128)S(1)} %add.68), channel_id=1, source_target_pairs={{0,8},{8,0},{16,24},{24,16},{32,40},{40,32},{48,56},{56,48},{64,72... | collective-permute-start | bytes 122888 | tf_op jit(solution)/shard_map/ppermute | solution.py:338
  76.5 3.1 %collective-permute-start.17 = (f32[80,128]{1,0:T(8,128)S(1)}, f32[80,128]{1,0:T(8,128)S(1)}, u32[]{:S(2)}, u32[]{:S(2)}) collective-permute-start(f32[80,128]{1,0:T(8,128)S(1)} %add.69), channel_id=1, source_target_pairs={{0,32},{8,40},{16,48},{24,56},{32,0},{40,8},{48,16},{56,24},{64,96... | collective-permute-start | bytes 122888 | tf_op jit(solution)/shard_map/ppermute | solution.py:338
  79.6 3.1 %collective-permute-start.18 = (f32[80,128]{1,0:T(8,128)S(1)}, f32[80,128]{1,0:T(8,128)S(1)}, u32[]{:S(2)}, u32[]{:S(2)}) collective-permute-start(f32[80,128]{1,0:T(8,128)S(1)} %add.70), channel_id=1, source_target_pairs={{0,24},{8,16},{16,8},{24,0},{32,56},{40,48},{48,40},{56,32},{64,88... | collective-permute-start | bytes 122888 | tf_op jit(solution)/shard_map/ppermute | solution.py:338
  82.8 4.5 %collective-permute-start.19 = (f32[80,128]{1,0:T(8,128)S(1)}, f32[80,128]{1,0:T(8,128)S(1)}, u32[]{:S(2)}, u32[]{:S(2)}) collective-permute-start(f32[80,128]{1,0:T(8,128)S(1)} %add.71), channel_id=1, source_target_pairs={{0,64},{8,72},{16,80},{24,88},{32,96},{40,104},{48,112},{56,120},{... | collective-permute-start | bytes 122888 | tf_op jit(solution)/shard_map/ppermute | solution.py:338
  87.3 5.0 %collective-permute-start.20 = (f32[80,128]{1,0:T(8,128)S(1)}, f32[80,128]{1,0:T(8,128)S(1)}, u32[]{:S(2)}, u32[]{:S(2)}) collective-permute-start(f32[80,128]{1,0:T(8,128)S(1)} %add.72), channel_id=1, source_target_pairs={{0,192},{8,200},{16,208},{24,216},{32,224},{40,232},{48,240},{56,2... | collective-permute-start | bytes 122888 | tf_op jit(solution)/shard_map/ppermute | solution.py:338
  90.7 8.9 %collective-permute-start.21 = (bf16[32,4096]{1,0:T(8,128)(2,1)S(1)}, bf16[32,4096]{1,0:T(8,128)(2,1)S(1)}, u32[]{:S(2)}, u32[]{:S(2)}) collective-permute-start(bf16[32,4096]{1,0:T(8,128)(2,1)S(1)} %get-tuple-element.36.refs_0_), channel_id=1, source_target_pairs={{0,4},{1,5},{2,6},{3,7},{4,0},{5,1},{6,2},{7,3},{8,12},{9,13},{10,... | collective-permute-start | bytes 786440 | tf_op jit(solution)/shard_map/ppermute | solution.py:338
  100.9 7.1 %collective-permute-start.24 = (f32[4,16384]{1,0:T(4,128)S(1)}, f32[4,16384]{1,0:T(4,128)S(1)}, u32[]{:S(2)}, u32[]{:S(2)}) collective-permute-start(f32[4,16384]{1,0:T(4,128)S(1)} %get-tuple-element.40), channel_id=1, source_target_pairs={{0,1},{1,0},{2,3},{3,2},{4,5},{5,4},{6,7},{7,6},{8,9},{9,8},{10,11... | collective-permute-start | bytes 786440 | tf_op jit(solution)/shard_map/ppermute | solution.py:338

commit v3 on v2

--- a/solution.py
+++ b/solution.py
@@ -408,6 +408,8 @@
     )(place, crossed, coeffs, other_coeffs, merge_mix, mine, other)
 
     got = [swap(pieces[i], "snap", 2 * i) for i in range(1, chips)]
+    far, got[0] = lax.optimization_barrier((pieces[0], got[0]))
+    far = swap(far, "snap", 4)
     gram, low_rest, high_rest = call(
         rows_gram_kernel,
         (shape((5 * modes // 2, chips * modes), F32), rest, rest),
@@ -417,8 +419,7 @@
         aliases={chips + 1: 1, chips + 2: 2},
     )(place, pieces[0], *got, low_rest, high_rest)
     gram = butterfly(gram, "snap", (1, 2))
-    gram, far, low_rest, high_rest = lax.optimization_barrier((gram, pieces[0], low_rest, high_rest))
-    far = swap(far, "snap", 4)
+    gram, far, low_rest, high_rest = lax.optimization_barrier((gram, far, low_rest, high_rest))
     low_rest = swap(low_rest, "snap", 2)
     high_rest = swap(high_rest, "snap", 6)
     gram = butterfly(gram, "snap", (6,))

time: 111 us -> 116 us (1.045)
  starting transfers between devices: 41.3 us -> 46 us
    ppermute x25, starting transfers between devices: 41.3 us -> 46 us  [swap(): return lax.ppermute(block, axis, [(i, i ^ mask) for i in range(count)])]
where the time goes in v3:
time: 116 us; the launch traced here: 114 us
  starting transfers between devices  46 us (40%)
  waiting for transfers between devices  43.7 us (38%)
  Pallas kernels  23.9 us (21%)
    ppermute x25, starting transfers between devices, swap(): return lax.ppermute(block, axis, [(i, i ^ mask) for i in range(count)])  46 us
    ppermute x25, waiting for transfers between devices, swap(): return lax.ppermute(block, axis, [(i, i ^ mask) for i in range(count)])  43.7 us
    pallas_call x1, Pallas kernels, shards(): call(merge_kernel, (piece,) * chips + (rest,) * 2, [SMEM] + [VMEM] * 5 +...  4.49 us
    pallas_call x1, Pallas kernels, shards(): call(tree_kernel, shape((modes, chips * modes), F32), [VMEM] * 2, 'tree',...  4.39 us
    pallas_call x1, Pallas kernels, shards(): call(own_gram_kernel, (shape((width, 2 * width), F32),) + (shape((width,...  3.99 us
    pallas_call x1, Pallas kernels, shards(): call(functools.partial(power_kernel, ITERS - ITERS // 2, True), shape((mo...  3.14 us
    pallas_call x1, Pallas kernels, shards(): call(functools.partial(power_kernel, ITERS // 2, False), shape((modes, wi...  2.76 us
  transfers between devices with their start and end apart: 25, of which 19 were waited for; matrix products, arithmetic and copies ran while one was open for 0% of the time, Pallas kernels for 11%

profile of v3, /device:TPU:17, one launch (start us, length us, event | category | flops | bytes accessed | tf_op | source)
XLA Modules:
  0.0 114.1 jit_solution(18446219172002433967)
XLA Ops:
  0.0 0.1 pad_add_fusion.place_ref
  0.1 4.0 %own_gram.1 = (f32[64,128]{1,0:T(8,128)S(1)}, bf16[64,16384]{1,0:T(8,128)(2,1)S(1)}, bf16[64,16384]{1,0:T(8,128)(2,1)S(1)}) custom-call(s32[2]{0:T(128)S(1)} %pad_add_fusion.place_ref, bf16[64,32768]{1,0:T(8,128)(2,1)} %snaps_ref.1), custom_call_target="tpu_custom_call" | custom-call | tf_op jit(solution)/shard_map/own_gram/pallas_call | solution.py:361
  4.1 0.8 collective-permute-start.2
  4.8 1.0 collective-permute-start
  5.9 1.8 %collective-permute-done = f32[64,128]{1,0:T(8,128)S(1)} collective-permute-done((f32[64,128]{1,0:T(8,128)S(1)}, f32[64,128]{1,0:T(8,128)S(1)}, u32[]{:S(2)}, u32[]{:S(2)}) %collective-permute-start) | collective-permute-done | bytes 32800 | tf_op jit(solution)/shard_map/ppermute | solution.py:338
  7.6 1.6 %collective-permute-start.1 = (f32[64,128]{1,0:T(8,128)S(1)}, f32[64,128]{1,0:T(8,128)S(1)}, u32[]{:S(2)}, u32[]{:S(2)}) collective-permute-start(f32[64,128]{1,0:T(8,128)S(1)} %add.57), channel_id=1, source_target_pairs={{0,32},{8,40},{16,48},{24,56},{32,0},{40,8},{48,16},{56,24},{64,96... | collective-permute-start | bytes 98312 | tf_op jit(solution)/shard_map/ppermute | solution.py:338
  9.3 0.0 collective-permute-done.2.other_ref.other_hbm
  9.3 1.3 %cross_gram.1 = f32[64,128]{1,0:T(8,128)S(1)} custom-call(s32[2]{0:T(128)S(1)} %pad_add_fusion.place_ref, bf16[64,16384]{1,0:T(8,128)(2,1)S(1)} %get-tuple-element.26.mine_ref, bf16[64,16384]{1,0:T(8,128)(2,1)S(1)} %collective-permute-done.2.other_ref.other_hbm), custom_call_target="tpu_custom_call" | custom-call | tf_op jit(solution)/shard_map/cross_gram/pallas_call | solution.py:372
  10.6 0.0 copy-done
  10.6 1.6 %collective-permute-start.3 = (f32[64,128]{1,0:T(8,128)S(1)}, f32[64,128]{1,0:T(8,128)S(1)}, u32[]{:S(2)}, u32[]{:S(2)}) collective-permute-start(f32[64,128]{1,0:T(8,128)S(1)} %cross_gram.1), channel_id=1, source_target_pairs={{0,1},{1,0},{2,3},{3,2},{4,5},{5,4},{6,7},{7,6},{8,9},{9,8},{10,11... | collective-permute-start | bytes 98312 | tf_op jit(solution)/shard_map/ppermute | solution.py:338
  12.2 0.0 collective-permute-done.1
  12.2 0.9 collective-permute-done.3
  13.0 0.3 collective-permute-start.4
  13.3 2.6 %collective-permute-done.4 = f32[64,128]{1,0:T(8,128)S(1)} collective-permute-done((f32[64,128]{1,0:T(8,128)S(1)}, f32[64,128]{1,0:T(8,128)S(1)}, u32[]{:S(2)}, u32[]{:S(2)}) %collective-permute-start.4) | collective-permute-done | bytes 32800 | tf_op jit(solution)/shard_map/ppermute | solution.py:338
  15.9 3.0 %collective-permute-start.5 = (f32[64,128]{1,0:T(8,128)S(1)}, f32[64,128]{1,0:T(8,128)S(1)}, u32[]{:S(2)}, u32[]{:S(2)}) collective-permute-start(f32[64,128]{1,0:T(8,128)S(1)} %add.61), channel_id=1, source_target_pairs={{0,64},{8,72},{16,80},{24,88},{32,96},{40,104},{48,112},{56,120},{... | collective-permute-start | bytes 98312 | tf_op jit(solution)/shard_map/ppermute | solution.py:338
  18.9 1.3 %collective-permute-done.5 = f32[64,128]{1,0:T(8,128)S(1)} collective-permute-done((f32[64,128]{1,0:T(8,128)S(1)}, f32[64,128]{1,0:T(8,128)S(1)}, u32[]{:S(2)}, u32[]{:S(2)}) %collective-permute-start.5) | collective-permute-done | bytes 32800 | tf_op jit(solution)/shard_map/ppermute | solution.py:338
  20.2 4.5 %collective-permute-start.6 = (f32[64,128]{1,0:T(8,128)S(1)}, f32[64,128]{1,0:T(8,128)S(1)}, u32[]{:S(2)}, u32[]{:S(2)}) collective-permute-start(f32[64,128]{1,0:T(8,128)S(1)} %add.62), channel_id=1, source_target_pairs={{0,192},{8,200},{16,208},{24,216},{32,224},{40,232},{48,240},{56,2... | collective-permute-start | bytes 98312 | tf_op jit(solution)/shard_map/ppermute | solution.py:338
  24.7 1.7 %collective-permute-done.6 = f32[64,128]{1,0:T(8,128)S(1)} collective-permute-done((f32[64,128]{1,0:T(8,128)S(1)}, f32[64,128]{1,0:T(8,128)S(1)}, u32[]{:S(2)}, u32[]{:S(2)}) %collective-permute-start.6) | collective-permute-done | bytes 32800 | tf_op jit(solution)/shard_map/ppermute | solution.py:338
  26.4 2.2 %collective-permute-start.7 = (f32[64,128]{1,0:T(8,128)S(1)}, f32[64,128]{1,0:T(8,128)S(1)}, u32[]{:S(2)}, u32[]{:S(2)}) collective-permute-start(f32[64,128]{1,0:T(8,128)S(1)} %add.63.gram_ref), channel_id=1, source_target_pairs={{0,8},{8,0},{16,24},{24,16},{32,40},{40,32},{48,56},{56,48},{64,72... | collective-permute-start | bytes 98312 | tf_op jit(solution)/shard_map/ppermute | solution.py:338
  28.6 0.0 copy-done.1
  28.6 2.8 %power_first.1.coeffs_ref = f32[32,64]{1,0:T(8,128)S(1)} custom-call(f32[64,128]{1,0:T(8,128)S(1)} %add.63.gram_ref, bf16[32,64]{1,0:T(8,128)(2,1)S(1)} %copy-done.1), custom_call_target="tpu_custom_call" | custom-call | flops 4000000000 | tf_op jit(solution)/shard_map/power_first/pallas_call | solution.py:383
  31.3 0.0 collective-permute-done.7
  31.4 0.0 copy-start.2
  31.4 0.5 collective-permute-start.8
  31.8 3.1 %power_last.1.mine_co_ref = f32[32,128]{1,0:T(8,128)S(1)} custom-call(f32[64,128]{1,0:T(8,128)S(1)} %add.63.gram_ref, f32[32,64]{1,0:T(8,128)S(1)} %power_first.1.coeffs_ref), custom_call_target="tpu_custom_call" | custom-call | flops 4000000000 | tf_op jit(solution)/shard_map/power_last/pallas_call | solution.py:390
  35.0 4.5 %collective-permute-start.9 = (f32[32,128]{1,0:T(8,128)S(1)}, f32[32,128]{1,0:T(8,128)S(1)}, u32[]{:S(2)}, u32[]{:S(2)}) collective-permute-start(f32[32,128]{1,0:T(8,128)S(1)} %power_last.1.mine_co_ref), channel_id=1, source_target_pairs={{0,1},{1,0},{2,3},{3,2},{4,5},{5,4},{6,7},{7,6},{8,9},{9,8},{10,11... | collective-permute-start | bytes 49160 | tf_op jit(solution)/shard_map/ppermute | solution.py:338
  39.5 0.1 copy.6.mix_ref
  39.6 0.0 collective-permute-done.8
  39.6 0.7 collective-permute-done.9.other_co_ref
  40.3 4.5 %merge.1 = (bf16[32,4096]{1,0:T(8,128)(2,1)S(1)}, bf16[32,4096]{1,0:T(8,128)(2,1)S(1)}, bf16[32,4096]{1,0:T(8,128)(2,1)S(1)}, bf16[32,4096]{1,0:T(8,128)(2,1)S(1...) custom-call(s32[2]{0:T(128)S(1)} %pad_add_fusion.place_ref, f32[64,128]{1,0:T(8,128)S(1)} %add.65.cross_ref, ...), custom_call_target="tpu_custom_call" | custom-call | tf_op jit(solution)/shard_map/merge/pallas_call | solution.py:401
  44.8 1.5 %collective-permute-start.10 = (bf16[32,4096]{1,0:T(8,128)(2,1)S(1)}, bf16[32,4096]{1,0:T(8,128)(2,1)S(1)}, u32[]{:S(2)}, u32[]{:S(2)}) collective-permute-start(bf16[32,4096]{1,0:T(8,128)(2,1)S(1)} %get-tuple-element.29.refs_1_), channel_id=1, source_target_pairs={{0,2},{1,3},{2,0},{3,1},{4,6},{5,7},{6,4},{7,5},{8,10},{9,11},{10,... | collective-permute-start | bytes 786440 | tf_op jit(solution)/shard_map/ppermute | solution.py:338
  46.3 2.5 %collective-permute-start.11 = (bf16[32,4096]{1,0:T(8,128)(2,1)S(1)}, bf16[32,4096]{1,0:T(8,128)(2,1)S(1)}, u32[]{:S(2)}, u32[]{:S(2)}) collective-permute-start(bf16[32,4096]{1,0:T(8,128)(2,1)S(1)} %get-tuple-element.31.refs_2_), channel_id=1, source_target_pairs={{0,4},{1,5},{2,6},{3,7},{4,0},{5,1},{6,2},{7,3},{8,12},{9,13},{10,... | collective-permute-start | bytes 786440 | tf_op jit(solution)/shard_map/ppermute | solution.py:338
  48.8 0.2 collective-permute-start.12
  49.0 3.7 %collective-permute-done.10.refs_1_.refs_4_ = bf16[32,4096]{1,0:T(8,128)(2,1)S(1)} collective-permute-done((bf16[32,4096]{1,0:T(8,128)(2,1)S(1)}, bf16[32,4096]{1,0:T(8,128)(2,1)S(1)}, u32[]{:S(2)}, u32[]{:S(2)}) %collective-permute-start.10) | collective-permute-done | bytes 262176 | tf_op jit(solution)/shard_map/ppermute | solution.py:338
  52.6 2.7 %collective-permute-start.15 = (bf16[32,4096]{1,0:T(8,128)(2,1)S(1)}, bf16[32,4096]{1,0:T(8,128)(2,1)S(1)}, u32[]{:S(2)}, u32[]{:S(2)}) collective-permute-start(bf16[32,4096]{1,0:T(8,128)(2,1)S(1)} %get-tuple-element.36.refs_0_), channel_id=1, source_target_pairs={{0,4},{1,5},{2,6},{3,7},{4,0},{5,1},{6,2},{7,3},{8,12},{9,13},{10,... | collective-permute-start | bytes 786440 | tf_op jit(solution)/shard_map/ppermute | solution.py:338
  55.4 5.1 %collective-permute-done.11.refs_2_.refs_5_ = bf16[32,4096]{1,0:T(8,128)(2,1)S(1)} collective-permute-done((bf16[32,4096]{1,0:T(8,128)(2,1)S(1)}, bf16[32,4096]{1,0:T(8,128)(2,1)S(1)}, u32[]{:S(2)}, u32[]{:S(2)}) %collective-permute-start.11) | collective-permute-done | bytes 262176 | tf_op jit(solution)/shard_map/ppermute | solution.py:338
  60.5 7.6 %collective-permute-done.12.refs_3_.refs_6_ = bf16[32,4096]{1,0:T(8,128)(2,1)S(1)} collective-permute-done((bf16[32,4096]{1,0:T(8,128)(2,1)S(1)}, bf16[32,4096]{1,0:T(8,128)(2,1)S(1)}, u32[]{:S(2)}, u32[]{:S(2)}) %collective-permute-start.12) | collective-permute-done | bytes 262176 | tf_op jit(solution)/shard_map/ppermute | solution.py:338
  68.1 1.1 %rows_gram.1 = (f32[80,128]{1,0:T(8,128)S(1)}, bf16[128,4096]{1,0:T(8,128)(2,1)S(1)}, bf16[128,4096]{1,0:T(8,128)(2,1)S(1)}) custom-call(s32[2]{0:T(128)S(1)} %pad_add_fusion.place_ref, bf16[32,4096]{1,0:T(8,128)(2,1)S(1)} %get-tuple-element.36.refs_0_, ...), custom_call_target="tpu_custom_call", output_to_operand_aliasing={{1}: (5, {}), {2}: (6, {})} | custom-call | tf_op jit(solution)/shard_map/rows_gram/pallas_call | solution.py:413
  69.3 1.9 %collective-permute-start.13 = (f32[80,128]{1,0:T(8,128)S(1)}, f32[80,128]{1,0:T(8,128)S(1)}, u32[]{:S(2)}, u32[]{:S(2)}) collective-permute-start(f32[80,128]{1,0:T(8,128)S(1)} %get-tuple-element.35), channel_id=1, source_target_pairs={{0,1},{1,0},{2,3},{3,2},{4,5},{5,4},{6,7},{7,6},{8,9},{9,8},{10,11... | collective-permute-start | bytes 122888 | tf_op jit(solution)/shard_map/ppermute | solution.py:338
  71.1 0.9 collective-permute-done.13
  72.0 0.0 collective-permute-start.14
  72.0 2.8 %collective-permute-done.14 = f32[80,128]{1,0:T(8,128)S(1)} collective-permute-done((f32[80,128]{1,0:T(8,128)S(1)}, f32[80,128]{1,0:T(8,128)S(1)}, u32[]{:S(2)}, u32[]{:S(2)}) %collective-permute-start.14) | collective-permute-done | bytes 40992 | tf_op jit(solution)/shard_map/ppermute | solution.py:338
  74.9 0.0 collective-permute-done.15.refs_7_
  74.9 0.3 collective-permute-start.16
  75.1 0.0 collective-permute-start.22
  75.1 2.5 %collective-permute-start.23 = (bf16[128,4096]{1,0:T(8,128)(2,1)S(1)}, bf16[128,4096]{1,0:T(8,128)(2,1)S(1)}, u32[]{:S(2)}, u32[]{:S(2)}) collective-permute-start(bf16[128,4096]{1,0:T(8,128)(2,1)S(1)} %get-tuple-element.42), channel_id=1, source_target_pairs={{0,6},{1,7},{2,4},{3,5},{4,2},{5,3},{6,0},{7,1},{8,14},{9,15},{10,... | collective-permute-start | bytes 3145736 | tf_op jit(solution)/shard_map/ppermute | solution.py:338
  77.6 1.4 %collective-permute-done.16 = f32[80,128]{1,0:T(8,128)S(1)} collective-permute-done((f32[80,128]{1,0:T(8,128)S(1)}, f32[80,128]{1,0:T(8,128)S(1)}, u32[]{:S(2)}, u32[]{:S(2)}) %collective-permute-start.16) | collective-permute-done | bytes 40992 | tf_op jit(solution)/shard_map/ppermute | solution.py:338
  79.0 0.8 collective-permute-start.17
  79.9 2.3 %collective-permute-done.17 = f32[80,128]{1,0:T(8,128)S(1)} collective-permute-done((f32[80,128]{1,0:T(8,128)S(1)}, f32[80,128]{1,0:T(8,128)S(1)}, u32[]{:S(2)}, u32[]{:S(2)}) %collective-permute-start.17) | collective-permute-done | bytes 40992 | tf_op jit(solution)/shard_map/ppermute | solution.py:338
  82.2 0.6 collective-permute-start.18
  82.8 2.5 %collective-permute-done.18 = f32[80,128]{1,0:T(8,128)S(1)} collective-permute-done((f32[80,128]{1,0:T(8,128)S(1)}, f32[80,128]{1,0:T(8,128)S(1)}, u32[]{:S(2)}, u32[]{:S(2)}) %collective-permute-start.18) | collective-permute-done | bytes 40992 | tf_op jit(solution)/shard_map/ppermute | solution.py:338
  85.3 0.0 collective-permute-start.19
  85.3 3.1 %collective-permute-done.19 = f32[80,128]{1,0:T(8,128)S(1)} collective-permute-done((f32[80,128]{1,0:T(8,128)S(1)}, f32[80,128]{1,0:T(8,128)S(1)}, u32[]{:S(2)}, u32[]{:S(2)}) %collective-permute-start.19) | collective-permute-done | bytes 40992 | tf_op jit(solution)/shard_map/ppermute | solution.py:338
  88.5 2.0 %collective-permute-start.20 = (f32[80,128]{1,0:T(8,128)S(1)}, f32[80,128]{1,0:T(8,128)S(1)}, u32[]{:S(2)}, u32[]{:S(2)}) collective-permute-start(f32[80,128]{1,0:T(8,128)S(1)} %add.71), channel_id=1, source_target_pairs={{0,64},{8,72},{16,80},{24,88},{32,96},{40,104},{48,112},{56,120},{... | collective-permute-start | bytes 122888 | tf_op jit(solution)/shard_map/ppermute | solution.py:338
  90.4 2.5 %collective-permute-done.20 = f32[80,128]{1,0:T(8,128)S(1)} collective-permute-done((f32[80,128]{1,0:T(8,128)S(1)}, f32[80,128]{1,0:T(8,128)S(1)}, u32[]{:S(2)}, u32[]{:S(2)}) %collective-permute-start.20) | collective-permute-done | bytes 40992 | tf_op jit(solution)/shard_map/ppermute | solution.py:338
  93.0 3.4 %collective-permute-start.21 = (f32[80,128]{1,0:T(8,128)S(1)}, f32[80,128]{1,0:T(8,128)S(1)}, u32[]{:S(2)}, u32[]{:S(2)}) collective-permute-start(f32[80,128]{1,0:T(8,128)S(1)} %add.72), channel_id=1, source_target_pairs={{0,192},{8,200},{16,208},{24,216},{32,224},{40,232},{48,240},{56,2... | collective-permute-start | bytes 122888 | tf_op jit(solution)/shard_map/ppermute | solution.py:338
  96.4 1.6 %collective-permute-done.21 = f32[80,128]{1,0:T(8,128)S(1)} collective-permute-done((f32[80,128]{1,0:T(8,128)S(1)}, f32[80,128]{1,0:T(8,128)S(1)}, u32[]{:S(2)}, u32[]{:S(2)}) %collective-permute-start.21) | collective-permute-done | bytes 40992 | tf_op jit(solution)/shard_map/ppermute | solution.py:338
  97.9 4.4 %tree.1.whole_ref = f32[32,128]{1,0:T(8,128)S(1)} custom-call(f32[80,128]{1,0:T(8,128)S(1)} %add.73.gram_ref, f32[64,32]{1,0:T(8,128)S(1)} %copy.6.mix_ref), custom_call_target="tpu_custom_call" | custom-call | flops 8800000000 | tf_op jit(solution)/shard_map/tree/pallas_call | solution.py:428
  102.3 0.0 collective-permute-done.22.refs_8_
  102.3 0.1 collective-permute-done.23.refs_9_
  102.4 1.3 %finish.1 = (f32[4,16384]{1,0:T(4,128)S(1)}, f32[4,16384]{1,0:T(4,128)S(1)}) custom-call(s32[2]{0:T(128)S(1)} %pad_add_fusion.place_ref, f32[32,128]{1,0:T(8,128)S(1)} %tree.1.whole_ref, bf16[32,4096]{1,0:T(8,128)(2,1)S(1)} %get-tuple-element.36.refs_0_, bf16[32,4096]{1,0:T(8,128)(2,1)S(1)} %get-tuple-element.29.refs_1_, ...), custom_call_target="tpu_custom_call" | custom-call | tf_op jit(solution)/shard_map/finish/pallas_call | solution.py:432
  103.7 7.8 %collective-permute-start.24 = (f32[4,16384]{1,0:T(4,128)S(1)}, f32[4,16384]{1,0:T(4,128)S(1)}, u32[]{:S(2)}, u32[]{:S(2)}) collective-permute-start(f32[4,16384]{1,0:T(4,128)S(1)} %get-tuple-element.44), channel_id=1, source_target_pairs={{0,1},{1,0},{2,3},{3,2},{4,5},{5,4},{6,7},{7,6},{8,9},{9,8},{10,11... | collective-permute-start | bytes 786440 | tf_op jit(solution)/shard_map/ppermute | solution.py:338
  111.5 1.2 %collective-permute-done.24.got_ref = f32[4,16384]{1,0:T(4,128)S(1)} collective-permute-done((f32[4,16384]{1,0:T(4,128)S(1)}, f32[4,16384]{1,0:T(4,128)S(1)}, u32[]{:S(2)}, u32[]{:S(2)}) %collective-permute-start.24) | collective-permute-done | bytes 262176 | tf_op jit(solution)/shard_map/ppermute | solution.py:338
  112.7 1.4 %assemble.1 = f32[4,32768]{1,0:T(4,128)} custom-call(s32[2]{0:T(128)S(1)} %pad_add_fusion.place_ref, f32[4,16384]{1,0:T(4,128)S(1)} %get-tuple-element.43.keep_ref, f32[4,16384]{1,0:T(4,128)S(1)} %collective-permute-done.24.got_ref), custom_call_target="tpu_custom_call" | custom-call | tf_op jit(solution)/shard_map/assemble/pallas_call | solution.py:438
  (18 shorter events, 0.1 us)
Async XLA Ops:
  4.1 5.2 %collective-permute-start.2 = (bf16[64,16384]{1,0:T(8,128)(2,1)S(1)}, bf16[64,16384]{1,0:T(8,128)(2,1)S(1)}, u32[]{:S(2)}, u32[]{:S(2)}) collective-permute-start(bf16[64,16384]{1,0:T(8,128)(2,1)S(1)} %get-tuple-element.27), channel_id=1, source_target_pairs={{0,1},{1,0},{2,3},{3,2},{4,5},{5,4},{6,7},{7,6},{8,9},{9,8},{10,11... | collective-permute-start | bytes 6291464 | tf_op jit(solution)/shard_map/ppermute | solution.py:338
  4.8 2.8 %collective-permute-start = (f32[64,128]{1,0:T(8,128)S(1)}, f32[64,128]{1,0:T(8,128)S(1)}, u32[]{:S(2)}, u32[]{:S(2)}) collective-permute-start(f32[64,128]{1,0:T(8,128)S(1)} %get-tuple-element.25), channel_id=1, source_target_pairs={{0,8},{8,0},{16,24},{24,16},{32,40},{40,32},{48,56},{56,48},{64,72... | collective-permute-start | bytes 98312 | tf_op jit(solution)/shard_map/ppermute | solution.py:338
  7.6 4.6 %collective-permute-start.1 = (f32[64,128]{1,0:T(8,128)S(1)}, f32[64,128]{1,0:T(8,128)S(1)}, u32[]{:S(2)}, u32[]{:S(2)}) collective-permute-start(f32[64,128]{1,0:T(8,128)S(1)} %add.57), channel_id=1, source_target_pairs={{0,32},{8,40},{16,48},{24,56},{32,0},{40,8},{48,16},{56,24},{64,96... | collective-permute-start | bytes 98312 | tf_op jit(solution)/shard_map/ppermute | solution.py:338
  9.3 1.3 %copy-start = (bf16[64,16384]{1,0:T(8,128)(2,1)}, bf16[64,16384]{1,0:T(8,128)(2,1)S(1)}, u32[]{:S(2)}) copy-start(bf16[64,16384]{1,0:T(8,128)(2,1)S(1)} %collective-permute-done.2.other_ref.other_hbm) | copy-start | bytes 6291460
  9.3 19.3 %copy-start.1 = (bf16[32,64]{1,0:T(8,128)(2,1)S(1)}, bf16[32,64]{1,0:T(8,128)(2,1)}, u32[]{:S(2)}) copy-start(bf16[32,64]{1,0:T(8,128)(2,1)} %coeffs_ref.1) | copy-start | bytes 12292
  10.6 2.4 %collective-permute-start.3 = (f32[64,128]{1,0:T(8,128)S(1)}, f32[64,128]{1,0:T(8,128)S(1)}, u32[]{:S(2)}, u32[]{:S(2)}) collective-permute-start(f32[64,128]{1,0:T(8,128)S(1)} %cross_gram.1), channel_id=1, source_target_pairs={{0,1},{1,0},{2,3},{3,2},{4,5},{5,4},{6,7},{7,6},{8,9},{9,8},{10,11... | collective-permute-start | bytes 98312 | tf_op jit(solution)/shard_map/ppermute | solution.py:338
  13.0 2.9 %collective-permute-start.4 = (f32[64,128]{1,0:T(8,128)S(1)}, f32[64,128]{1,0:T(8,128)S(1)}, u32[]{:S(2)}, u32[]{:S(2)}) collective-permute-start(f32[64,128]{1,0:T(8,128)S(1)} %add_add_fusion), channel_id=1, source_target_pairs={{0,24},{8,16},{16,8},{24,0},{32,56},{40,48},{48,40},{56,32},{64,88... | collective-permute-start | bytes 98312 | tf_op jit(solution)/shard_map/ppermute | solution.py:338
  15.9 4.3 %collective-permute-start.5 = (f32[64,128]{1,0:T(8,128)S(1)}, f32[64,128]{1,0:T(8,128)S(1)}, u32[]{:S(2)}, u32[]{:S(2)}) collective-permute-start(f32[64,128]{1,0:T(8,128)S(1)} %add.61), channel_id=1, source_target_pairs={{0,64},{8,72},{16,80},{24,88},{32,96},{40,104},{48,112},{56,120},{... | collective-permute-start | bytes 98312 | tf_op jit(solution)/shard_map/ppermute | solution.py:338
  20.2 6.1 %collective-permute-start.6 = (f32[64,128]{1,0:T(8,128)S(1)}, f32[64,128]{1,0:T(8,128)S(1)}, u32[]{:S(2)}, u32[]{:S(2)}) collective-permute-start(f32[64,128]{1,0:T(8,128)S(1)} %add.62), channel_id=1, source_target_pairs={{0,192},{8,200},{16,208},{24,216},{32,224},{40,232},{48,240},{56,2... | collective-permute-start | bytes 98312 | tf_op jit(solution)/shard_map/ppermute | solution.py:338
  26.4 5.0 %collective-permute-start.7 = (f32[64,128]{1,0:T(8,128)S(1)}, f32[64,128]{1,0:T(8,128)S(1)}, u32[]{:S(2)}, u32[]{:S(2)}) collective-permute-start(f32[64,128]{1,0:T(8,128)S(1)} %add.63.gram_ref), channel_id=1, source_target_pairs={{0,8},{8,0},{16,24},{24,16},{32,40},{40,32},{48,56},{56,48},{64,72... | collective-permute-start | bytes 98312 | tf_op jit(solution)/shard_map/ppermute | solution.py:338
  31.4 8.1 %copy-start.2 = (f32[64,32]{0,1:T(8,128)S(1)}, f32[64,32]{0,1:T(8,128)}, u32[]{:S(2)}) copy-start(f32[64,32]{0,1:T(8,128)} %param.5) | copy-start | bytes 24580
  31.4 8.2 %collective-permute-start.8 = (f32[64,128]{1,0:T(8,128)S(1)}, f32[64,128]{1,0:T(8,128)S(1)}, u32[]{:S(2)}, u32[]{:S(2)}) collective-permute-start(f32[64,128]{1,0:T(8,128)S(1)} %add.64), channel_id=1, source_target_pairs={{0,32},{8,40},{16,48},{24,56},{32,0},{40,8},{48,16},{56,24},{64,96... | collective-permute-start | bytes 98312 | tf_op jit(solution)/shard_map/ppermute | solution.py:338
  35.0 5.4 %collective-permute-start.9 = (f32[32,128]{1,0:T(8,128)S(1)}, f32[32,128]{1,0:T(8,128)S(1)}, u32[]{:S(2)}, u32[]{:S(2)}) collective-permute-start(f32[32,128]{1,0:T(8,128)S(1)} %power_last.1.mine_co_ref), channel_id=1, source_target_pairs={{0,1},{1,0},{2,3},{3,2},{4,5},{5,4},{6,7},{7,6},{8,9},{9,8},{10,11... | collective-permute-start | bytes 49160 | tf_op jit(solution)/shard_map/ppermute | solution.py:338
  44.8 7.8 %collective-permute-start.10 = (bf16[32,4096]{1,0:T(8,128)(2,1)S(1)}, bf16[32,4096]{1,0:T(8,128)(2,1)S(1)}, u32[]{:S(2)}, u32[]{:S(2)}) collective-permute-start(bf16[32,4096]{1,0:T(8,128)(2,1)S(1)} %get-tuple-element.29.refs_1_), channel_id=1, source_target_pairs={{0,2},{1,3},{2,0},{3,1},{4,6},{5,7},{6,4},{7,5},{8,10},{9,11},{10,... | collective-permute-start | bytes 786440 | tf_op jit(solution)/shard_map/ppermute | solution.py:338
  46.3 14.2 %collective-permute-start.11 = (bf16[32,4096]{1,0:T(8,128)(2,1)S(1)}, bf16[32,4096]{1,0:T(8,128)(2,1)S(1)}, u32[]{:S(2)}, u32[]{:S(2)}) collective-permute-start(bf16[32,4096]{1,0:T(8,128)(2,1)S(1)} %get-tuple-element.31.refs_2_), channel_id=1, source_target_pairs={{0,4},{1,5},{2,6},{3,7},{4,0},{5,1},{6,2},{7,3},{8,12},{9,13},{10,... | collective-permute-start | bytes 786440 | tf_op jit(solution)/shard_map/ppermute | solution.py:338
  48.8 19.4 %collective-permute-start.12 = (bf16[32,4096]{1,0:T(8,128)(2,1)S(1)}, bf16[32,4096]{1,0:T(8,128)(2,1)S(1)}, u32[]{:S(2)}, u32[]{:S(2)}) collective-permute-start(bf16[32,4096]{1,0:T(8,128)(2,1)S(1)} %get-tuple-element.32.refs_3_), channel_id=1, source_target_pairs={{0,6},{1,7},{2,4},{3,5},{4,2},{5,3},{6,0},{7,1},{8,14},{9,15},{10,... | collective-permute-start | bytes 786440 | tf_op jit(solution)/shard_map/ppermute | solution.py:338
  52.6 22.2 %collective-permute-start.15 = (bf16[32,4096]{1,0:T(8,128)(2,1)S(1)}, bf16[32,4096]{1,0:T(8,128)(2,1)S(1)}, u32[]{:S(2)}, u32[]{:S(2)}) collective-permute-start(bf16[32,4096]{1,0:T(8,128)(2,1)S(1)} %get-tuple-element.36.refs_0_), channel_id=1, source_target_pairs={{0,4},{1,5},{2,6},{3,7},{4,0},{5,1},{6,2},{7,3},{8,12},{9,13},{10,... | collective-permute-start | bytes 786440 | tf_op jit(solution)/shard_map/ppermute | solution.py:338
  69.3 2.7 %collective-permute-start.13 = (f32[80,128]{1,0:T(8,128)S(1)}, f32[80,128]{1,0:T(8,128)S(1)}, u32[]{:S(2)}, u32[]{:S(2)}) collective-permute-start(f32[80,128]{1,0:T(8,128)S(1)} %get-tuple-element.35), channel_id=1, source_target_pairs={{0,1},{1,0},{2,3},{3,2},{4,5},{5,4},{6,7},{7,6},{8,9},{9,8},{10,11... | collective-permute-start | bytes 122888 | tf_op jit(solution)/shard_map/ppermute | solution.py:338
  72.0 2.9 %collective-permute-start.14 = (f32[80,128]{1,0:T(8,128)S(1)}, f32[80,128]{1,0:T(8,128)S(1)}, u32[]{:S(2)}, u32[]{:S(2)}) collective-permute-start(f32[80,128]{1,0:T(8,128)S(1)} %add.66), channel_id=1, source_target_pairs={{0,2},{1,3},{2,0},{3,1},{4,6},{5,7},{6,4},{7,5},{8,10},{9,11},{10,... | collective-permute-start | bytes 122888 | tf_op jit(solution)/shard_map/ppermute | solution.py:338
  74.9 4.2 %collective-permute-start.16 = (f32[80,128]{1,0:T(8,128)S(1)}, f32[80,128]{1,0:T(8,128)S(1)}, u32[]{:S(2)}, u32[]{:S(2)}) collective-permute-start(f32[80,128]{1,0:T(8,128)S(1)} %add.67), channel_id=1, source_target_pairs={{0,6},{1,7},{2,4},{3,5},{4,2},{5,3},{6,0},{7,1},{8,14},{9,15},{10,... | collective-permute-start | bytes 122888 | tf_op jit(solution)/shard_map/ppermute | solution.py:338
  75.1 27.2 %collective-permute-start.22 = (bf16[128,4096]{1,0:T(8,128)(2,1)S(1)}, bf16[128,4096]{1,0:T(8,128)(2,1)S(1)}, u32[]{:S(2)}, u32[]{:S(2)}) collective-permute-start(bf16[128,4096]{1,0:T(8,128)(2,1)S(1)} %get-tuple-element.41), channel_id=1, source_target_pairs={{0,2},{1,3},{2,0},{3,1},{4,6},{5,7},{6,4},{7,5},{8,10},{9,11},{10,... | collective-permute-start | bytes 3145736 | tf_op jit(solution)/shard_map/ppermute | solution.py:338
  75.1 27.2 %collective-permute-start.23 = (bf16[128,4096]{1,0:T(8,128)(2,1)S(1)}, bf16[128,4096]{1,0:T(8,128)(2,1)S(1)}, u32[]{:S(2)}, u32[]{:S(2)}) collective-permute-start(bf16[128,4096]{1,0:T(8,128)(2,1)S(1)} %get-tuple-element.42), channel_id=1, source_target_pairs={{0,6},{1,7},{2,4},{3,5},{4,2},{5,3},{6,0},{7,1},{8,14},{9,15},{10,... | collective-permute-start | bytes 3145736 | tf_op jit(solution)/shard_map/ppermute | solution.py:338
  79.0 3.1 %collective-permute-start.17 = (f32[80,128]{1,0:T(8,128)S(1)}, f32[80,128]{1,0:T(8,128)S(1)}, u32[]{:S(2)}, u32[]{:S(2)}) collective-permute-start(f32[80,128]{1,0:T(8,128)S(1)} %add.68), channel_id=1, source_target_pairs={{0,8},{8,0},{16,24},{24,16},{32,40},{40,32},{48,56},{56,48},{64,72... | collective-permute-start | bytes 122888 | tf_op jit(solution)/shard_map/ppermute | solution.py:338
  82.2 3.1 %collective-permute-start.18 = (f32[80,128]{1,0:T(8,128)S(1)}, f32[80,128]{1,0:T(8,128)S(1)}, u32[]{:S(2)}, u32[]{:S(2)}) collective-permute-start(f32[80,128]{1,0:T(8,128)S(1)} %add.69), channel_id=1, source_target_pairs={{0,32},{8,40},{16,48},{24,56},{32,0},{40,8},{48,16},{56,24},{64,96... | collective-permute-start | bytes 122888 | tf_op jit(solution)/shard_map/ppermute | solution.py:338
  85.3 3.1 %collective-permute-start.19 = (f32[80,128]{1,0:T(8,128)S(1)}, f32[80,128]{1,0:T(8,128)S(1)}, u32[]{:S(2)}, u32[]{:S(2)}) collective-permute-start(f32[80,128]{1,0:T(8,128)S(1)} %add.70), channel_id=1, source_target_pairs={{0,24},{8,16},{16,8},{24,0},{32,56},{40,48},{48,40},{56,32},{64,88... | collective-permute-start | bytes 122888 | tf_op jit(solution)/shard_map/ppermute | solution.py:338
  88.5 4.5 %collective-permute-start.20 = (f32[80,128]{1,0:T(8,128)S(1)}, f32[80,128]{1,0:T(8,128)S(1)}, u32[]{:S(2)}, u32[]{:S(2)}) collective-permute-start(f32[80,128]{1,0:T(8,128)S(1)} %add.71), channel_id=1, source_target_pairs={{0,64},{8,72},{16,80},{24,88},{32,96},{40,104},{48,112},{56,120},{... | collective-permute-start | bytes 122888 | tf_op jit(solution)/shard_map/ppermute | solution.py:338
  93.0 5.0 %collective-permute-start.21 = (f32[80,128]{1,0:T(8,128)S(1)}, f32[80,128]{1,0:T(8,128)S(1)}, u32[]{:S(2)}, u32[]{:S(2)}) collective-permute-start(f32[80,128]{1,0:T(8,128)S(1)} %add.72), channel_id=1, source_target_pairs={{0,192},{8,200},{16,208},{24,216},{32,224},{40,232},{48,240},{56,2... | collective-permute-start | bytes 122888 | tf_op jit(solution)/shard_map/ppermute | solution.py:338
  103.7 9.0 %collective-permute-start.24 = (f32[4,16384]{1,0:T(4,128)S(1)}, f32[4,16384]{1,0:T(4,128)S(1)}, u32[]{:S(2)}, u32[]{:S(2)}) collective-permute-start(f32[4,16384]{1,0:T(4,128)S(1)} %get-tuple-element.44), channel_id=1, source_target_pairs={{0,1},{1,0},{2,3},{3,2},{4,5},{5,4},{6,7},{7,6},{8,9},{9,8},{10,11... | collective-permute-start | bytes 786440 | tf_op jit(solution)/shard_map/ppermute | solution.py:338

commit v4 on v2

--- a/solution.py
+++ b/solution.py
@@ -181,12 +181,12 @@
 
 def merge_kernel(place_ref, cross_ref, mine_co_ref, other_co_ref, mix_ref, mine_ref, other_hbm, *refs):
     out_refs, (other_ref, sem) = refs[:-2], refs[-2:]
-    parts = sem.shape[0]
-    part = other_ref.shape[0] // parts
-    fetches = [
-        pltpu.make_async_copy(other_hbm.at[pl.ds(i * part, part)], other_ref.at[pl.ds(i * part, part)], sem.at[i])
-        for i in range(parts)
-    ]
+    chunk = out_refs[0].shape[1]
+    fetches = []
+    for i in range(sem.shape[0]):
+        there = pl.ds(pl.multiple_of((place_ref[1] ^ i) * chunk, chunk), chunk)
+        slot = other_ref.at[:, pl.ds(i * chunk, chunk)]
+        fetches.append(pltpu.make_async_copy(other_hbm.at[:, there], slot, sem.at[i]))
     for fetch in fetches:
         fetch.start()
     first = place_ref[0] == 0
@@ -209,13 +209,13 @@
     mine_split = split_two(jnp.where(first, low_mix, high_mix))
     other_split = split_two(jnp.where(first, high_mix, low_mix))
     piece_refs, rest_refs = out_refs[:-2], out_refs[-2:]
-    chunk = piece_refs[0].shape[1]
     split = jnp.concatenate([mine_split, other_split], axis=1)
-    for fetch in fetches:
-        fetch.wait()
     for i, piece_ref in enumerate(piece_refs):
+        if i % 2 == 0:
+            fetches[i].wait()
+            fetches[i + 1].wait()
         here = pl.ds(pl.multiple_of((place_ref[1] ^ i) * chunk, chunk), chunk)
-        rows = jnp.concatenate([mine_ref[:, here], other_ref[:, here]], axis=0)
+        rows = jnp.concatenate([mine_ref[:, here], other_ref[:, i * chunk : (i + 1) * chunk]], axis=0)
         piece = joined(bf16_dot(split, rows)).astype(BF16)
         piece_ref[...] = piece
         for rest_ref, slots in zip(rest_refs, REST_SLOTS):

time: 111 us -> 111 us (level)
  no operation moved by 1% of the time
where the time goes in v4:
time: 111 us; the launch traced here: 109 us
  waiting for transfers between devices  43.7 us (39%)
  starting transfers between devices  41.3 us (37%)
  Pallas kernels  24 us (22%)
    ppermute x25, waiting for transfers between devices, swap(): return lax.ppermute(block, axis, [(i, i ^ mask) for i in range(count)])  43.7 us
    ppermute x25, starting transfers between devices, swap(): return lax.ppermute(block, axis, [(i, i ^ mask) for i in range(count)])  41.3 us
    pallas_call x1, Pallas kernels, shards(): call(merge_kernel, (piece,) * chips + (rest,) * 2, [SMEM] + [VMEM] * 5 +...  4.58 us
    pallas_call x1, Pallas kernels, shards(): call(tree_kernel, shape((modes, chips * modes), F32), [VMEM] * 2, 'tree',...  4.39 us
    pallas_call x1, Pallas kernels, shards(): call(own_gram_kernel, (shape((width, 2 * width), F32),) + (shape((width,...  3.99 us
    pallas_call x1, Pallas kernels, shards(): call(functools.partial(power_kernel, ITERS - ITERS // 2, True), shape((mo...  3.14 us
    pallas_call x1, Pallas kernels, shards(): call(functools.partial(power_kernel, ITERS // 2, False), shape((modes, wi...  2.76 us
  transfers between devices with their start and end apart: 25, of which 19 were waited for; matrix products, arithmetic and copies ran while one was open for 0% of the time, Pallas kernels for 11%

profile of v4, /device:TPU:17, one launch (start us, length us, event | category | flops | bytes accessed | tf_op | source)
XLA Modules:
  0.0 109.4 jit_solution(10093170186264531941)
XLA Ops:
  0.0 0.1 pad_add_fusion.place_ref
  0.1 4.0 %own_gram.1 = (f32[64,128]{1,0:T(8,128)S(1)}, bf16[64,16384]{1,0:T(8,128)(2,1)S(1)}, bf16[64,16384]{1,0:T(8,128)(2,1)S(1)}) custom-call(s32[2]{0:T(128)S(1)} %pad_add_fusion.place_ref, bf16[64,32768]{1,0:T(8,128)(2,1)} %snaps_ref.1), custom_call_target="tpu_custom_call" | custom-call | tf_op jit(solution)/shard_map/own_gram/pallas_call | solution.py:361
  4.1 0.8 collective-permute-start.2
  4.8 1.0 collective-permute-start
  5.9 1.8 %collective-permute-done = f32[64,128]{1,0:T(8,128)S(1)} collective-permute-done((f32[64,128]{1,0:T(8,128)S(1)}, f32[64,128]{1,0:T(8,128)S(1)}, u32[]{:S(2)}, u32[]{:S(2)}) %collective-permute-start) | collective-permute-done | bytes 32800 | tf_op jit(solution)/shard_map/ppermute | solution.py:338
  7.6 1.6 %collective-permute-start.1 = (f32[64,128]{1,0:T(8,128)S(1)}, f32[64,128]{1,0:T(8,128)S(1)}, u32[]{:S(2)}, u32[]{:S(2)}) collective-permute-start(f32[64,128]{1,0:T(8,128)S(1)} %add.57), channel_id=1, source_target_pairs={{0,32},{8,40},{16,48},{24,56},{32,0},{40,8},{48,16},{56,24},{64,96... | collective-permute-start | bytes 98312 | tf_op jit(solution)/shard_map/ppermute | solution.py:338
  9.3 0.0 collective-permute-done.2.other_ref.other_hbm
  9.3 1.3 %cross_gram.1 = f32[64,128]{1,0:T(8,128)S(1)} custom-call(s32[2]{0:T(128)S(1)} %pad_add_fusion.place_ref, bf16[64,16384]{1,0:T(8,128)(2,1)S(1)} %get-tuple-element.24.mine_ref, bf16[64,16384]{1,0:T(8,128)(2,1)S(1)} %collective-permute-done.2.other_ref.other_hbm), custom_call_target="tpu_custom_call" | custom-call | tf_op jit(solution)/shard_map/cross_gram/pallas_call | solution.py:372
  10.6 0.0 copy-done
  10.6 1.6 %collective-permute-start.3 = (f32[64,128]{1,0:T(8,128)S(1)}, f32[64,128]{1,0:T(8,128)S(1)}, u32[]{:S(2)}, u32[]{:S(2)}) collective-permute-start(f32[64,128]{1,0:T(8,128)S(1)} %cross_gram.1), channel_id=1, source_target_pairs={{0,1},{1,0},{2,3},{3,2},{4,5},{5,4},{6,7},{7,6},{8,9},{9,8},{10,11... | collective-permute-start | bytes 98312 | tf_op jit(solution)/shard_map/ppermute | solution.py:338
  12.2 0.0 collective-permute-done.1
  12.2 0.9 collective-permute-done.3
  13.0 0.3 collective-permute-start.4
  13.3 2.6 %collective-permute-done.4 = f32[64,128]{1,0:T(8,128)S(1)} collective-permute-done((f32[64,128]{1,0:T(8,128)S(1)}, f32[64,128]{1,0:T(8,128)S(1)}, u32[]{:S(2)}, u32[]{:S(2)}) %collective-permute-start.4) | collective-permute-done | bytes 32800 | tf_op jit(solution)/shard_map/ppermute | solution.py:338
  15.9 3.0 %collective-permute-start.5 = (f32[64,128]{1,0:T(8,128)S(1)}, f32[64,128]{1,0:T(8,128)S(1)}, u32[]{:S(2)}, u32[]{:S(2)}) collective-permute-start(f32[64,128]{1,0:T(8,128)S(1)} %add.61), channel_id=1, source_target_pairs={{0,64},{8,72},{16,80},{24,88},{32,96},{40,104},{48,112},{56,120},{... | collective-permute-start | bytes 98312 | tf_op jit(solution)/shard_map/ppermute | solution.py:338
  18.9 1.3 %collective-permute-done.5 = f32[64,128]{1,0:T(8,128)S(1)} collective-permute-done((f32[64,128]{1,0:T(8,128)S(1)}, f32[64,128]{1,0:T(8,128)S(1)}, u32[]{:S(2)}, u32[]{:S(2)}) %collective-permute-start.5) | collective-permute-done | bytes 32800 | tf_op jit(solution)/shard_map/ppermute | solution.py:338
  20.2 4.5 %collective-permute-start.6 = (f32[64,128]{1,0:T(8,128)S(1)}, f32[64,128]{1,0:T(8,128)S(1)}, u32[]{:S(2)}, u32[]{:S(2)}) collective-permute-start(f32[64,128]{1,0:T(8,128)S(1)} %add.62), channel_id=1, source_target_pairs={{0,192},{8,200},{16,208},{24,216},{32,224},{40,232},{48,240},{56,2... | collective-permute-start | bytes 98312 | tf_op jit(solution)/shard_map/ppermute | solution.py:338
  24.7 1.7 %collective-permute-done.6 = f32[64,128]{1,0:T(8,128)S(1)} collective-permute-done((f32[64,128]{1,0:T(8,128)S(1)}, f32[64,128]{1,0:T(8,128)S(1)}, u32[]{:S(2)}, u32[]{:S(2)}) %collective-permute-start.6) | collective-permute-done | bytes 32800 | tf_op jit(solution)/shard_map/ppermute | solution.py:338
  26.4 2.2 %collective-permute-start.7 = (f32[64,128]{1,0:T(8,128)S(1)}, f32[64,128]{1,0:T(8,128)S(1)}, u32[]{:S(2)}, u32[]{:S(2)}) collective-permute-start(f32[64,128]{1,0:T(8,128)S(1)} %add.63.gram_ref), channel_id=1, source_target_pairs={{0,8},{8,0},{16,24},{24,16},{32,40},{40,32},{48,56},{56,48},{64,72... | collective-permute-start | bytes 98312 | tf_op jit(solution)/shard_map/ppermute | solution.py:338
  28.6 0.0 copy-done.1
  28.6 2.8 %power_first.1.coeffs_ref = f32[32,64]{1,0:T(8,128)S(1)} custom-call(f32[64,128]{1,0:T(8,128)S(1)} %add.63.gram_ref, bf16[32,64]{1,0:T(8,128)(2,1)S(1)} %copy-done.1), custom_call_target="tpu_custom_call" | custom-call | flops 4000000000 | tf_op jit(solution)/shard_map/power_first/pallas_call | solution.py:383
  31.3 0.0 collective-permute-done.7
  31.4 0.0 copy-start.2
  31.4 0.5 collective-permute-start.8
  31.8 3.1 %power_last.1.mine_co_ref = f32[32,128]{1,0:T(8,128)S(1)} custom-call(f32[64,128]{1,0:T(8,128)S(1)} %add.63.gram_ref, f32[32,64]{1,0:T(8,128)S(1)} %power_first.1.coeffs_ref), custom_call_target="tpu_custom_call" | custom-call | flops 4000000000 | tf_op jit(solution)/shard_map/power_last/pallas_call | solution.py:390
  35.0 4.5 %collective-permute-start.9 = (f32[32,128]{1,0:T(8,128)S(1)}, f32[32,128]{1,0:T(8,128)S(1)}, u32[]{:S(2)}, u32[]{:S(2)}) collective-permute-start(f32[32,128]{1,0:T(8,128)S(1)} %power_last.1.mine_co_ref), channel_id=1, source_target_pairs={{0,1},{1,0},{2,3},{3,2},{4,5},{5,4},{6,7},{7,6},{8,9},{9,8},{10,11... | collective-permute-start | bytes 49160 | tf_op jit(solution)/shard_map/ppermute | solution.py:338
  39.5 0.1 copy.6.mix_ref
  39.6 0.0 collective-permute-done.8
  39.6 0.7 collective-permute-done.9.other_co_ref
  40.3 4.6 %merge.1 = (bf16[32,4096]{1,0:T(8,128)(2,1)S(1)}, bf16[32,4096]{1,0:T(8,128)(2,1)S(1)}, bf16[32,4096]{1,0:T(8,128)(2,1)S(1)}, bf16[32,4096]{1,0:T(8,128)(2,1)S(1...) custom-call(s32[2]{0:T(128)S(1)} %pad_add_fusion.place_ref, f32[64,128]{1,0:T(8,128)S(1)} %add.65.cross_ref, ...), custom_call_target="tpu_custom_call" | custom-call | tf_op jit(solution)/shard_map/merge/pallas_call | solution.py:401
  44.9 1.5 %collective-permute-start.10 = (bf16[32,4096]{1,0:T(8,128)(2,1)S(1)}, bf16[32,4096]{1,0:T(8,128)(2,1)S(1)}, u32[]{:S(2)}, u32[]{:S(2)}) collective-permute-start(bf16[32,4096]{1,0:T(8,128)(2,1)S(1)} %get-tuple-element.27.refs_1_), channel_id=1, source_target_pairs={{0,2},{1,3},{2,0},{3,1},{4,6},{5,7},{6,4},{7,5},{8,10},{9,11},{10,... | collective-permute-start | bytes 786440 | tf_op jit(solution)/shard_map/ppermute | solution.py:338
  46.4 2.4 %collective-permute-start.11 = (bf16[32,4096]{1,0:T(8,128)(2,1)S(1)}, bf16[32,4096]{1,0:T(8,128)(2,1)S(1)}, u32[]{:S(2)}, u32[]{:S(2)}) collective-permute-start(bf16[32,4096]{1,0:T(8,128)(2,1)S(1)} %get-tuple-element.28.refs_2_), channel_id=1, source_target_pairs={{0,4},{1,5},{2,6},{3,7},{4,0},{5,1},{6,2},{7,3},{8,12},{9,13},{10,... | collective-permute-start | bytes 786440 | tf_op jit(solution)/shard_map/ppermute | solution.py:338
  48.8 0.2 collective-permute-start.12
  49.0 3.7 %collective-permute-done.10.refs_1_.refs_4_ = bf16[32,4096]{1,0:T(8,128)(2,1)S(1)} collective-permute-done((bf16[32,4096]{1,0:T(8,128)(2,1)S(1)}, bf16[32,4096]{1,0:T(8,128)(2,1)S(1)}, u32[]{:S(2)}, u32[]{:S(2)}) %collective-permute-start.10) | collective-permute-done | bytes 262176 | tf_op jit(solution)/shard_map/ppermute | solution.py:338
  52.7 7.9 %collective-permute-done.11.refs_2_.refs_5_ = bf16[32,4096]{1,0:T(8,128)(2,1)S(1)} collective-permute-done((bf16[32,4096]{1,0:T(8,128)(2,1)S(1)}, bf16[32,4096]{1,0:T(8,128)(2,1)S(1)}, u32[]{:S(2)}, u32[]{:S(2)}) %collective-permute-start.11) | collective-permute-done | bytes 262176 | tf_op jit(solution)/shard_map/ppermute | solution.py:338
  60.6 2.0 %collective-permute-done.12.refs_3_.refs_6_ = bf16[32,4096]{1,0:T(8,128)(2,1)S(1)} collective-permute-done((bf16[32,4096]{1,0:T(8,128)(2,1)S(1)}, bf16[32,4096]{1,0:T(8,128)(2,1)S(1)}, u32[]{:S(2)}, u32[]{:S(2)}) %collective-permute-start.12) | collective-permute-done | bytes 262176 | tf_op jit(solution)/shard_map/ppermute | solution.py:338
  62.6 1.1 %rows_gram.1 = (f32[80,128]{1,0:T(8,128)S(1)}, bf16[128,4096]{1,0:T(8,128)(2,1)S(1)}, bf16[128,4096]{1,0:T(8,128)(2,1)S(1)}) custom-call(s32[2]{0:T(128)S(1)} %pad_add_fusion.place_ref, bf16[32,4096]{1,0:T(8,128)(2,1)S(1)} %get-tuple-element.36.refs_0_, ...), custom_call_target="tpu_custom_call", output_to_operand_aliasing={{1}: (5, {}), {2}: (6, {})} | custom-call | tf_op jit(solution)/shard_map/rows_gram/pallas_call | solution.py:411
  63.7 1.9 %collective-permute-start.13 = (f32[80,128]{1,0:T(8,128)S(1)}, f32[80,128]{1,0:T(8,128)S(1)}, u32[]{:S(2)}, u32[]{:S(2)}) collective-permute-start(f32[80,128]{1,0:T(8,128)S(1)} %get-tuple-element.32), channel_id=1, source_target_pairs={{0,1},{1,0},{2,3},{3,2},{4,5},{5,4},{6,7},{7,6},{8,9},{9,8},{10,11... | collective-permute-start | bytes 122888 | tf_op jit(solution)/shard_map/ppermute | solution.py:338
  65.6 0.9 collective-permute-done.13
  66.5 0.0 collective-permute-start.14
  66.5 2.8 %collective-permute-done.14 = f32[80,128]{1,0:T(8,128)S(1)} collective-permute-done((f32[80,128]{1,0:T(8,128)S(1)}, f32[80,128]{1,0:T(8,128)S(1)}, u32[]{:S(2)}, u32[]{:S(2)}) %collective-permute-start.14) | collective-permute-done | bytes 40992 | tf_op jit(solution)/shard_map/ppermute | solution.py:338
  69.3 0.2 collective-permute-start.15
  69.5 0.0 collective-permute-start.22
  69.5 2.5 %collective-permute-start.23 = (bf16[128,4096]{1,0:T(8,128)(2,1)S(1)}, bf16[128,4096]{1,0:T(8,128)(2,1)S(1)}, u32[]{:S(2)}, u32[]{:S(2)}) collective-permute-start(bf16[128,4096]{1,0:T(8,128)(2,1)S(1)} %get-tuple-element.38), channel_id=1, source_target_pairs={{0,6},{1,7},{2,4},{3,5},{4,2},{5,3},{6,0},{7,1},{8,14},{9,15},{10,... | collective-permute-start | bytes 3145736 | tf_op jit(solution)/shard_map/ppermute | solution.py:338
  72.0 1.4 %collective-permute-done.15 = f32[80,128]{1,0:T(8,128)S(1)} collective-permute-done((f32[80,128]{1,0:T(8,128)S(1)}, f32[80,128]{1,0:T(8,128)S(1)}, u32[]{:S(2)}, u32[]{:S(2)}) %collective-permute-start.15) | collective-permute-done | bytes 40992 | tf_op jit(solution)/shard_map/ppermute | solution.py:338
  73.4 0.8 collective-permute-start.16
  74.2 2.3 %collective-permute-done.16 = f32[80,128]{1,0:T(8,128)S(1)} collective-permute-done((f32[80,128]{1,0:T(8,128)S(1)}, f32[80,128]{1,0:T(8,128)S(1)}, u32[]{:S(2)}, u32[]{:S(2)}) %collective-permute-start.16) | collective-permute-done | bytes 40992 | tf_op jit(solution)/shard_map/ppermute | solution.py:338
  76.5 0.6 collective-permute-start.17
  77.2 2.5 %collective-permute-done.17 = f32[80,128]{1,0:T(8,128)S(1)} collective-permute-done((f32[80,128]{1,0:T(8,128)S(1)}, f32[80,128]{1,0:T(8,128)S(1)}, u32[]{:S(2)}, u32[]{:S(2)}) %collective-permute-start.17) | collective-permute-done | bytes 40992 | tf_op jit(solution)/shard_map/ppermute | solution.py:338
  79.7 0.0 collective-permute-start.18
  79.7 3.1 %collective-permute-done.18 = f32[80,128]{1,0:T(8,128)S(1)} collective-permute-done((f32[80,128]{1,0:T(8,128)S(1)}, f32[80,128]{1,0:T(8,128)S(1)}, u32[]{:S(2)}, u32[]{:S(2)}) %collective-permute-start.18) | collective-permute-done | bytes 40992 | tf_op jit(solution)/shard_map/ppermute | solution.py:338
  82.9 2.0 %collective-permute-start.19 = (f32[80,128]{1,0:T(8,128)S(1)}, f32[80,128]{1,0:T(8,128)S(1)}, u32[]{:S(2)}, u32[]{:S(2)}) collective-permute-start(f32[80,128]{1,0:T(8,128)S(1)} %add.71), channel_id=1, source_target_pairs={{0,64},{8,72},{16,80},{24,88},{32,96},{40,104},{48,112},{56,120},{... | collective-permute-start | bytes 122888 | tf_op jit(solution)/shard_map/ppermute | solution.py:338
  84.8 2.5 %collective-permute-done.19 = f32[80,128]{1,0:T(8,128)S(1)} collective-permute-done((f32[80,128]{1,0:T(8,128)S(1)}, f32[80,128]{1,0:T(8,128)S(1)}, u32[]{:S(2)}, u32[]{:S(2)}) %collective-permute-start.19) | collective-permute-done | bytes 40992 | tf_op jit(solution)/shard_map/ppermute | solution.py:338
  87.3 3.4 %collective-permute-start.20 = (f32[80,128]{1,0:T(8,128)S(1)}, f32[80,128]{1,0:T(8,128)S(1)}, u32[]{:S(2)}, u32[]{:S(2)}) collective-permute-start(f32[80,128]{1,0:T(8,128)S(1)} %add.72), channel_id=1, source_target_pairs={{0,192},{8,200},{16,208},{24,216},{32,224},{40,232},{48,240},{56,2... | collective-permute-start | bytes 122888 | tf_op jit(solution)/shard_map/ppermute | solution.py:338
  90.7 0.0 collective-permute-start.21
  90.7 1.6 %collective-permute-done.20 = f32[80,128]{1,0:T(8,128)S(1)} collective-permute-done((f32[80,128]{1,0:T(8,128)S(1)}, f32[80,128]{1,0:T(8,128)S(1)}, u32[]{:S(2)}, u32[]{:S(2)}) %collective-permute-start.20) | collective-permute-done | bytes 40992 | tf_op jit(solution)/shard_map/ppermute | solution.py:338
  92.3 4.4 %tree.1.whole_ref = f32[32,128]{1,0:T(8,128)S(1)} custom-call(f32[80,128]{1,0:T(8,128)S(1)} %add.73.gram_ref, f32[64,32]{1,0:T(8,128)S(1)} %copy.6.mix_ref), custom_call_target="tpu_custom_call" | custom-call | flops 8800000000 | tf_op jit(solution)/shard_map/tree/pallas_call | solution.py:427
  96.7 2.9 %collective-permute-done.21.refs_7_ = bf16[32,4096]{1,0:T(8,128)(2,1)S(1)} collective-permute-done((bf16[32,4096]{1,0:T(8,128)(2,1)S(1)}, bf16[32,4096]{1,0:T(8,128)(2,1)S(1)}, u32[]{:S(2)}, u32[]{:S(2)}) %collective-permute-start.21) | collective-permute-done | bytes 262176 | tf_op jit(solution)/shard_map/ppermute | solution.py:338
  99.6 0.0 collective-permute-done.22.refs_8_
  99.6 0.0 collective-permute-done.23.refs_9_
  99.6 1.3 %finish.1 = (f32[4,16384]{1,0:T(4,128)S(1)}, f32[4,16384]{1,0:T(4,128)S(1)}) custom-call(s32[2]{0:T(128)S(1)} %pad_add_fusion.place_ref, f32[32,128]{1,0:T(8,128)S(1)} %tree.1.whole_ref, bf16[32,4096]{1,0:T(8,128)(2,1)S(1)} %get-tuple-element.36.refs_0_, bf16[32,4096]{1,0:T(8,128)(2,1)S(1)} %get-tuple-element.27.refs_1_, ...), custom_call_target="tpu_custom_call" | custom-call | tf_op jit(solution)/shard_map/finish/pallas_call | solution.py:431
  101.0 5.9 %collective-permute-start.24 = (f32[4,16384]{1,0:T(4,128)S(1)}, f32[4,16384]{1,0:T(4,128)S(1)}, u32[]{:S(2)}, u32[]{:S(2)}) collective-permute-start(f32[4,16384]{1,0:T(4,128)S(1)} %get-tuple-element.40), channel_id=1, source_target_pairs={{0,1},{1,0},{2,3},{3,2},{4,5},{5,4},{6,7},{7,6},{8,9},{9,8},{10,11... | collective-permute-start | bytes 786440 | tf_op jit(solution)/shard_map/ppermute | solution.py:338
  106.9 1.2 %collective-permute-done.24.got_ref = f32[4,16384]{1,0:T(4,128)S(1)} collective-permute-done((f32[4,16384]{1,0:T(4,128)S(1)}, f32[4,16384]{1,0:T(4,128)S(1)}, u32[]{:S(2)}, u32[]{:S(2)}) %collective-permute-start.24) | collective-permute-done | bytes 262176 | tf_op jit(solution)/shard_map/ppermute | solution.py:338
  108.1 1.4 %assemble.1 = f32[4,32768]{1,0:T(4,128)} custom-call(s32[2]{0:T(128)S(1)} %pad_add_fusion.place_ref, f32[4,16384]{1,0:T(4,128)S(1)} %get-tuple-element.39.keep_ref, f32[4,16384]{1,0:T(4,128)S(1)} %collective-permute-done.24.got_ref), custom_call_target="tpu_custom_call" | custom-call | tf_op jit(solution)/shard_map/assemble/pallas_call | solution.py:437
  (18 shorter events, 0.1 us)
Async XLA Ops:
  4.1 5.2 %collective-permute-start.2 = (bf16[64,16384]{1,0:T(8,128)(2,1)S(1)}, bf16[64,16384]{1,0:T(8,128)(2,1)S(1)}, u32[]{:S(2)}, u32[]{:S(2)}) collective-permute-start(bf16[64,16384]{1,0:T(8,128)(2,1)S(1)} %get-tuple-element.25), channel_id=1, source_target_pairs={{0,1},{1,0},{2,3},{3,2},{4,5},{5,4},{6,7},{7,6},{8,9},{9,8},{10,11... | collective-permute-start | bytes 6291464 | tf_op jit(solution)/shard_map/ppermute | solution.py:338
  4.8 2.8 %collective-permute-start = (f32[64,128]{1,0:T(8,128)S(1)}, f32[64,128]{1,0:T(8,128)S(1)}, u32[]{:S(2)}, u32[]{:S(2)}) collective-permute-start(f32[64,128]{1,0:T(8,128)S(1)} %get-tuple-element.23), channel_id=1, source_target_pairs={{0,8},{8,0},{16,24},{24,16},{32,40},{40,32},{48,56},{56,48},{64,72... | collective-permute-start | bytes 98312 | tf_op jit(solution)/shard_map/ppermute | solution.py:338
  7.6 4.6 %collective-permute-start.1 = (f32[64,128]{1,0:T(8,128)S(1)}, f32[64,128]{1,0:T(8,128)S(1)}, u32[]{:S(2)}, u32[]{:S(2)}) collective-permute-start(f32[64,128]{1,0:T(8,128)S(1)} %add.57), channel_id=1, source_target_pairs={{0,32},{8,40},{16,48},{24,56},{32,0},{40,8},{48,16},{56,24},{64,96... | collective-permute-start | bytes 98312 | tf_op jit(solution)/shard_map/ppermute | solution.py:338
  9.3 1.3 %copy-start = (bf16[64,16384]{1,0:T(8,128)(2,1)}, bf16[64,16384]{1,0:T(8,128)(2,1)S(1)}, u32[]{:S(2)}) copy-start(bf16[64,16384]{1,0:T(8,128)(2,1)S(1)} %collective-permute-done.2.other_ref.other_hbm) | copy-start | bytes 6291460
  9.3 19.3 %copy-start.1 = (bf16[32,64]{1,0:T(8,128)(2,1)S(1)}, bf16[32,64]{1,0:T(8,128)(2,1)}, u32[]{:S(2)}) copy-start(bf16[32,64]{1,0:T(8,128)(2,1)} %coeffs_ref.1) | copy-start | bytes 12292
  10.6 2.4 %collective-permute-start.3 = (f32[64,128]{1,0:T(8,128)S(1)}, f32[64,128]{1,0:T(8,128)S(1)}, u32[]{:S(2)}, u32[]{:S(2)}) collective-permute-start(f32[64,128]{1,0:T(8,128)S(1)} %cross_gram.1), channel_id=1, source_target_pairs={{0,1},{1,0},{2,3},{3,2},{4,5},{5,4},{6,7},{7,6},{8,9},{9,8},{10,11... | collective-permute-start | bytes 98312 | tf_op jit(solution)/shard_map/ppermute | solution.py:338
  13.0 2.9 %collective-permute-start.4 = (f32[64,128]{1,0:T(8,128)S(1)}, f32[64,128]{1,0:T(8,128)S(1)}, u32[]{:S(2)}, u32[]{:S(2)}) collective-permute-start(f32[64,128]{1,0:T(8,128)S(1)} %add_add_fusion), channel_id=1, source_target_pairs={{0,24},{8,16},{16,8},{24,0},{32,56},{40,48},{48,40},{56,32},{64,88... | collective-permute-start | bytes 98312 | tf_op jit(solution)/shard_map/ppermute | solution.py:338
  15.9 4.3 %collective-permute-start.5 = (f32[64,128]{1,0:T(8,128)S(1)}, f32[64,128]{1,0:T(8,128)S(1)}, u32[]{:S(2)}, u32[]{:S(2)}) collective-permute-start(f32[64,128]{1,0:T(8,128)S(1)} %add.61), channel_id=1, source_target_pairs={{0,64},{8,72},{16,80},{24,88},{32,96},{40,104},{48,112},{56,120},{... | collective-permute-start | bytes 98312 | tf_op jit(solution)/shard_map/ppermute | solution.py:338
  20.2 6.1 %collective-permute-start.6 = (f32[64,128]{1,0:T(8,128)S(1)}, f32[64,128]{1,0:T(8,128)S(1)}, u32[]{:S(2)}, u32[]{:S(2)}) collective-permute-start(f32[64,128]{1,0:T(8,128)S(1)} %add.62), channel_id=1, source_target_pairs={{0,192},{8,200},{16,208},{24,216},{32,224},{40,232},{48,240},{56,2... | collective-permute-start | bytes 98312 | tf_op jit(solution)/shard_map/ppermute | solution.py:338
  26.4 5.0 %collective-permute-start.7 = (f32[64,128]{1,0:T(8,128)S(1)}, f32[64,128]{1,0:T(8,128)S(1)}, u32[]{:S(2)}, u32[]{:S(2)}) collective-permute-start(f32[64,128]{1,0:T(8,128)S(1)} %add.63.gram_ref), channel_id=1, source_target_pairs={{0,8},{8,0},{16,24},{24,16},{32,40},{40,32},{48,56},{56,48},{64,72... | collective-permute-start | bytes 98312 | tf_op jit(solution)/shard_map/ppermute | solution.py:338
  31.4 8.1 %copy-start.2 = (f32[64,32]{0,1:T(8,128)S(1)}, f32[64,32]{0,1:T(8,128)}, u32[]{:S(2)}) copy-start(f32[64,32]{0,1:T(8,128)} %param.5) | copy-start | bytes 24580
  31.4 8.2 %collective-permute-start.8 = (f32[64,128]{1,0:T(8,128)S(1)}, f32[64,128]{1,0:T(8,128)S(1)}, u32[]{:S(2)}, u32[]{:S(2)}) collective-permute-start(f32[64,128]{1,0:T(8,128)S(1)} %add.64), channel_id=1, source_target_pairs={{0,32},{8,40},{16,48},{24,56},{32,0},{40,8},{48,16},{56,24},{64,96... | collective-permute-start | bytes 98312 | tf_op jit(solution)/shard_map/ppermute | solution.py:338
  35.0 5.4 %collective-permute-start.9 = (f32[32,128]{1,0:T(8,128)S(1)}, f32[32,128]{1,0:T(8,128)S(1)}, u32[]{:S(2)}, u32[]{:S(2)}) collective-permute-start(f32[32,128]{1,0:T(8,128)S(1)} %power_last.1.mine_co_ref), channel_id=1, source_target_pairs={{0,1},{1,0},{2,3},{3,2},{4,5},{5,4},{6,7},{7,6},{8,9},{9,8},{10,11... | collective-permute-start | bytes 49160 | tf_op jit(solution)/shard_map/ppermute | solution.py:338
  44.9 7.8 %collective-permute-start.10 = (bf16[32,4096]{1,0:T(8,128)(2,1)S(1)}, bf16[32,4096]{1,0:T(8,128)(2,1)S(1)}, u32[]{:S(2)}, u32[]{:S(2)}) collective-permute-start(bf16[32,4096]{1,0:T(8,128)(2,1)S(1)} %get-tuple-element.27.refs_1_), channel_id=1, source_target_pairs={{0,2},{1,3},{2,0},{3,1},{4,6},{5,7},{6,4},{7,5},{8,10},{9,11},{10,... | collective-permute-start | bytes 786440 | tf_op jit(solution)/shard_map/ppermute | solution.py:338
  46.4 14.2 %collective-permute-start.11 = (bf16[32,4096]{1,0:T(8,128)(2,1)S(1)}, bf16[32,4096]{1,0:T(8,128)(2,1)S(1)}, u32[]{:S(2)}, u32[]{:S(2)}) collective-permute-start(bf16[32,4096]{1,0:T(8,128)(2,1)S(1)} %get-tuple-element.28.refs_2_), channel_id=1, source_target_pairs={{0,4},{1,5},{2,6},{3,7},{4,0},{5,1},{6,2},{7,3},{8,12},{9,13},{10,... | collective-permute-start | bytes 786440 | tf_op jit(solution)/shard_map/ppermute | solution.py:338
  48.8 13.7 %collective-permute-start.12 = (bf16[32,4096]{1,0:T(8,128)(2,1)S(1)}, bf16[32,4096]{1,0:T(8,128)(2,1)S(1)}, u32[]{:S(2)}, u32[]{:S(2)}) collective-permute-start(bf16[32,4096]{1,0:T(8,128)(2,1)S(1)} %get-tuple-element.29.refs_3_), channel_id=1, source_target_pairs={{0,6},{1,7},{2,4},{3,5},{4,2},{5,3},{6,0},{7,1},{8,14},{9,15},{10,... | collective-permute-start | bytes 786440 | tf_op jit(solution)/shard_map/ppermute | solution.py:338
  63.7 2.7 %collective-permute-start.13 = (f32[80,128]{1,0:T(8,128)S(1)}, f32[80,128]{1,0:T(8,128)S(1)}, u32[]{:S(2)}, u32[]{:S(2)}) collective-permute-start(f32[80,128]{1,0:T(8,128)S(1)} %get-tuple-element.32), channel_id=1, source_target_pairs={{0,1},{1,0},{2,3},{3,2},{4,5},{5,4},{6,7},{7,6},{8,9},{9,8},{10,11... | collective-permute-start | bytes 122888 | tf_op jit(solution)/shard_map/ppermute | solution.py:338
  66.5 2.9 %collective-permute-start.14 = (f32[80,128]{1,0:T(8,128)S(1)}, f32[80,128]{1,0:T(8,128)S(1)}, u32[]{:S(2)}, u32[]{:S(2)}) collective-permute-start(f32[80,128]{1,0:T(8,128)S(1)} %add.66), channel_id=1, source_target_pairs={{0,2},{1,3},{2,0},{3,1},{4,6},{5,7},{6,4},{7,5},{8,10},{9,11},{10,... | collective-permute-start | bytes 122888 | tf_op jit(solution)/shard_map/ppermute | solution.py:338
  69.3 4.1 %collective-permute-start.15 = (f32[80,128]{1,0:T(8,128)S(1)}, f32[80,128]{1,0:T(8,128)S(1)}, u32[]{:S(2)}, u32[]{:S(2)}) collective-permute-start(f32[80,128]{1,0:T(8,128)S(1)} %add.67), channel_id=1, source_target_pairs={{0,6},{1,7},{2,4},{3,5},{4,2},{5,3},{6,0},{7,1},{8,14},{9,15},{10,... | collective-permute-start | bytes 122888 | tf_op jit(solution)/shard_map/ppermute | solution.py:338
  69.5 30.1 %collective-permute-start.22 = (bf16[128,4096]{1,0:T(8,128)(2,1)S(1)}, bf16[128,4096]{1,0:T(8,128)(2,1)S(1)}, u32[]{:S(2)}, u32[]{:S(2)}) collective-permute-start(bf16[128,4096]{1,0:T(8,128)(2,1)S(1)} %get-tuple-element.37), channel_id=1, source_target_pairs={{0,2},{1,3},{2,0},{3,1},{4,6},{5,7},{6,4},{7,5},{8,10},{9,11},{10,... | collective-permute-start | bytes 3145736 | tf_op jit(solution)/shard_map/ppermute | solution.py:338
  69.5 30.1 %collective-permute-start.23 = (bf16[128,4096]{1,0:T(8,128)(2,1)S(1)}, bf16[128,4096]{1,0:T(8,128)(2,1)S(1)}, u32[]{:S(2)}, u32[]{:S(2)}) collective-permute-start(bf16[128,4096]{1,0:T(8,128)(2,1)S(1)} %get-tuple-element.38), channel_id=1, source_target_pairs={{0,6},{1,7},{2,4},{3,5},{4,2},{5,3},{6,0},{7,1},{8,14},{9,15},{10,... | collective-permute-start | bytes 3145736 | tf_op jit(solution)/shard_map/ppermute | solution.py:338
  73.4 3.1 %collective-permute-start.16 = (f32[80,128]{1,0:T(8,128)S(1)}, f32[80,128]{1,0:T(8,128)S(1)}, u32[]{:S(2)}, u32[]{:S(2)}) collective-permute-start(f32[80,128]{1,0:T(8,128)S(1)} %add.68), channel_id=1, source_target_pairs={{0,8},{8,0},{16,24},{24,16},{32,40},{40,32},{48,56},{56,48},{64,72... | collective-permute-start | bytes 122888 | tf_op jit(solution)/shard_map/ppermute | solution.py:338
  76.5 3.1 %collective-permute-start.17 = (f32[80,128]{1,0:T(8,128)S(1)}, f32[80,128]{1,0:T(8,128)S(1)}, u32[]{:S(2)}, u32[]{:S(2)}) collective-permute-start(f32[80,128]{1,0:T(8,128)S(1)} %add.69), channel_id=1, source_target_pairs={{0,32},{8,40},{16,48},{24,56},{32,0},{40,8},{48,16},{56,24},{64,96... | collective-permute-start | bytes 122888 | tf_op jit(solution)/shard_map/ppermute | solution.py:338
  79.7 3.1 %collective-permute-start.18 = (f32[80,128]{1,0:T(8,128)S(1)}, f32[80,128]{1,0:T(8,128)S(1)}, u32[]{:S(2)}, u32[]{:S(2)}) collective-permute-start(f32[80,128]{1,0:T(8,128)S(1)} %add.70), channel_id=1, source_target_pairs={{0,24},{8,16},{16,8},{24,0},{32,56},{40,48},{48,40},{56,32},{64,88... | collective-permute-start | bytes 122888 | tf_op jit(solution)/shard_map/ppermute | solution.py:338
  82.9 4.5 %collective-permute-start.19 = (f32[80,128]{1,0:T(8,128)S(1)}, f32[80,128]{1,0:T(8,128)S(1)}, u32[]{:S(2)}, u32[]{:S(2)}) collective-permute-start(f32[80,128]{1,0:T(8,128)S(1)} %add.71), channel_id=1, source_target_pairs={{0,64},{8,72},{16,80},{24,88},{32,96},{40,104},{48,112},{56,120},{... | collective-permute-start | bytes 122888 | tf_op jit(solution)/shard_map/ppermute | solution.py:338
  87.3 5.0 %collective-permute-start.20 = (f32[80,128]{1,0:T(8,128)S(1)}, f32[80,128]{1,0:T(8,128)S(1)}, u32[]{:S(2)}, u32[]{:S(2)}) collective-permute-start(f32[80,128]{1,0:T(8,128)S(1)} %add.72), channel_id=1, source_target_pairs={{0,192},{8,200},{16,208},{24,216},{32,224},{40,232},{48,240},{56,2... | collective-permute-start | bytes 122888 | tf_op jit(solution)/shard_map/ppermute | solution.py:338
  90.7 8.9 %collective-permute-start.21 = (bf16[32,4096]{1,0:T(8,128)(2,1)S(1)}, bf16[32,4096]{1,0:T(8,128)(2,1)S(1)}, u32[]{:S(2)}, u32[]{:S(2)}) collective-permute-start(bf16[32,4096]{1,0:T(8,128)(2,1)S(1)} %get-tuple-element.36.refs_0_), channel_id=1, source_target_pairs={{0,4},{1,5},{2,6},{3,7},{4,0},{5,1},{6,2},{7,3},{8,12},{9,13},{10,... | collective-permute-start | bytes 786440 | tf_op jit(solution)/shard_map/ppermute | solution.py:338
  101.0 7.1 %collective-permute-start.24 = (f32[4,16384]{1,0:T(4,128)S(1)}, f32[4,16384]{1,0:T(4,128)S(1)}, u32[]{:S(2)}, u32[]{:S(2)}) collective-permute-start(f32[4,16384]{1,0:T(4,128)S(1)} %get-tuple-element.40), channel_id=1, source_target_pairs={{0,1},{1,0},{2,3},{3,2},{4,5},{5,4},{6,7},{7,6},{8,9},{9,8},{10,11... | collective-permute-start | bytes 786440 | tf_op jit(solution)/shard_map/ppermute | solution.py:338
